TPU v7x, 32 devices: a whole 2x2x4 slice. The times are simulated.
32 devices in a mesh: seq: 8 (over y, x, core), grp: 4 (over z).
Axes of the slice: x: 2, y: 2, z: 4, core: 2. Of those that a mesh axis runs over, the one named last changes fastest.
Arguments:
- queries: bfloat16 [4096, 8, 128], P(('grp', 'seq')), may hold values from -6 to 6
- key_rows: bfloat16 [4096, 8, 128], P(('grp', 'seq')), may hold values from -6 to 6
- value_rows: bfloat16 [4096, 8, 256], P(('grp', 'seq')), may hold values from -6 to 6
- log_gate: float32 [8, 4096], P(None, ('grp', 'seq')), may hold values from -1.5 to 0
- beta_rate: float32 [8, 4096], P(None, ('grp', 'seq')), may hold values from 0 to 0.9
Outputs:
- outputs: bfloat16 [4096, 8, 256], P(('grp', 'seq'))
All inputs are finite; a program needn't handle non-finite values.
Results may differ from a plain program's by a relative error of at most 0.0012.
Values sent between devices are 32-bit elements; how exact they have to be, the bound alone decides.
No kernel may reach another device: no remote copies, remote signals or barrier semaphores. Data moves between devices by JAX's collectives and lax.ppermute only.
A program may use at most 128 MiB of HBM per device.

v0:
```python
import jax
import jax.numpy as jnp
from jax import lax
from jax.sharding import PartitionSpec as P

STRETCH = 64


EXACT_MATMUL = lax.Precision.HIGHEST


def carried_in(part, axis, combine, identity):
    place = lax.axis_index(axis)
    gathered = jax.tree.map(lambda a: lax.all_gather(a, axis), part)
    state = jax.tree.map(lambda a, e: jnp.zeros_like(a) + jnp.asarray(e, a.dtype), part, identity)

    def one(lap, state):
        return combine(
            state, jax.tree.map(lambda a: lax.dynamic_index_in_dim(a, lap, 0, False), gathered)
        )

    return lax.fori_loop(0, place, one, state)


def passed_along(value, axis, steps):
    count = lax.axis_size(axis)
    leading, last = (max(0, -steps), min(count, count - steps))
    return lax.ppermute(value, axis, [(source, source + steps) for source in range(leading, last)])


def from_root(value, axis, source):
    kept = jnp.where(lax.axis_index(axis) == source, value, 0).astype(value.dtype)
    return lax.psum(kept, axis)


def unit_rows(vectors):
    wide = vectors.astype(jnp.float32)
    return wide / jnp.sqrt(jnp.sum(wide * wide, axis=-1, keepdims=True) + 1e-06)


def invert_unit_lower(strict):
    order_len = strict.shape[-1]
    identity = jnp.eye(order_len, dtype=strict.dtype)
    powered = -strict
    inverse = identity + powered
    span_len = 2
    while span_len < order_len:
        powered = jnp.einsum("hij,hjk->hik", powered, powered, precision=EXACT_MATMUL)
        inverse = inverse + jnp.einsum("hij,hjk->hik", inverse, powered, precision=EXACT_MATMUL)
        span_len = span_len * 2
    return inverse


def stretch_terms(q_head, k_head, v_head, gates, betas):
    order_len = gates.shape[1]
    rows_idx = lax.broadcasted_iota(jnp.int32, (order_len, order_len), 0)
    cols_idx = lax.broadcasted_iota(jnp.int32, (order_len, order_len), 1)
    lower_incl = rows_idx >= cols_idx
    lower_strict = rows_idx > cols_idx
    cum_log = jnp.cumsum(gates, axis=1)
    gaps_log = cum_log[:, :, None] - cum_log[:, None, :]
    decay_mask = jnp.where(lower_incl, jnp.exp(jnp.where(lower_incl, gaps_log, 0.0)), 0.0)
    key_gram = jnp.einsum("hik,hjk->hij", k_head, k_head, precision=EXACT_MATMUL)
    strict = jnp.where(lower_strict, betas[:, :, None] * key_gram, 0.0)
    inv_plain = invert_unit_lower(strict)
    inv_decay = inv_plain * decay_mask
    w_plain = jnp.einsum(
        "hij,hjk->hik", inv_plain, betas[:, :, None] * k_head, precision=EXACT_MATMUL
    )
    decayed_weight = jnp.exp(cum_log)[:, :, None] * w_plain
    update_basis = jnp.einsum(
        "hij,hjv->hiv", inv_decay, betas[:, :, None] * v_head, precision=EXACT_MATMUL
    )
    scores = jnp.einsum("hik,hjk->hij", q_head, k_head, precision=EXACT_MATMUL) * decay_mask
    gated_query = jnp.exp(cum_log)[:, :, None] * q_head
    return (cum_log, w_plain, decayed_weight, update_basis, scores, gated_query)


def advance_stretch(passed_state, stretch_parts, k_head):
    cum_log, w_plain, decayed_weight, update_basis, scores, gated_query = stretch_parts
    triangular_solve = update_basis - jnp.einsum(
        "rzi,rib->rzb", decayed_weight, passed_state, precision=EXACT_MATMUL
    )
    segment_output = jnp.einsum("rzi,rib->rzb", gated_query, passed_state, precision=EXACT_MATMUL)
    segment_output = segment_output + jnp.einsum(
        "hij,hjv->hiv", scores, triangular_solve, precision=EXACT_MATMUL
    )
    final_log = cum_log[:, -1]
    trailing_keys = jnp.exp(final_log[:, None] - cum_log)[:, :, None] * k_head
    following_state = jnp.exp(final_log)[:, None, None] * passed_state
    following_state = following_state + jnp.einsum(
        "atb,atm->abm", trailing_keys, triangular_solve, precision=EXACT_MATMUL
    )
    return (segment_output, following_state)


def compose(earlier, later):
    log_early, trans_early, state_early = earlier
    log_late, trans_late, state_late = later
    joined_log = log_early + log_late
    joined_trans = jnp.einsum("hij,hjk->hik", trans_late, trans_early, precision=EXACT_MATMUL)
    joined_state = (
        jnp.exp(log_late)[:, None, None]
        * jnp.einsum("hij,hjv->hiv", trans_late, state_early, precision=EXACT_MATMUL)
        + state_late
    )
    return (joined_log, joined_trans, joined_state)


def apply_map(state_map, entering):
    map_log, map_trans, map_state = state_map
    moved = jnp.einsum("hij,hjv->hiv", map_trans, entering, precision=EXACT_MATMUL)
    return jnp.exp(map_log)[:, None, None] * moved + map_state


def body(queries, key_rows, value_rows, log_gate, beta_rate):
    tok_rows = queries.shape[0]
    heads = queries.shape[1]
    key_dim = queries.shape[2]
    value_dim = value_rows.shape[2]
    stretch_count = tok_rows // STRETCH
    q_blocks = queries.reshape(stretch_count, STRETCH, heads, key_dim)
    k_blocks = key_rows.reshape(stretch_count, STRETCH, heads, key_dim)
    v_blocks = value_rows.reshape(stretch_count, STRETCH, heads, value_dim)
    g_blocks = jnp.transpose(log_gate.reshape(heads, stretch_count, STRETCH), (1, 0, 2))
    b_blocks = jnp.transpose(beta_rate.reshape(heads, stretch_count, STRETCH), (1, 0, 2))
    identity = jnp.broadcast_to(jnp.eye(key_dim, dtype=jnp.float32), (heads, key_dim, key_dim))

    def local_step(carry, blocks):
        run_state, run_log, run_trans = carry
        q_part, k_part, v_part, gates, betas = blocks
        q_head = jnp.transpose(unit_rows(q_part), (1, 0, 2))
        k_head = jnp.transpose(unit_rows(k_part), (1, 0, 2))
        v_head = jnp.transpose(v_part.astype(jnp.float32), (1, 0, 2))
        stretch_parts = stretch_terms(q_head, k_head, v_head, gates, betas)
        segment_output, following_state = advance_stretch(run_state, stretch_parts, k_head)
        cum_log, w_plain, decayed_weight, update_basis, scores, gated_query = stretch_parts
        eff_query = gated_query - jnp.einsum(
            "hij,hjk->hik", scores, decayed_weight, precision=EXACT_MATMUL
        )
        fold_rows = jnp.exp(run_log)[:, None, None] * jnp.einsum(
            "hck,hkj->hcj", eff_query, run_trans, precision=EXACT_MATMUL
        )
        stretch_trans = identity - jnp.einsum(
            "hck,hcj->hkj", k_head, w_plain, precision=EXACT_MATMUL
        )
        next_trans = jnp.einsum("hij,hjk->hik", stretch_trans, run_trans, precision=EXACT_MATMUL)
        next_log = run_log + cum_log[:, -1]
        return ((following_state, next_log, next_trans), (segment_output, fold_rows))

    zero_state = jnp.zeros((heads, key_dim, value_dim), jnp.float32)
    zero_log = jnp.zeros((heads,), jnp.float32)
    (own_state, own_log, own_trans), (local_outs, combine_every) = lax.scan(
        local_step,
        (zero_state, zero_log, identity),
        (q_blocks, k_blocks, v_blocks, g_blocks, b_blocks),
    )
    own_map = (own_log, own_trans, own_state)
    neutral = (zero_log, identity, zero_state)
    before = carried_in((own_log, own_trans, own_state), "seq", compose, neutral)
    through = compose(before, own_map)
    last_seq = lax.axis_size("seq") - 1

    def relay_step(index, carried):
        return passed_along(apply_map(through, carried), "grp", 1)

    entering = from_root(
        lax.fori_loop(0, lax.axis_size("grp") - 1, relay_step, zero_state), "seq", last_seq
    )
    initial_state = apply_map(before, entering)
    corrections = jnp.einsum("usxz,szl->usxl", combine_every, initial_state, precision=EXACT_MATMUL)
    merged = jnp.transpose(local_outs + corrections, (0, 2, 1, 3))
    return merged.reshape(tok_rows, heads, value_dim).astype(jnp.bfloat16)


def solution(mesh):
    return jax.shard_map(
        body,
        mesh=mesh,
        in_specs=(
            P(("grp", "seq"), None, None),
            P(("grp", "seq"), None, None),
            P(("grp", "seq"), None, None),
            P(None, ("grp", "seq")),
            P(None, ("grp", "seq")),
        ),
        out_specs=P(("grp", "seq"), None, None),
        check_vma=False,
    )
```

profile of v0, /device:TPU:0, one launch (start us, length us, event | category | flops | bytes accessed | tf_op | source)
XLA Modules:
  0.0 323.5 jit_solution(284150019677191865)
XLA Ops:
  6.6 0.8 reshape.87
  7.4 0.8 reshape.89
  8.2 32.1 %while.47 = (s32[]{:T(128)}, f32[8,128,256]{2,1,0:T(8,128)S(1)}, f32[8]{0:T(128)S(1)}, f32[8,128,128]{2,1,0:T(8,128)S(1)}, f32[2,8,64,256]{3,2,0,1:T(8,128)}, /*...) while((s32[]{:T(128)}, f32[8,128,256]{2,1,0:T(8,128)S(1)}, ...), condition=%wide.region_4.5_spmd.clone, body=%wide.region_0.4_spmd.clone.sunk | while | flops 1665482752 | bytes 31253568 | solution.py:153
  8.2 1.0 constant_dynamic-slice_fusion.11
  9.4 0.7 fusion.244
  15.0 0.7 convolution_multiply_fusion.8
  16.5 1.3 fusion.258
  17.8 0.8 fusion.251
  18.6 0.8 convolution_subtract_fusion.6
  19.3 0.6 fusion.256
  19.9 0.8 fusion.257
  20.7 1.6 convolution_add_fusion.18
  22.3 1.1 convolution_subtract_fusion.7
  23.5 0.6 fusion.254
  24.1 1.0 constant_dynamic-slice_fusion.11
  25.3 0.7 fusion.244
  30.9 0.7 convolution_multiply_fusion.8
  32.5 1.3 fusion.258
  33.8 0.8 fusion.251
  34.5 0.8 convolution_subtract_fusion.6
  35.3 0.6 fusion.256
  35.9 0.8 fusion.257
  36.7 1.6 convolution_add_fusion.18
  38.3 1.1 convolution_subtract_fusion.7
  39.4 0.6 fusion.254
  40.3 0.8 copy-done.2
  41.9 0.6 dynamic-slice
  43.5 15.3 %all-reduce = f32[64]{0:T(128)S(1)} all-reduce(f32[64]{0:T(128)S(1)} %dynamic-update-slice), channel_id=2, replica_groups=mesh['seq'=8,'grp'=4] {'seq'}, use_global_device_ids=true, to_apply=%add | all-reduce | flops 64 | bytes 512
  58.9 21.8 %all-gather.6.cloned.1.call-done = f32[64,128,128]{2,1,0:T(8,128)} async-done(((f32[8,128,128]{2,1,0:T(8,128)}), f32[64,128,128]{2,1,0:T(8,128)}) %all-gather.6.cloned.1.call-update) | async-done | bytes 4194320 | tf_op jit(solution)/shard_map/all_gather | solution.py:14
  80.7 56.3 %all-gather.8.cloned.1.call-done = f32[64,128,256]{2,1,0:T(8,128)} async-done(((f32[8,128,256]{2,1,0:T(8,128)}), f32[64,128,256]{2,1,0:T(8,128)}) %all-gather.8.cloned.1.call-update) | async-done | bytes 8388624 | tf_op jit(solution)/shard_map/all_gather | solution.py:14
  137.2 1.0 copy-done.3
  138.2 1.4 fusion.79
  139.6 2.0 fusion.67
  141.7 88.8 %while.46 = (s32[]{:T(128)}, f32[8,128,256]{2,1,0:T(8,128)S(1)}, f32[8,1,1]{0,2,1:T(1,128)S(1)}, f32[8,128,128]{2,1,0:T(8,128)}, f32[8,128,256]{2,1,0:T(8,128)}, /*index=5*/s32[]{:T(128)}) while((s32[]{:T(128)}, f32[8,128,256]{2,1,0:T(8,128)S(1)}, f32[8,1,1]{0,2,1:T(1,128)S(1)}, f32[8,128,128]{2,1,0:T(8,128)}, f32[8,128,256]{2,1,0:T(8,128)}, ...), condition=%wide.region_8.9_spmd, body=%wide.region_7.8_spmd.sunk | while | flops 403177472 | bytes 7864461 | solution.py:168
  141.7 3.4 %fusion.199 = f32[8,128,256]{2,1,0:T(8,128)} fusion(f32[8,128,256]{2,1,0:T(8,128)} %get-tuple-element.586, f32[8,128,128]{2,1,0:T(8,128)} %get-tuple-element.585, f32[8,128,256]{2,1,0:T(8,128)S(1)} %get-tuple-element.577, f32[8]{0:T(128)S(1)} %bitcast.291), kind=kOutput, calls=%fused_computation.15.clone.1 | convolution fusion | flops 403177472 | bytes 3670048 | tf_op jit(solution)/shard_map/while/body/eval_jaxpr/hij,hjv->hiv/dot_general | solution.py:112
  145.2 3.4 %collective-permute-start = (f32[8,128,256]{2,1,0:T(8,128)}, f32[8,128,256]{2,1,0:T(8,128)S(1)}, u32[]{:S(2)}, u32[]{:S(2)}) collective-permute-start(f32[8,128,256]{2,1,0:T(8,128)} %fusion.199), channel_id=1, source_target_pairs={{0,1},{1,2},{2,3},{4,5},{5,6},{6,7},{8,9},{9,10},{10,11},{12,13},{... | collective-permute-start | bytes 3145736 | tf_op jit(solution)/shard_map/while/body/eval_jaxpr/ppermute | solution.py:28
  148.6 21.0 %collective-permute-done = f32[8,128,256]{2,1,0:T(8,128)S(1)} collective-permute-done((f32[8,128,256]{2,1,0:T(8,128)}, f32[8,128,256]{2,1,0:T(8,128)S(1)}, u32[]{:S(2)}, u32[]{:S(2)}) %collective-permute-start) | collective-permute-done | bytes 1048608 | tf_op jit(solution)/shard_map/while/body/eval_jaxpr/ppermute | solution.py:28
  169.6 3.4 %fusion.199 = f32[8,128,256]{2,1,0:T(8,128)} fusion(f32[8,128,256]{2,1,0:T(8,128)} %get-tuple-element.586, f32[8,128,128]{2,1,0:T(8,128)} %get-tuple-element.585, f32[8,128,256]{2,1,0:T(8,128)S(1)} %get-tuple-element.577, f32[8]{0:T(128)S(1)} %bitcast.291), kind=kOutput, calls=%fused_computation.15.clone.1 | convolution fusion | flops 403177472 | bytes 3670048 | tf_op jit(solution)/shard_map/while/body/eval_jaxpr/hij,hjv->hiv/dot_general | solution.py:112
  173.0 4.3 %collective-permute-start = (f32[8,128,256]{2,1,0:T(8,128)}, f32[8,128,256]{2,1,0:T(8,128)S(1)}, u32[]{:S(2)}, u32[]{:S(2)}) collective-permute-start(f32[8,128,256]{2,1,0:T(8,128)} %fusion.199), channel_id=1, source_target_pairs={{0,1},{1,2},{2,3},{4,5},{5,6},{6,7},{8,9},{9,10},{10,11},{12,13},{... | collective-permute-start | bytes 3145736 | tf_op jit(solution)/shard_map/while/body/eval_jaxpr/ppermute | solution.py:28
  177.4 22.1 %collective-permute-done = f32[8,128,256]{2,1,0:T(8,128)S(1)} collective-permute-done((f32[8,128,256]{2,1,0:T(8,128)}, f32[8,128,256]{2,1,0:T(8,128)S(1)}, u32[]{:S(2)}, u32[]{:S(2)}) %collective-permute-start) | collective-permute-done | bytes 1048608 | tf_op jit(solution)/shard_map/while/body/eval_jaxpr/ppermute | solution.py:28
  199.4 3.4 %fusion.199 = f32[8,128,256]{2,1,0:T(8,128)} fusion(f32[8,128,256]{2,1,0:T(8,128)} %get-tuple-element.586, f32[8,128,128]{2,1,0:T(8,128)} %get-tuple-element.585, f32[8,128,256]{2,1,0:T(8,128)S(1)} %get-tuple-element.577, f32[8]{0:T(128)S(1)} %bitcast.291), kind=kOutput, calls=%fused_computation.15.clone.1 | convolution fusion | flops 403177472 | bytes 3670048 | tf_op jit(solution)/shard_map/while/body/eval_jaxpr/hij,hjv->hiv/dot_general | solution.py:112
  202.9 4.3 %collective-permute-start = (f32[8,128,256]{2,1,0:T(8,128)}, f32[8,128,256]{2,1,0:T(8,128)S(1)}, u32[]{:S(2)}, u32[]{:S(2)}) collective-permute-start(f32[8,128,256]{2,1,0:T(8,128)} %fusion.199), channel_id=1, source_target_pairs={{0,1},{1,2},{2,3},{4,5},{5,6},{6,7},{8,9},{9,10},{10,11},{12,13},{... | collective-permute-start | bytes 3145736 | tf_op jit(solution)/shard_map/while/body/eval_jaxpr/ppermute | solution.py:28
  207.2 23.3 %collective-permute-done = f32[8,128,256]{2,1,0:T(8,128)S(1)} collective-permute-done((f32[8,128,256]{2,1,0:T(8,128)}, f32[8,128,256]{2,1,0:T(8,128)S(1)}, u32[]{:S(2)}, u32[]{:S(2)}) %collective-permute-start) | collective-permute-done | bytes 1048608 | tf_op jit(solution)/shard_map/while/body/eval_jaxpr/ppermute | solution.py:28
  230.5 1.1 broadcast_select_fusion.1
  231.6 80.9 %all-reduce.3.cloned.1.call-done = f32[8,128,256]{2,1,0:T(8,128)} async-done(((f32[8,128,256]{2,1,0:T(8,128)}), f32[8,128,256]{2,1,0:T(8,128)}) %all-reduce.3.cloned.1.call-update) | async-done | bytes 1048592 | tf_op jit(solution)/shard_map/psum | solution.py:33
  312.5 2.3 fusion.66
  314.9 1.1 fusion.69
  315.9 1.1 copy.24
  (97 shorter events, 13.0 us)
Async XLA Ops:
  6.5 74.2 %all-gather.6.cloned.1.call-start = ((), (), s32[]{:S(2)}) async-start(), calls=%async_computation.1 | async-start | bytes 4718592 | tf_op jit(solution)/shard_map/all_gather | solution.py:14
  8.2 33.7 %copy-start.9 = (u32[32]{0:T(128)S(1)}, u32[32]{0:T(128)}, u32[]{:S(2)}) copy-start(u32[32]{0:T(128)} %constant.67) | copy-start | bytes 388
  13.6 4.2 %copy-start.4 = (bf16[2,64,8,256]{3,2,1,0:T(8,128)(2,1)S(1)}, bf16[2,64,8,256]{3,2,1,0:T(8,128)(2,1)}, u32[]{:S(2)}) copy-start(bf16[2,64,8,256]{3,2,1,0:T(8,128)(2,1)} %get-tuple-element.531) | copy-start | bytes 1572868 | tf_op jit(solution)/shard_map/while
  16.4 3.5 %copy-start.5 = (f32[2,8,64,256]{3,2,0,1:T(8,128)S(1)}, f32[2,8,64,256]{3,2,0,1:T(8,128)}, u32[]{:S(2)}) copy-start(f32[2,8,64,256]{3,2,0,1:T(8,128)} %get-tuple-element.511) | copy-start | bytes 3145732 | tf_op jit(solution)/shard_map/while
  20.7 3.4 %copy-start.6 = (f32[2,8,64,256]{3,2,0,1:T(8,128)}, f32[2,8,64,256]{3,2,0,1:T(8,128)S(1)}, u32[]{:S(2)}) copy-start(f32[2,8,64,256]{3,2,0,1:T(8,128)S(1)} %fusion.257) | copy-start | bytes 3145732 | tf_op jit(solution)/shard_map/while
  29.6 4.2 %copy-start.4 = (bf16[2,64,8,256]{3,2,1,0:T(8,128)(2,1)S(1)}, bf16[2,64,8,256]{3,2,1,0:T(8,128)(2,1)}, u32[]{:S(2)}) copy-start(bf16[2,64,8,256]{3,2,1,0:T(8,128)(2,1)} %get-tuple-element.531) | copy-start | bytes 1572868 | tf_op jit(solution)/shard_map/while
  32.4 3.5 %copy-start.5 = (f32[2,8,64,256]{3,2,0,1:T(8,128)S(1)}, f32[2,8,64,256]{3,2,0,1:T(8,128)}, u32[]{:S(2)}) copy-start(f32[2,8,64,256]{3,2,0,1:T(8,128)} %get-tuple-element.511) | copy-start | bytes 3145732 | tf_op jit(solution)/shard_map/while
  36.7 3.4 %copy-start.6 = (f32[2,8,64,256]{3,2,0,1:T(8,128)}, f32[2,8,64,256]{3,2,0,1:T(8,128)S(1)}, u32[]{:S(2)}) copy-start(f32[2,8,64,256]{3,2,0,1:T(8,128)S(1)} %fusion.257) | copy-start | bytes 3145732 | tf_op jit(solution)/shard_map/while
  40.3 0.8 copy-start.2
  40.3 1.2 copy-start
  41.1 95.9 %all-gather.8.cloned.1.call-start = ((), (), s32[]{:S(2)}) async-start(), calls=%async_computation.2 | async-start | bytes 9437184 | tf_op jit(solution)/shard_map/all_gather | solution.py:14
  41.8 270.7 %all-reduce.3.cloned.1.call-start = ((), (), s32[]{:S(2)}) async-start(), calls=%async_computation | async-start | bytes 2097152 | tf_op jit(solution)/shard_map/psum | solution.py:33
  137.2 1.0 copy-start.3
  137.2 2.5 copy-start.1
  145.2 24.4 %collective-permute-start = (f32[8,128,256]{2,1,0:T(8,128)}, f32[8,128,256]{2,1,0:T(8,128)S(1)}, u32[]{:S(2)}, u32[]{:S(2)}) collective-permute-start(f32[8,128,256]{2,1,0:T(8,128)} %fusion.199), channel_id=1, source_target_pairs={{0,1},{1,2},{2,3},{4,5},{5,6},{6,7},{8,9},{9,10},{10,11},{12,13},{... | collective-permute-start | bytes 3145736 | tf_op jit(solution)/shard_map/while/body/eval_jaxpr/ppermute | solution.py:28
  173.0 26.4 %collective-permute-start = (f32[8,128,256]{2,1,0:T(8,128)}, f32[8,128,256]{2,1,0:T(8,128)S(1)}, u32[]{:S(2)}, u32[]{:S(2)}) collective-permute-start(f32[8,128,256]{2,1,0:T(8,128)} %fusion.199), channel_id=1, source_target_pairs={{0,1},{1,2},{2,3},{4,5},{5,6},{6,7},{8,9},{9,10},{10,11},{12,13},{... | collective-permute-start | bytes 3145736 | tf_op jit(solution)/shard_map/while/body/eval_jaxpr/ppermute | solution.py:28
  202.9 27.6 %collective-permute-start = (f32[8,128,256]{2,1,0:T(8,128)}, f32[8,128,256]{2,1,0:T(8,128)S(1)}, u32[]{:S(2)}, u32[]{:S(2)}) collective-permute-start(f32[8,128,256]{2,1,0:T(8,128)} %fusion.199), channel_id=1, source_target_pairs={{0,1},{1,2},{2,3},{4,5},{5,6},{6,7},{8,9},{9,10},{10,11},{12,13},{... | collective-permute-start | bytes 3145736 | tf_op jit(solution)/shard_map/while/body/eval_jaxpr/ppermute | solution.py:28
  230.5 84.3 %copy-start.8 = (f32[2,8,64,128]{3,2,0,1:T(8,128)S(1)}, f32[2,8,64,128]{3,2,0,1:T(8,128)}, u32[]{:S(2)}) copy-start(f32[2,8,64,128]{3,2,0,1:T(8,128)} %get-tuple-element.185) | copy-start | bytes 1572868
  231.6 83.2 %copy-start.7 = (f32[2,8,64,256]{3,2,0,1:T(8,128)S(1)}, f32[2,8,64,256]{3,2,0,1:T(8,128)}, u32[]{:S(2)}) copy-start(f32[2,8,64,256]{3,2,0,1:T(8,128)} %get-tuple-element.177) | copy-start | bytes 3145732
Sparse Core Ops, SparseCore 0:
  41.2 39.4 all-gather.5
  82.6 54.3 all-gather.7
  231.7 80.7 all-reduce.2
where the time goes:
time: 324 us
  waiting for transfers between devices  226 us (70%)
  matrix products  44.6 us (14%)
  blocking collectives  15.3 us (5%)
  between operations  14 us (4%)
  starting transfers between devices  12.2 us (4%)
  local copies, waits for them, and re-layouts  8.46 us (3%)
    psum x1, waiting for transfers between devices, from_root(): return lax.psum(kept, axis)  80.9 us
    all_gather x2, waiting for transfers between devices, carried_in(): gathered = jax.tree.map(lambda a: lax.all_gather(a, axis), part)  78.1 us
    ppermute x3, waiting for transfers between devices, passed_along(): lax.ppermute(value, axis, [(source, source + steps) for source in range(l...  66.3 us
    unnamed x1, blocking collectives  15.3 us
    dot_general x4, matrix products, apply_map(): jnp.einsum('hij,hjv->hiv', map_trans, entering, precision=EXACT_MATMUL)  12.5 us
    ppermute x3, starting transfers between devices, passed_along(): lax.ppermute(value, axis, [(source, source + steps) for source in range(l...  12.1 us
  transfers between devices with their start and end apart: 6, of which 6 were waited for; matrix products, arithmetic and copies ran while one was open for 0% of the time, Pallas kernels for 0%

commit v1 on v0

v1 whole, which is shorter than its diff:
```python
import functools

import jax
import jax.numpy as jnp
from jax import lax
from jax.experimental import pallas as pl
from jax.experimental.pallas import tpu as pltpu
from jax.sharding import PartitionSpec as P

F32 = jnp.float32
BF16 = jnp.bfloat16
VMEM_LIMIT = 48 * 1024 * 1024


def split2(a):
    high = a.astype(BF16)
    low = (a - high.astype(F32)).astype(BF16)
    return high, low


def mm(a, b):
    return jnp.dot(a, b, preferred_element_type=F32)


def mm_nt(a, b):
    return lax.dot_general(a, b, (((1,), (1,)), ((), ())), preferred_element_type=F32)


def mm_tn(a, b):
    return lax.dot_general(a, b, (((0,), (0,)), ((), ())), preferred_element_type=F32)


def mm_exact_right(a, b):
    high, low = split2(a)
    return mm(jnp.concatenate([high, low], axis=1), jnp.concatenate([b, b], axis=0))


def mm3(a, b):
    ah, al = split2(a)
    bh, bl = split2(b)
    return mm(jnp.concatenate([ah, al], axis=1), jnp.concatenate([bh, bh], axis=0)) + mm(ah, bl)


def compose(later, earlier, key_dim):
    moved = mm3(later[:, :key_dim], earlier)
    return jnp.concatenate(
        [moved[:, :key_dim], moved[:, key_dim:] + later[:, key_dim:]], axis=1
    )


def vmem(count):
    return [pl.BlockSpec(memory_space=pltpu.VMEM)] * count


SMEM_SPEC = pl.BlockSpec(memory_space=pltpu.SMEM)


def call(kernel, out_shape, scratch=(), flops=0, nbytes=0):
    def run(place, *arrays):
        return pl.pallas_call(
            kernel,
            out_shape=out_shape,
            in_specs=[SMEM_SPEC] + vmem(len(arrays)),
            out_specs=jax.tree.map(lambda _: pl.BlockSpec(memory_space=pltpu.VMEM), out_shape),
            scratch_shapes=list(scratch),
            compiler_params=pltpu.CompilerParams(vmem_limit_bytes=VMEM_LIMIT),
            cost_estimate=pl.CostEstimate(flops=flops, bytes_accessed=nbytes, transcendentals=0),
        )(place, *arrays)

    return run


def lane_cumsum(a):
    size = a.shape[1]
    lane = lax.broadcasted_iota(jnp.int32, a.shape, 1)
    step = 1
    while step < size:
        a = a + jnp.where(lane >= step, pltpu.roll(a, step, 1), 0.0)
        step *= 2
    return a


def head_rows(scratch, head, heads):
    count = scratch.shape[0] // heads
    return scratch[pl.ds(head, count, stride=heads), :]


def halves_of(a, flip, half):
    return jnp.where(flip, a[half:], a[:half])


def stage_rows(ref, scratch):
    wide = ref[...].astype(F32)
    scratch[...] = wide.reshape(scratch.shape)


def map_kernel(own, place, k_ref, v_ref, g_ref, b_ref, m_ref, r_ref, ks, vs0, vs1):
    tok, heads, key_dim = k_ref.shape
    value_dim = v_ref.shape[2]
    half = heads // 2
    core = place[0]
    side = core if own else 1 - core
    base = side * half
    stage_rows(k_ref, ks)
    wide = v_ref[...].astype(F32)
    vs0[...] = wide[:, :, : value_dim // 2].reshape(vs0.shape)
    vs1[...] = wide[:, :, value_dim // 2 :].reshape(vs1.shape)
    cum_row = lane_cumsum(halves_of(g_ref[...], side == 1, half))
    beta_row = halves_of(b_ref[...], side == 1, half)
    last_row = cum_row[:, tok - 1 :]
    decay_row = jnp.exp(cum_row)
    cum_col = cum_row.T
    beta_col = beta_row.T
    trail_col = jnp.exp(last_row - cum_row).T
    rows = lax.broadcasted_iota(jnp.int32, (tok, tok), 0)
    cols = lax.broadcasted_iota(jnp.int32, (tok, tok), 1)
    lower = rows > cols
    eye = rows == cols
    eye_key = (
        lax.broadcasted_iota(jnp.int32, (key_dim, key_dim), 0)
        == lax.broadcasted_iota(jnp.int32, (key_dim, key_dim), 1)
    )
    every = range(half)
    k_wide = [head_rows(ks, base + i, heads) for i in every]
    k_raw = [a.astype(BF16) for a in k_wide]
    v_raw = [
        jnp.concatenate(
            [head_rows(vs0, base + i, heads), head_rows(vs1, base + i, heads)], axis=1
        ).astype(BF16)
        for i in every
    ]
    gram = [mm_nt(a, a) for a in k_raw]
    inv_col = [lax.rsqrt(jnp.sum(a * a, axis=1, keepdims=True) + 1e-6) for a in k_wide]
    inv_row = [
        lax.rsqrt(jnp.sum(jnp.where(eye, a, 0.0), axis=0, keepdims=True) + 1e-6) for a in gram
    ]
    strict = []
    for i in every:
        gap = cum_col[:, i : i + 1] - cum_row[i : i + 1, :]
        decay = jnp.exp(jnp.where(lower, gap, 0.0))
        left = beta_col[:, i : i + 1] * inv_col[i]
        strict.append(jnp.where(lower, gram[i] * decay * left * inv_row[i], 0.0))
    pair = (rows // 2) == (cols // 2)
    inverse = [jnp.where(eye, 1.0, jnp.where(pair, -a, 0.0)) for a in strict]
    span = 2
    while span < tok:
        joint = ((rows // (2 * span)) == (cols // (2 * span))) & (
            (rows // span) != (cols // span)
        )
        off = [jnp.where(joint, a, 0.0) for a in strict]
        first = [mm3(x, o) for x, o in zip(inverse, off)]
        second = [mm3(f, x) for f, x in zip(first, inverse)]
        inverse = [x - s for x, s in zip(inverse, second)]
        span *= 2
    for i in every:
        beta_i = beta_row[i : i + 1, :]
        key_scale = -(decay_row[i : i + 1, :] * beta_i * inv_row[i])
        key_part = mm_exact_right(inverse[i] * key_scale, k_raw[i])
        value_part = mm_exact_right(inverse[i] * beta_i, v_raw[i])
        basis = jnp.concatenate([key_part, value_part], axis=1)
        r_ref[i] = basis
        bh, bl = split2(basis * (trail_col[:, i : i + 1] * inv_col[i]))
        k_twice = jnp.concatenate([k_raw[i], k_raw[i]], axis=0)
        moved = mm_tn(k_twice, jnp.concatenate([bh, bl], axis=0))
        diagonal = jnp.where(eye_key, jnp.exp(last_row[i : i + 1, :]), 0.0)
        m_ref[i] = jnp.concatenate(
            [moved[:, :key_dim] + diagonal, moved[:, key_dim:]], axis=1
        )


def query_kernel(own, place, q_ref, k_ref, g_ref, r_ref, f_ref, qs, ks):
    tok, heads, key_dim = k_ref.shape
    half = heads // 2
    core = place[0]
    side = core if own else 1 - core
    base = side * half
    stage_rows(q_ref, qs)
    stage_rows(k_ref, ks)
    cum_row = lane_cumsum(halves_of(g_ref[...], side == 1, half))
    cum_col = cum_row.T
    rows = lax.broadcasted_iota(jnp.int32, (tok, tok), 0)
    cols = lax.broadcasted_iota(jnp.int32, (tok, tok), 1)
    lower = rows >= cols
    for i in range(half):
        q_wide = head_rows(qs, base + i, heads)
        k_wide = head_rows(ks, base + i, heads)
        q_inv = lax.rsqrt(jnp.sum(q_wide * q_wide, axis=1, keepdims=True) + 1e-6)
        k_inv = lax.rsqrt(jnp.sum(k_wide * k_wide, axis=1, keepdims=True) + 1e-6)
        k_inv_row = jnp.broadcast_to(k_inv, (tok, tok)).T[:1, :]
        dots = mm_nt(q_wide.astype(BF16), k_wide.astype(BF16))
        gap = cum_col[:, i : i + 1] - cum_row[i : i + 1, :]
        decay = jnp.exp(jnp.where(lower, gap, 0.0))
        scores = jnp.where(lower, dots * decay * q_inv * k_inv_row, 0.0)
        folded = mm3(scores, r_ref[i])
        gated = q_wide * (q_inv * jnp.exp(cum_col[:, i : i + 1]))
        f_ref[i] = jnp.concatenate(
            [folded[:, :key_dim] + gated, folded[:, key_dim:]], axis=1
        )


def chip_kernel(key_dim, outs_per, place, own_ref, got_ref, *out_refs):
    core, chip = place[0], place[1]
    half = own_ref.shape[0]
    owners = half // outs_per
    for r, out in enumerate(out_refs):
        owner = jnp.bitwise_xor(chip, r)
        owner = jnp.where(owner < owners, owner, 0)
        for j in range(outs_per):
            head = owner * outs_per + j
            own, got = own_ref[head], got_ref[head]
            earlier = jnp.where(core == 0, own, got)
            later = jnp.where(core == 0, got, own)
            out[j] = compose(later, earlier, key_dim)


def plane_kernel(key_dim, chips, place, *refs):
    maps, total, prefix = refs[:chips], refs[chips], refs[chips + 1]
    chip = place[1]
    per = total.shape[0]
    prefix_store = prefix
    for j in range(per):
        ordered = []
        for index in range(chips):
            value = maps[0][j]
            for r in range(1, chips):
                value = jnp.where(jnp.bitwise_xor(chip, r) == index, maps[r][j], value)
            ordered.append(value)
        running = ordered[0]
        prefix_store[0, j] = running
        for index in range(1, chips):
            running = compose(ordered[index], running, key_dim)
            if index < chips - 1:
                prefix_store[index, j] = running
        total[j] = running


def group_kernel(key_dim, level, place, total_ref, got_ref, before_ref, new_total, new_before):
    group = place[2]
    upper = jnp.bitwise_and(jnp.right_shift(group, level), 1) == 1
    for j in range(total_ref.shape[0]):
        mine, got = total_ref[j], got_ref[j]
        later = jnp.where(upper, mine, got)
        earlier = jnp.where(upper, got, mine)
        new_total[j] = compose(later, earlier, key_dim)
        if before_ref is None:
            identity = jnp.where(
                lax.broadcasted_iota(jnp.int32, mine.shape, 0)
                == lax.broadcasted_iota(jnp.int32, mine.shape, 1),
                1.0,
                0.0,
            )
            new_before[j] = jnp.where(upper, got, identity)
        else:
            before = before_ref[j]
            new_before[j] = jnp.where(upper, compose(before, got, key_dim), before)


def first_group_kernel(key_dim, place, total_ref, got_ref, new_total, new_before):
    group_kernel(key_dim, 0, place, total_ref, got_ref, None, new_total, new_before)


def enter_kernel(key_dim, chips, level, place, got_ref, before_ref, prefix_ref, *out_refs):
    chip, group = place[1], place[2]
    upper = jnp.bitwise_and(jnp.right_shift(group, level), 1) == 1
    for j in range(got_ref.shape[0]):
        before = before_ref[j]
        joined = mm3(before[:, :key_dim], got_ref[j]) + before[:, key_dim:]
        entering = jnp.where(upper, joined, before[:, key_dim:])
        eh, el = split2(entering)
        twice = jnp.concatenate([eh, eh], axis=0)
        states = [entering]
        for index in range(chips - 1):
            one = prefix_ref[index, j]
            th, tl = split2(one[:, :key_dim])
            moved = mm(jnp.concatenate([th, tl], axis=1), twice) + mm(th, el)
            states.append(moved + one[:, key_dim:])
        for r, out in enumerate(out_refs):
            value = states[0]
            for index in range(1, chips):
                value = jnp.where(jnp.bitwise_xor(chip, r) == index, states[index], value)
            out[j] = value


def core_kernel(key_dim, outs_per, owners, place, own_ref, got_ref, *refs):
    parts, keep, give = refs[:-2], refs[-2], refs[-1]
    core, chip = place[0], place[1]
    for r, part in enumerate(parts):
        owner = jnp.bitwise_xor(chip, r)

        @pl.when(owner < owners)
        def _():
            for j in range(outs_per):
                head = owner * outs_per + j
                state = part[j]
                first = jnp.where(core == 0, own_ref[head], got_ref[head])
                second = mm3(first[:, :key_dim], state) + first[:, key_dim:]
                keep[head] = jnp.where(core == 0, state, second)
                give[head] = jnp.where(core == 0, second, state)


def output_kernel(place, keep_ref, got_ref, f_own, f_give, o_ref, os0, os1):
    half, key_dim, value_dim = keep_ref.shape
    tok = f_own.shape[1]
    heads = 2 * half
    core = place[0]
    mid = value_dim // 2
    for state_ref, folded_ref, side in ((keep_ref, f_own, core), (got_ref, f_give, 1 - core)):
        for i in range(half):
            folded = folded_ref[i]
            out = mm3(folded[:, :key_dim], state_ref[i]) + folded[:, key_dim:]
            head = side * half + i
            os0[pl.ds(head, tok, stride=heads), :] = out[:, :mid]
            os1[pl.ds(head, tok, stride=heads), :] = out[:, mid:]
    o_ref[:, :, :mid] = os0[...].reshape(tok, heads, mid).astype(BF16)
    o_ref[:, :, mid:] = os1[...].reshape(tok, heads, value_dim - mid).astype(BF16)


def body(queries, key_rows, value_rows, log_gate, beta_rate):
    tok, heads, key_dim = queries.shape
    value_dim = value_rows.shape[2]
    wide = key_dim + value_dim
    half = heads // 2
    seq, grp = lax.axis_size("seq"), lax.axis_size("grp")
    chips = seq // 2
    owners = min(chips, half)
    per = half // owners
    place_seq, place_grp = lax.axis_index("seq"), lax.axis_index("grp")
    place = jnp.stack([place_seq % 2, place_seq // 2, place_grp]).astype(jnp.int32)
    f32 = lambda *shape: jax.ShapeDtypeStruct(shape, F32)
    tall = lambda width: pltpu.VMEM((tok * heads, width), F32)
    unit = 2 * tok * key_dim * key_dim

    def maps(own):
        return call(
            functools.partial(map_kernel, own),
            (f32(half, key_dim, wide), f32(half, tok, wide)),
            [tall(key_dim), tall(value_dim // 2), tall(value_dim // 2)],
            flops=50 * half * unit,
        )(place, key_rows, value_rows, log_gate, beta_rate)

    def folded(own, basis):
        return call(
            functools.partial(query_kernel, own),
            f32(half, tok, wide),
            [tall(key_dim), tall(key_dim)],
            flops=10 * half * unit,
        )(place, queries, key_rows, log_gate, basis)

    sibling = [(i, i ^ 1) for i in range(seq)]
    give_map, give_basis = maps(False)
    got_map = lax.ppermute(give_map, "seq", sibling)
    own_map, own_basis = maps(True)
    chip_maps = call(
        functools.partial(chip_kernel, key_dim, per), [f32(per, key_dim, wide)] * chips
    )(place, own_map, got_map)
    f_own = folded(True, own_basis)
    f_give = folded(False, give_basis)

    def across(parts, to_owner):
        moved = [parts[0]]
        for r in range(1, chips):
            pairs = [
                (i, i ^ (2 * r))
                for i in range(seq)
                if ((i ^ (2 * r)) // 2 if to_owner else i // 2) < owners
            ]
            moved.append(lax.ppermute(parts[r], "seq", pairs))
        return moved

    owned = across(chip_maps, True)
    total, prefix = call(
        functools.partial(plane_kernel, key_dim, chips),
        (f32(per, key_dim, wide), f32(chips - 1, per, key_dim, wide)),
    )(place, *owned)
    before = None
    level = 0
    while 2 << level <= grp:
        swap = [(i, i ^ (1 << level)) for i in range(grp)]
        final = 4 << level > grp
        if final and before is not None:
            got_state = lax.ppermute(total[:, :, key_dim:], "grp", swap)
            states = call(
                functools.partial(enter_kernel, key_dim, chips, level),
                [f32(per, key_dim, value_dim)] * chips,
            )(place, got_state, before, prefix)
        else:
            got = lax.ppermute(total, "grp", swap)
            shapes = (f32(per, key_dim, wide), f32(per, key_dim, wide))
            if before is None:
                total, before = call(
                    functools.partial(first_group_kernel, key_dim), shapes
                )(place, total, got)
            else:
                total, before = call(
                    functools.partial(group_kernel, key_dim, level), shapes
                )(place, total, got, before)
        level += 1
    arrived = across(states, False)
    keep, give = call(
        functools.partial(core_kernel, key_dim, per, owners), [f32(half, key_dim, value_dim)] * 2
    )(place, own_map, got_map, *arrived)
    got = lax.ppermute(give, "seq", sibling)
    return call(
        output_kernel,
        jax.ShapeDtypeStruct((tok, heads, value_dim), BF16),
        [tall(value_dim // 2), tall(value_dim // 2)],
    )(place, keep, got, f_own, f_give)


def solution(mesh):
    return jax.shard_map(
        body,
        mesh=mesh,
        in_specs=(
            P(("grp", "seq"), None, None),
            P(("grp", "seq"), None, None),
            P(("grp", "seq"), None, None),
            P(None, ("grp", "seq")),
            P(None, ("grp", "seq")),
        ),
        out_specs=P(("grp", "seq"), None, None),
        check_vma=False,
    )
```

time: 324 us -> 59.9 us (0.18)
  waiting for transfers between devices: 226 us -> 24.3 us
  matrix products: 44.6 us -> 0 us
  Pallas kernels: 0 us -> 20.1 us
  blocking collectives: 15.3 us -> 0 us
  between operations: 14 us -> 0.12 us
  local copies, waits for them, and re-layouts: 8.46 us -> 2.63 us
    psum x1 -> x0, waiting for transfers between devices: 80.9 us -> none  [from_root(): return lax.psum(kept, axis)]
    all_gather x2 -> x0, waiting for transfers between devices: 78.1 us -> none  [carried_in(): gathered = jax.tree.map(lambda a: lax.all_gather(a, axis), part)]
    dot_general x51 -> x0, matrix products: 44.6 us -> none  [the longest x4 12.5 us: apply_map(): jnp.einsum('hij,hjv->hiv', map_trans, entering, precision=EXACT_MATMUL)]
    ppermute x3 -> x10, waiting for transfers between devices: 66.3 us -> 24.3 us  [the longest x6 14.3 us: across(): moved.append(lax.ppermute(parts[r], 'seq', pairs))]
    pallas_call x0 -> x10, Pallas kernels: none -> 20.1 us  [run(): pl.pallas_call(kernel, out_shape=out_shape, in_specs=[SMEM_SPEC] + vmem(l...]
    unnamed x1 -> x0, blocking collectives: 15.3 us -> none
    ppermute x3 -> x10, starting transfers between devices: 12.1 us -> 12.5 us  [the longest x6 7.63 us: across(): moved.append(lax.ppermute(parts[r], 'seq', pairs))]
  transfers between devices with their start and end apart: 6 -> 10, of which waited for: 6 -> 6; matrix products, arithmetic and copies ran while one was open for 0% -> 0% of each run, Pallas kernels for 0% -> 14%
where the time goes in v1:
time: 59.9 us; the launch traced here: 59.7 us
  waiting for transfers between devices  24.3 us (41%)
  Pallas kernels  20.1 us (34%)
  starting transfers between devices  12.5 us (21%)
  local copies, waits for them, and re-layouts  2.63 us (4%)
    pallas_call x10, Pallas kernels, run(): pl.pallas_call(kernel, out_shape=out_shape, in_specs=[SMEM_SPEC] + vmem(l...  20.1 us
    ppermute x6, waiting for transfers between devices, across(): moved.append(lax.ppermute(parts[r], 'seq', pairs))  14.3 us
    ppermute x6, starting transfers between devices, across(): moved.append(lax.ppermute(parts[r], 'seq', pairs))  7.63 us
    ppermute x1, waiting for transfers between devices, body(): got_state = lax.ppermute(total[:, :, key_dim:], 'grp', swap)  5.17 us
    ppermute x1, waiting for transfers between devices, body(): got = lax.ppermute(total, 'grp', swap)  4.77 us
    unnamed x12, local copies, waits for them, and re-layouts  2.62 us
    ppermute x1, starting transfers between devices, body(): got_state = lax.ppermute(total[:, :, key_dim:], 'grp', swap)  2.6 us
    ppermute x1, starting transfers between devices, body(): got = lax.ppermute(total, 'grp', swap)  1.61 us
  transfers between devices with their start and end apart: 10, of which 6 were waited for; matrix products, arithmetic and copies ran while one was open for 0% of the time, Pallas kernels for 14%

profile of v1, /device:TPU:0, one launch (start us, length us, event | category | flops | bytes accessed | tf_op | source)
XLA Modules:
  0.0 59.7 jit_solution(16336947725623423048)
XLA Ops:
  0.0 0.0 copy-start.5
  0.0 0.0 copy-start.3
  0.0 0.1 pad_add_fusion.place
  0.1 0.6 %copy-done.5 = f32[8,128]{1,0:T(8,128)S(1)} copy-done((f32[8,128]{1,0:T(8,128)S(1)}, f32[8,128]{1,0:T(8,128)}, u32[]{:S(2)}) %copy-start.5) | copy-done | bytes 4120
  0.7 0.0 copy-done.3
  0.7 0.0 copy-start
  0.7 0.9 %copy-done = bf16[128,8,128]{2,1,0:T(8,128)(2,1)S(1)} copy-done((bf16[128,8,128]{2,1,0:T(8,128)(2,1)S(1)}, bf16[128,8,128]{2,1,0:T(8,128)(2,1)}, u32[]{:S(2)}) %copy-start) | copy-done | bytes 262168
  1.7 0.0 copy-start.4
  1.7 1.0 %copy-done.4 = bf16[128,8,256]{2,1,0:T(8,128)(2,1)S(1)} copy-done((bf16[128,8,256]{2,1,0:T(8,128)(2,1)S(1)}, bf16[128,8,256]{2,1,0:T(8,128)(2,1)}, u32[]{:S(2)}) %copy-start.4) | copy-done | bytes 524312
  2.7 4.3 %shard_map.56 = (f32[4,128,384]{2,1,0:T(8,128)S(1)}, f32[4,128,384]{2,1,0:T(8,128)S(1)}) custom-call(s32[3]{0:T(128)S(1)} %pad_add_fusion.place, bf16[128,8,128]{2,1,0:T(8,128)(2,1)S(1)} %copy-done, bf16[128,8,256]{2,1,0:T(8,128)(2,1)S(1)} %copy-done.4, f32[8,128]{1,0:T(8,128)S(1)} %copy-done.3, f32[8,128]{1,0:T(8,128)S(1)} %copy-done.5), custom_call_target="tpu_custom_call" | custom-call | flops 838860800 | tf_op jit(solution)/shard_map/pallas_call | solution.py:60
  7.0 0.6 collective-permute-start
  7.6 4.4 %shard_map.55 = (f32[4,128,384]{2,1,0:T(8,128)S(1)}, f32[4,128,384]{2,1,0:T(8,128)S(1)}) custom-call(s32[3]{0:T(128)S(1)} %pad_add_fusion.place, bf16[128,8,128]{2,1,0:T(8,128)(2,1)S(1)} %copy-done, bf16[128,8,256]{2,1,0:T(8,128)(2,1)S(1)} %copy-done.4, f32[8,128]{1,0:T(8,128)S(1)} %copy-done.3, f32[8,128]{1,0:T(8,128)S(1)} %copy-done.5), custom_call_target="tpu_custom_call" | custom-call | flops 838860800 | tf_op jit(solution)/shard_map/pallas_call | solution.py:60
  12.0 0.0 collective-permute-done.got_ref
  12.0 1.0 %shard_map.57 = (f32[1,128,384]{2,1,0:T(8,128)S(1)}, f32[1,128,384]{2,1,0:T(8,128)S(1)}, f32[1,128,384]{2,1,0:T(8,128)S(1)}, f32[1,128,384]{2,1,0:T(8,128)S(1)}) custom-call(s32[3]{0:T(128)S(1)} %pad_add_fusion.place, f32[4,128,384]{2,1,0:T(8,128)S(1)} %get-tuple-element.23.own_ref, f32[4,128,384]{2,1,0:T(8,128)S(1)} %collective-permute-done.got_ref), custom_call_target="tpu_custom_call" | custom-call | tf_op jit(solution)/shard_map/pallas_call | solution.py:60
  13.0 2.5 %collective-permute-start.1 = (f32[1,128,384]{2,1,0:T(8,128)S(1)}, f32[1,128,384]{2,1,0:T(8,128)S(1)}, u32[]{:S(2)}, u32[]{:S(2)}) collective-permute-start(f32[1,128,384]{2,1,0:T(8,128)S(1)} %get-tuple-element.26), channel_id=1, source_target_pairs={{0,8},{4,12},{8,0},{12,4},{16,24},{20,28},{24,16},{28,20},{1,9},{5... | collective-permute-start | bytes 589832 | tf_op jit(solution)/shard_map/ppermute | solution.py:367
  15.5 1.5 %collective-permute-start.2 = (f32[1,128,384]{2,1,0:T(8,128)S(1)}, f32[1,128,384]{2,1,0:T(8,128)S(1)}, u32[]{:S(2)}, u32[]{:S(2)}) collective-permute-start(f32[1,128,384]{2,1,0:T(8,128)S(1)} %get-tuple-element.27), channel_id=1, source_target_pairs={{0,16},{4,20},{8,24},{12,28},{16,0},{20,4},{24,8},{28,12},{1,17},{... | collective-permute-start | bytes 589832 | tf_op jit(solution)/shard_map/ppermute | solution.py:367
  17.0 0.1 collective-permute-start.3
  17.0 4.2 %collective-permute-done.1.refs_1_ = f32[1,128,384]{2,1,0:T(8,128)S(1)} collective-permute-done((f32[1,128,384]{2,1,0:T(8,128)S(1)}, f32[1,128,384]{2,1,0:T(8,128)S(1)}, u32[]{:S(2)}, u32[]{:S(2)}) %collective-permute-start.1) | collective-permute-done | bytes 196640 | tf_op jit(solution)/shard_map/ppermute | solution.py:367
  21.2 5.5 %collective-permute-done.2.refs_2_ = f32[1,128,384]{2,1,0:T(8,128)S(1)} collective-permute-done((f32[1,128,384]{2,1,0:T(8,128)S(1)}, f32[1,128,384]{2,1,0:T(8,128)S(1)}, u32[]{:S(2)}, u32[]{:S(2)}) %collective-permute-start.2) | collective-permute-done | bytes 196640 | tf_op jit(solution)/shard_map/ppermute | solution.py:367
  26.8 0.0 collective-permute-done.3.refs_3_
  26.8 1.2 %shard_map.58 = (f32[1,128,384]{2,1,0:T(8,128)S(1)}, f32[3,1,128,384]{3,2,1,0:T(8,128)S(1)}) custom-call(s32[3]{0:T(128)S(1)} %pad_add_fusion.place, f32[1,128,384]{2,1,0:T(8,128)S(1)} %get-tuple-element.25.refs_0_, f32[1,128,384]{2,1,0:T(8,128)S(1)} %collective-permute-done.1.refs_1_, f32[1,128,384]{2,1,0:T(8,128)S(1)} %collective-permute-done.2.refs_2_, ...), custom_call_target="tpu_custom_call" | custom-call | tf_op jit(solution)/shard_map/pallas_call | solution.py:60
  28.0 1.6 %collective-permute-start.4 = (f32[1,128,384]{2,1,0:T(8,128)S(1)}, f32[1,128,384]{2,1,0:T(8,128)S(1)}, u32[]{:S(2)}, u32[]{:S(2)}) collective-permute-start(f32[1,128,384]{2,1,0:T(8,128)S(1)} %get-tuple-element.29.total_ref), channel_id=1, source_target_pairs={{0,1},{1,0},{2,3},{3,2},{4,5},{5,4},{6,7},{7,6},{8,9},{9,8},{10,11... | collective-permute-start | bytes 589832 | tf_op jit(solution)/shard_map/ppermute | solution.py:387
  29.6 4.8 %collective-permute-done.4.got_ref = f32[1,128,384]{2,1,0:T(8,128)S(1)} collective-permute-done((f32[1,128,384]{2,1,0:T(8,128)S(1)}, f32[1,128,384]{2,1,0:T(8,128)S(1)}, u32[]{:S(2)}, u32[]{:S(2)}) %collective-permute-start.4) | collective-permute-done | bytes 196640 | tf_op jit(solution)/shard_map/ppermute | solution.py:387
  34.4 0.8 %shard_map.59 = (f32[1,128,384]{2,1,0:T(8,128)S(1)}, f32[1,128,384]{2,1,0:T(8,128)S(1)}) custom-call(s32[3]{0:T(128)S(1)} %pad_add_fusion.place, f32[1,128,384]{2,1,0:T(8,128)S(1)} %get-tuple-element.29.total_ref, f32[1,128,384]{2,1,0:T(8,128)S(1)} %collective-permute-done.4.got_ref), custom_call_target="tpu_custom_call" | custom-call | tf_op jit(solution)/shard_map/pallas_call | solution.py:60
  35.2 2.6 %collective-permute-start.5 = (f32[1,128,256]{2,1,0:T(8,128)S(1)}, f32[1,128,256]{2,1,0:T(8,128)S(1)}, u32[]{:S(2)}, u32[]{:S(2)}) collective-permute-start(f32[1,128,256]{2,1,0:T(8,128)S(1)} %slice.3), channel_id=1, source_target_pairs={{0,2},{1,3},{2,0},{3,1},{4,6},{5,7},{6,4},{7,5},{8,10},{9,11},{10,... | collective-permute-start | bytes 393224 | tf_op jit(solution)/shard_map/ppermute | solution.py:381
  37.8 5.2 %collective-permute-done.5.got_ref = f32[1,128,256]{2,1,0:T(8,128)S(1)} collective-permute-done((f32[1,128,256]{2,1,0:T(8,128)S(1)}, f32[1,128,256]{2,1,0:T(8,128)S(1)}, u32[]{:S(2)}, u32[]{:S(2)}) %collective-permute-start.5) | collective-permute-done | bytes 131104 | tf_op jit(solution)/shard_map/ppermute | solution.py:381
  42.9 1.0 %shard_map.60 = (f32[1,128,256]{2,1,0:T(8,128)S(1)}, f32[1,128,256]{2,1,0:T(8,128)S(1)}, f32[1,128,256]{2,1,0:T(8,128)S(1)}, f32[1,128,256]{2,1,0:T(8,128)S(1)}) custom-call(s32[3]{0:T(128)S(1)} %pad_add_fusion.place, f32[1,128,256]{2,1,0:T(8,128)S(1)} %collective-permute-done.5.got_ref, f32[1,128,384]{2,1,0:T(8,128)S(1)} %get-tuple-element.31.before_ref, ...), custom_call_target="tpu_custom_call" | custom-call | tf_op jit(solution)/shard_map/pallas_call | solution.py:60
  44.0 1.8 %collective-permute-start.6 = (f32[1,128,256]{2,1,0:T(8,128)S(1)}, f32[1,128,256]{2,1,0:T(8,128)S(1)}, u32[]{:S(2)}, u32[]{:S(2)}) collective-permute-start(f32[1,128,256]{2,1,0:T(8,128)S(1)} %get-tuple-element.34), channel_id=1, source_target_pairs={{0,8},{4,12},{8,0},{12,4},{16,24},{20,28},{24,16},{28,20},{1,9},{5... | collective-permute-start | bytes 393224 | tf_op jit(solution)/shard_map/ppermute | solution.py:367
  45.8 0.3 collective-permute-start.7
  46.1 1.4 %collective-permute-start.8 = (f32[1,128,256]{2,1,0:T(8,128)S(1)}, f32[1,128,256]{2,1,0:T(8,128)S(1)}, u32[]{:S(2)}, u32[]{:S(2)}) collective-permute-start(f32[1,128,256]{2,1,0:T(8,128)S(1)} %get-tuple-element.36), channel_id=1, source_target_pairs={{0,24},{4,28},{8,16},{12,20},{16,8},{20,12},{24,0},{28,4},{1,25},{... | collective-permute-start | bytes 393224 | tf_op jit(solution)/shard_map/ppermute | solution.py:367
  47.5 2.0 %collective-permute-done.6.refs_1_ = f32[1,128,256]{2,1,0:T(8,128)S(1)} collective-permute-done((f32[1,128,256]{2,1,0:T(8,128)S(1)}, f32[1,128,256]{2,1,0:T(8,128)S(1)}, u32[]{:S(2)}, u32[]{:S(2)}) %collective-permute-start.6) | collective-permute-done | bytes 131104 | tf_op jit(solution)/shard_map/ppermute | solution.py:367
  49.6 2.6 %collective-permute-done.7.refs_2_ = f32[1,128,256]{2,1,0:T(8,128)S(1)} collective-permute-done((f32[1,128,256]{2,1,0:T(8,128)S(1)}, f32[1,128,256]{2,1,0:T(8,128)S(1)}, u32[]{:S(2)}, u32[]{:S(2)}) %collective-permute-start.7) | collective-permute-done | bytes 131104 | tf_op jit(solution)/shard_map/ppermute | solution.py:367
  52.1 0.0 collective-permute-done.8.refs_3_
  52.1 0.0 copy-start.1
  52.1 0.0 copy-start.2
  52.1 1.3 %shard_map.61 = (f32[4,128,256]{2,1,0:T(8,128)S(1)}, f32[4,128,256]{2,1,0:T(8,128)S(1)}) custom-call(s32[3]{0:T(128)S(1)} %pad_add_fusion.place, f32[4,128,384]{2,1,0:T(8,128)S(1)} %get-tuple-element.23.own_ref, f32[4,128,384]{2,1,0:T(8,128)S(1)} %collective-permute-done.got_ref, f32[1,128,256]{2,1,0:T(8,128)S(1)} %get-tuple-element.33.refs_0_, ...), custom_call_target="tpu_custom_call" | custom-call | tf_op jit(solution)/shard_map/pallas_call | solution.py:60
  53.4 0.1 collective-permute-start.9
  53.5 0.0 copy-done.1
  53.5 0.0 copy-done.2
  53.5 2.1 %shard_map.63.f_give = f32[4,128,384]{2,1,0:T(8,128)S(1)} custom-call(s32[3]{0:T(128)S(1)} %pad_add_fusion.place, bf16[128,8,128]{2,1,0:T(8,128)(2,1)S(1)} %copy-done.2, bf16[128,8,128]{2,1,0:T(8,128)(2,1)S(1)} %copy-done.1, f32[8,128]{1,0:T(8,128)S(1)} %copy-done.3, f32[4,128,384]{2,1,0:T(8,128)S(1)} %get-tuple-element.40.r_ref), custom_call_target="tpu_custom_call" | custom-call | flops 167772160 | tf_op jit(solution)/shard_map/pallas_call | solution.py:60
  55.6 2.1 %shard_map.62.f_own = f32[4,128,384]{2,1,0:T(8,128)S(1)} custom-call(s32[3]{0:T(128)S(1)} %pad_add_fusion.place, bf16[128,8,128]{2,1,0:T(8,128)(2,1)S(1)} %copy-done.2, bf16[128,8,128]{2,1,0:T(8,128)(2,1)S(1)} %copy-done.1, f32[8,128]{1,0:T(8,128)S(1)} %copy-done.3, f32[4,128,384]{2,1,0:T(8,128)S(1)} %get-tuple-element.39.r_ref), custom_call_target="tpu_custom_call" | custom-call | flops 167772160 | tf_op jit(solution)/shard_map/pallas_call | solution.py:60
  57.8 0.0 collective-permute-done.9.got_ref
  57.8 1.9 %shard_map.64 = bf16[128,8,256]{2,1,0:T(8,128)(2,1)} custom-call(s32[3]{0:T(128)S(1)} %pad_add_fusion.place, f32[4,128,256]{2,1,0:T(8,128)S(1)} %get-tuple-element.37.keep_ref, f32[4,128,256]{2,1,0:T(8,128)S(1)} %collective-permute-done.9.got_ref, f32[4,128,384]{2,1,0:T(8,128)S(1)} %shard_map.62.f_own, f32[4,128,384]{2,1,0:T(8,128)S(1)} %shard_map.63.f_give), custom_call_target="tpu_custom_call" | custom-call | tf_op jit(solution)/shard_map/pallas_call | solution.py:60
  (1 shorter events, 0.0 us)
Async XLA Ops:
  0.0 0.7 %copy-start.5 = (f32[8,128]{1,0:T(8,128)S(1)}, f32[8,128]{1,0:T(8,128)}, u32[]{:S(2)}) copy-start(f32[8,128]{1,0:T(8,128)} %b_ref.3) | copy-start | bytes 12292
  0.0 0.7 %copy-start.3 = (f32[8,128]{1,0:T(8,128)S(1)}, f32[8,128]{1,0:T(8,128)}, u32[]{:S(2)}) copy-start(f32[8,128]{1,0:T(8,128)} %g_ref.7) | copy-start | bytes 12292
  0.7 0.9 %copy-start = (bf16[128,8,128]{2,1,0:T(8,128)(2,1)S(1)}, bf16[128,8,128]{2,1,0:T(8,128)(2,1)}, u32[]{:S(2)}) copy-start(bf16[128,8,128]{2,1,0:T(8,128)(2,1)} %k_ref.7) | copy-start | bytes 786436
  1.7 1.0 %copy-start.4 = (bf16[128,8,256]{2,1,0:T(8,128)(2,1)S(1)}, bf16[128,8,256]{2,1,0:T(8,128)(2,1)}, u32[]{:S(2)}) copy-start(bf16[128,8,256]{2,1,0:T(8,128)(2,1)} %v_ref.3) | copy-start | bytes 1572868
  7.0 4.9 %collective-permute-start = (f32[4,128,384]{2,1,0:T(8,128)S(1)}, f32[4,128,384]{2,1,0:T(8,128)S(1)}, u32[]{:S(2)}, u32[]{:S(2)}) collective-permute-start(f32[4,128,384]{2,1,0:T(8,128)S(1)} %get-tuple-element.24), channel_id=1, source_target_pairs={{0,4},{4,0},{8,12},{12,8},{16,20},{20,16},{24,28},{28,24},{1,5},{5... | collective-permute-start | bytes 2359304 | tf_op jit(solution)/shard_map/ppermute | solution.py:351
  13.0 8.3 %collective-permute-start.1 = (f32[1,128,384]{2,1,0:T(8,128)S(1)}, f32[1,128,384]{2,1,0:T(8,128)S(1)}, u32[]{:S(2)}, u32[]{:S(2)}) collective-permute-start(f32[1,128,384]{2,1,0:T(8,128)S(1)} %get-tuple-element.26), channel_id=1, source_target_pairs={{0,8},{4,12},{8,0},{12,4},{16,24},{20,28},{24,16},{28,20},{1,9},{5... | collective-permute-start | bytes 589832 | tf_op jit(solution)/shard_map/ppermute | solution.py:367
  15.5 11.3 %collective-permute-start.2 = (f32[1,128,384]{2,1,0:T(8,128)S(1)}, f32[1,128,384]{2,1,0:T(8,128)S(1)}, u32[]{:S(2)}, u32[]{:S(2)}) collective-permute-start(f32[1,128,384]{2,1,0:T(8,128)S(1)} %get-tuple-element.27), channel_id=1, source_target_pairs={{0,16},{4,20},{8,24},{12,28},{16,0},{20,4},{24,8},{28,12},{1,17},{... | collective-permute-start | bytes 589832 | tf_op jit(solution)/shard_map/ppermute | solution.py:367
  17.0 9.8 %collective-permute-start.3 = (f32[1,128,384]{2,1,0:T(8,128)S(1)}, f32[1,128,384]{2,1,0:T(8,128)S(1)}, u32[]{:S(2)}, u32[]{:S(2)}) collective-permute-start(f32[1,128,384]{2,1,0:T(8,128)S(1)} %get-tuple-element.28), channel_id=1, source_target_pairs={{0,24},{4,28},{8,16},{12,20},{16,8},{20,12},{24,0},{28,4},{1,25},{... | collective-permute-start | bytes 589832 | tf_op jit(solution)/shard_map/ppermute | solution.py:367
  28.0 6.4 %collective-permute-start.4 = (f32[1,128,384]{2,1,0:T(8,128)S(1)}, f32[1,128,384]{2,1,0:T(8,128)S(1)}, u32[]{:S(2)}, u32[]{:S(2)}) collective-permute-start(f32[1,128,384]{2,1,0:T(8,128)S(1)} %get-tuple-element.29.total_ref), channel_id=1, source_target_pairs={{0,1},{1,0},{2,3},{3,2},{4,5},{5,4},{6,7},{7,6},{8,9},{9,8},{10,11... | collective-permute-start | bytes 589832 | tf_op jit(solution)/shard_map/ppermute | solution.py:387
  35.2 7.8 %collective-permute-start.5 = (f32[1,128,256]{2,1,0:T(8,128)S(1)}, f32[1,128,256]{2,1,0:T(8,128)S(1)}, u32[]{:S(2)}, u32[]{:S(2)}) collective-permute-start(f32[1,128,256]{2,1,0:T(8,128)S(1)} %slice.3), channel_id=1, source_target_pairs={{0,2},{1,3},{2,0},{3,1},{4,6},{5,7},{6,4},{7,5},{8,10},{9,11},{10,... | collective-permute-start | bytes 393224 | tf_op jit(solution)/shard_map/ppermute | solution.py:381
  44.0 5.6 %collective-permute-start.6 = (f32[1,128,256]{2,1,0:T(8,128)S(1)}, f32[1,128,256]{2,1,0:T(8,128)S(1)}, u32[]{:S(2)}, u32[]{:S(2)}) collective-permute-start(f32[1,128,256]{2,1,0:T(8,128)S(1)} %get-tuple-element.34), channel_id=1, source_target_pairs={{0,8},{4,12},{8,0},{12,4},{16,24},{20,28},{24,16},{28,20},{1,9},{5... | collective-permute-start | bytes 393224 | tf_op jit(solution)/shard_map/ppermute | solution.py:367
  45.8 6.4 %collective-permute-start.7 = (f32[1,128,256]{2,1,0:T(8,128)S(1)}, f32[1,128,256]{2,1,0:T(8,128)S(1)}, u32[]{:S(2)}, u32[]{:S(2)}) collective-permute-start(f32[1,128,256]{2,1,0:T(8,128)S(1)} %get-tuple-element.35), channel_id=1, source_target_pairs={{0,16},{4,20},{8,24},{12,28},{16,0},{20,4},{24,8},{28,12},{1,17},{... | collective-permute-start | bytes 393224 | tf_op jit(solution)/shard_map/ppermute | solution.py:367
  46.1 6.1 %collective-permute-start.8 = (f32[1,128,256]{2,1,0:T(8,128)S(1)}, f32[1,128,256]{2,1,0:T(8,128)S(1)}, u32[]{:S(2)}, u32[]{:S(2)}) collective-permute-start(f32[1,128,256]{2,1,0:T(8,128)S(1)} %get-tuple-element.36), channel_id=1, source_target_pairs={{0,24},{4,28},{8,16},{12,20},{16,8},{20,12},{24,0},{28,4},{1,25},{... | collective-permute-start | bytes 393224 | tf_op jit(solution)/shard_map/ppermute | solution.py:367
  52.1 1.4 %copy-start.1 = (bf16[128,8,128]{2,1,0:T(8,128)(2,1)S(1)}, bf16[128,8,128]{2,1,0:T(8,128)(2,1)}, u32[]{:S(2)}) copy-start(bf16[128,8,128]{2,1,0:T(8,128)(2,1)} %k_ref.7) | copy-start | bytes 786436
  52.1 1.4 %copy-start.2 = (bf16[128,8,128]{2,1,0:T(8,128)(2,1)S(1)}, bf16[128,8,128]{2,1,0:T(8,128)(2,1)}, u32[]{:S(2)}) copy-start(bf16[128,8,128]{2,1,0:T(8,128)(2,1)} %q_ref.3) | copy-start | bytes 786436
  53.4 4.3 %collective-permute-start.9 = (f32[4,128,256]{2,1,0:T(8,128)S(1)}, f32[4,128,256]{2,1,0:T(8,128)S(1)}, u32[]{:S(2)}, u32[]{:S(2)}) collective-permute-start(f32[4,128,256]{2,1,0:T(8,128)S(1)} %get-tuple-element.38), channel_id=1, source_target_pairs={{0,4},{4,0},{8,12},{12,8},{16,20},{20,16},{24,28},{28,24},{1,5},{5... | collective-permute-start | bytes 1572872 | tf_op jit(solution)/shard_map/ppermute | solution.py:402

commit v2 on v1

v2 whole, which is shorter than its diff:
```python
import functools

import jax
import jax.numpy as jnp
from jax import lax
from jax.experimental import pallas as pl
from jax.experimental.pallas import tpu as pltpu
from jax.sharding import PartitionSpec as P

F32 = jnp.float32
BF16 = jnp.bfloat16
VMEM_LIMIT = 48 * 1024 * 1024


def split2(a):
    high = a.astype(BF16)
    low = (a - high.astype(F32)).astype(BF16)
    return high, low


def mm(a, b):
    return jnp.dot(a, b, preferred_element_type=F32)


def mm_nt(a, b):
    return lax.dot_general(a, b, (((1,), (1,)), ((), ())), preferred_element_type=F32)


def mm_tn(a, b):
    return lax.dot_general(a, b, (((0,), (0,)), ((), ())), preferred_element_type=F32)


def mm_exact_right(a, b):
    high, low = split2(a)
    return mm(jnp.concatenate([high, low], axis=1), jnp.concatenate([b, b], axis=0))


def mm3(a, b):
    ah, al = split2(a)
    bh, bl = split2(b)
    return mm(jnp.concatenate([ah, al], axis=1), jnp.concatenate([bh, bh], axis=0)) + mm(ah, bl)


def compose(later, earlier, key_dim):
    moved = mm3(later[:, :key_dim], earlier)
    return jnp.concatenate(
        [moved[:, :key_dim], moved[:, key_dim:] + later[:, key_dim:]], axis=1
    )


def vmem(count):
    return [pl.BlockSpec(memory_space=pltpu.VMEM)] * count


SMEM_SPEC = pl.BlockSpec(memory_space=pltpu.SMEM)


def call(kernel, out_shape, scratch=(), flops=0, nbytes=0):
    def run(place, *arrays):
        return pl.pallas_call(
            kernel,
            out_shape=out_shape,
            in_specs=[SMEM_SPEC] + vmem(len(arrays)),
            out_specs=jax.tree.map(lambda _: pl.BlockSpec(memory_space=pltpu.VMEM), out_shape),
            scratch_shapes=list(scratch),
            compiler_params=pltpu.CompilerParams(vmem_limit_bytes=VMEM_LIMIT),
            cost_estimate=pl.CostEstimate(flops=flops, bytes_accessed=nbytes, transcendentals=0),
        )(place, *arrays)

    return run


def lane_cumsum(a):
    size = a.shape[1]
    lane = lax.broadcasted_iota(jnp.int32, a.shape, 1)
    step = 1
    while step < size:
        a = a + jnp.where(lane >= step, pltpu.roll(a, step, 1), 0.0)
        step *= 2
    return a


def head_rows(scratch, head, heads):
    count = scratch.shape[0] // heads
    return scratch[pl.ds(head, count, stride=heads), :]


def stage_rows(ref, scratch):
    wide = ref[...].astype(F32)
    scratch[...] = wide.reshape(scratch.shape)


def rolled(a, flip):
    half = a.shape[0] // 2
    return jnp.where(flip, jnp.concatenate([a[half:], a[:half]], axis=0), a)


def block_inverse(strict, rows, cols):
    size = rows.shape[0]
    base = min(16, size)
    eye = rows == cols
    within = (rows // base) == (cols // base)
    power = [jnp.where(within, -a, 0.0) for a in strict]
    inverse = [jnp.where(eye, 1.0, a) for a in power]
    span = 2
    while span < base:
        power = [mm3(a, a) for a in power]
        inverse = [x + mm3(x, a) for x, a in zip(inverse, power)]
        span *= 2
    span = base
    while span < size:
        joint = ((rows // (2 * span)) == (cols // (2 * span))) & (
            (rows // span) != (cols // span)
        )
        off = [jnp.where(joint, a, 0.0) for a in strict]
        first = [mm3(x, o) for x, o in zip(inverse, off)]
        inverse = [x - mm3(f, x) for f, x in zip(first, inverse)]
        span *= 2
    return inverse


def trailing_map(basis, trail, k_raw, last, eye_key, key_dim):
    bh, bl = split2(basis * trail)
    moved = mm_tn(
        jnp.concatenate([k_raw, k_raw], axis=0), jnp.concatenate([bh, bl], axis=0)
    )
    return jnp.concatenate(
        [moved[:, :key_dim] + jnp.where(eye_key, last, 0.0), moved[:, key_dim:]], axis=1
    )


def eye_mask(size):
    return lax.broadcasted_iota(jnp.int32, (size, size), 0) == lax.broadcasted_iota(
        jnp.int32, (size, size), 1
    )


def basis_kernel(
    place, k_hbm, v_hbm, g_hbm, b_hbm, m_ref, r_ref, kh_ref, trail_ref, rows_ref,
    k_ref, v_ref, g_ref, b_ref, ks, vs0, vs1, sems,
):
    copies = [
        pltpu.make_async_copy(src, dst, sems.at[n])
        for n, (src, dst) in enumerate(
            ((g_hbm, g_ref), (b_hbm, b_ref), (k_hbm, k_ref), (v_hbm, v_ref))
        )
    ]
    for copy in copies:
        copy.start()
    tok, heads, key_dim = k_ref.shape
    value_dim = v_ref.shape[2]
    half = heads // 2
    first_side = 1 - place[0]
    flip = first_side == 1
    order = [first_side * half + i for i in range(half)]
    order += [(1 - first_side) * half + i for i in range(half)]
    copies[0].wait()
    copies[1].wait()
    cum_row = lane_cumsum(rolled(g_ref[...], flip))
    beta_row = rolled(b_ref[...], flip)
    last_row = cum_row[:, tok - 1 :]
    decay_row = jnp.exp(cum_row)
    cum_col = cum_row.T
    beta_col = beta_row.T
    trail_col = jnp.exp(last_row - cum_row).T
    rows = lax.broadcasted_iota(jnp.int32, (tok, tok), 0)
    cols = lax.broadcasted_iota(jnp.int32, (tok, tok), 1)
    lower = rows > cols
    eye = rows == cols
    eye_key = eye_mask(key_dim)
    every = range(heads)
    copies[2].wait()
    stage_rows(k_ref, ks)
    k_wide = [head_rows(ks, h, heads) for h in order]
    k_raw = [a.astype(BF16) for a in k_wide]
    for i in every:
        kh_ref[i] = k_raw[i]
    gram = [mm_nt(a, a) for a in k_raw]
    inv_col = [lax.rsqrt(jnp.sum(a * a, axis=1, keepdims=True) + 1e-6) for a in k_wide]
    inv_row = [
        lax.rsqrt(jnp.sum(jnp.where(eye, a, 0.0), axis=0, keepdims=True) + 1e-6) for a in gram
    ]
    strict = []
    for i in every:
        gap = cum_col[:, i : i + 1] - cum_row[i : i + 1, :]
        decay = jnp.exp(jnp.where(lower, gap, 0.0))
        left = beta_col[:, i : i + 1] * inv_col[i]
        strict.append(jnp.where(lower, gram[i] * decay * left * inv_row[i], 0.0))
    inverse = block_inverse(strict, rows, cols)
    copies[3].wait()
    wide = v_ref[...].astype(F32)
    vs0[...] = wide[:, :, : value_dim // 2].reshape(vs0.shape)
    vs1[...] = wide[:, :, value_dim // 2 :].reshape(vs1.shape)
    rows_ref[0] = jnp.concatenate(inv_row, axis=0)
    rows_ref[1] = cum_row
    for i in every:
        v_raw = jnp.concatenate(
            [head_rows(vs0, order[i], heads), head_rows(vs1, order[i], heads)], axis=1
        ).astype(BF16)
        beta_i = beta_row[i : i + 1, :]
        key_scale = -(decay_row[i : i + 1, :] * beta_i * inv_row[i])
        key_part = mm_exact_right(inverse[i] * key_scale, k_raw[i])
        value_part = mm_exact_right(inverse[i] * beta_i, v_raw)
        basis = jnp.concatenate([key_part, value_part], axis=1)
        r_ref[i] = basis
        trail = trail_col[:, i : i + 1] * inv_col[i]
        if i < half:
            m_ref[i] = trailing_map(
                basis, trail, k_raw[i], jnp.exp(last_row[i : i + 1, :]), eye_key, key_dim
            )
        else:
            trail_ref[i - half] = jnp.broadcast_to(trail, (tok, key_dim))


def own_map_kernel(place, r_ref, kh_ref, trail_ref, rows_ref, m_ref):
    half, key_dim, wide = m_ref.shape
    tok = r_ref.shape[1]
    eye_key = eye_mask(key_dim)
    for i in range(half):
        trail = trail_ref[i][:, :1]
        last = jnp.exp(rows_ref[1, half + i : half + i + 1, tok - 1 :])
        m_ref[i] = trailing_map(r_ref[half + i], trail, kh_ref[half + i], last, eye_key, key_dim)


def query_kernel(place, q_ref, kh_ref, rows_ref, r_ref, got_ref, got_own_ref, f_ref, qs):
    heads, tok, key_dim = kh_ref.shape
    half = heads // 2
    core = place[0]
    stage_rows(q_ref, qs)
    cum_row = rows_ref[1]
    cum_col = cum_row.T
    rows = lax.broadcasted_iota(jnp.int32, (tok, tok), 0)
    cols = lax.broadcasted_iota(jnp.int32, (tok, tok), 1)
    lower = rows >= cols
    for i in range(heads):
        head = ((1 - core) * half + i) if i < half else (core * half + i - half)
        q_wide = head_rows(qs, head, heads)
        q_inv = lax.rsqrt(jnp.sum(q_wide * q_wide, axis=1, keepdims=True) + 1e-6)
        dots = mm_nt(q_wide.astype(BF16), kh_ref[i])
        gap = cum_col[:, i : i + 1] - cum_row[i : i + 1, :]
        decay = jnp.exp(jnp.where(lower, gap, 0.0))
        scores = jnp.where(lower, dots * decay * q_inv * rows_ref[0, i : i + 1, :], 0.0)
        folded = mm3(scores, r_ref[i])
        gated = q_wide * (q_inv * jnp.exp(cum_col[:, i : i + 1]))
        f_ref[i] = jnp.concatenate(
            [folded[:, :key_dim] + gated, folded[:, key_dim:]], axis=1
        )

    @pl.when(core == 1)
    def _():
        for i in range(heads):
            earlier = got_own_ref[i] if i < half else got_ref[i - half]
            f_ref[i] = compose(f_ref[i], earlier, key_dim)


def chip_kernel(key_dim, outs_per, place, own_ref, got_ref, *out_refs):
    core, chip = place[0], place[1]
    half = own_ref.shape[0]
    owners = half // outs_per
    for r, out in enumerate(out_refs):
        owner = jnp.bitwise_xor(chip, r)
        owner = jnp.where(owner < owners, owner, 0)
        for j in range(outs_per):
            head = owner * outs_per + j
            own, got = own_ref[head], got_ref[head]
            earlier = jnp.where(core == 0, own, got)
            later = jnp.where(core == 0, got, own)
            out[j] = compose(later, earlier, key_dim)


def in_order(chip, maps):
    maps = list(maps)
    bit = 1
    while bit < len(maps):
        swapped = jnp.bitwise_and(chip, bit) != 0
        maps = [jnp.where(swapped, maps[i ^ bit], maps[i]) for i in range(len(maps))]
        bit *= 2
    return maps


def total_kernel(key_dim, place, *refs):
    maps, total = refs[:-1], refs[-1]
    chip = place[1]
    for j in range(total.shape[0]):
        level = [ref[j] for ref in maps]
        bit = 1
        while len(level) > 1:
            swapped = jnp.bitwise_and(chip, bit) != 0
            level = [
                compose(
                    jnp.where(swapped, low, high), jnp.where(swapped, high, low), key_dim
                )
                for low, high in zip(level[::2], level[1::2])
            ]
            bit *= 2
        total[j] = level[0]


def prefix_kernel(key_dim, place, *refs):
    maps, prefix = refs[:-1], refs[-1]
    for j in range(prefix.shape[1]):
        ordered = in_order(place[1], [ref[j] for ref in maps])
        running = ordered[0]
        prefix[0, j] = running
        for index in range(1, len(ordered) - 1):
            running = compose(ordered[index], running, key_dim)
            prefix[index, j] = running


def is_upper(place, level):
    return jnp.bitwise_and(jnp.right_shift(place[2], level), 1) == 1


def group_total_kernel(key_dim, level, place, total_ref, got_ref, out_ref):
    upper = is_upper(place, level)
    for j in range(total_ref.shape[0]):
        mine, got = total_ref[j], got_ref[j]
        later = jnp.where(upper, mine, got)
        earlier = jnp.where(upper, got, mine)
        if out_ref.shape[2] == mine.shape[1]:
            out_ref[j] = compose(later, earlier, key_dim)
        else:
            out_ref[j] = mm3(later[:, :key_dim], earlier[:, key_dim:]) + later[:, key_dim:]


def before_kernel(key_dim, level, place, got_ref, prefix_ref, out_ref):
    upper = is_upper(place, level)
    count = out_ref.shape[0]

    @pl.when(upper)
    def _():
        for j in range(out_ref.shape[1]):
            for index in range(count):
                if prefix_ref.shape[0] == count:
                    out_ref[index, j] = compose(prefix_ref[index, j], got_ref[j], key_dim)
                elif index == 0:
                    out_ref[index, j] = got_ref[j]
                else:
                    out_ref[index, j] = compose(prefix_ref[index - 1, j], got_ref[j], key_dim)

    @pl.when(jnp.logical_not(upper))
    def _():
        for j in range(out_ref.shape[1]):
            for index in range(count):
                if prefix_ref.shape[0] == count:
                    out_ref[index, j] = prefix_ref[index, j]
                elif index == 0:
                    out_ref[index, j] = jnp.where(
                        lax.broadcasted_iota(jnp.int32, out_ref.shape[2:], 0)
                        == lax.broadcasted_iota(jnp.int32, out_ref.shape[2:], 1),
                        1.0,
                        0.0,
                    )
                else:
                    out_ref[index, j] = prefix_ref[index - 1, j]


def enter_kernel(key_dim, level, place, got_ref, prefix_ref, *out_refs):
    chip = place[1]
    upper = is_upper(place, level)
    for j in range(got_ref.shape[0]):
        eh, el = split2(jnp.where(upper, got_ref[j], 0.0))
        twice = jnp.concatenate([eh, eh], axis=0)
        for r, out in enumerate(out_refs):
            one = prefix_ref[jnp.bitwise_xor(chip, r), j]
            th, tl = split2(one[:, :key_dim])
            moved = mm(jnp.concatenate([th, tl], axis=1), twice) + mm(th, el)
            out[j] = moved + one[:, key_dim:]


def output_kernel(per, owners, place, f_ref, *refs):
    o_ref, os0, os1 = refs[-3:]
    parts = refs[:-3]
    chips = len(parts) // 2
    heads, tok, wide = f_ref.shape
    half = heads // 2
    key_dim = wide - o_ref.shape[2]
    core, chip = place[0], place[1]
    mid = o_ref.shape[2] // 2

    def one(index, state, head):
        folded = f_ref[index]
        out = mm3(folded[:, :key_dim], state) + folded[:, key_dim:]
        os0[pl.ds(head, tok, stride=heads), :] = out[:, :mid]
        os1[pl.ds(head, tok, stride=heads), :] = out[:, mid:]

    for r in range(chips):
        owner = jnp.bitwise_xor(chip, r)

        def both(owner=owner, r=r):
            for j in range(per):
                head = owner * per + j
                one(half + head, parts[r][j], core * half + head)
                one(head, parts[chips + r][j], (1 - core) * half + head)

        if owners < chips:
            pl.when(owner < owners)(both)
        else:
            both()
    o_ref[:, :, :mid] = os0[...].reshape(tok, heads, mid).astype(BF16)
    o_ref[:, :, mid:] = os1[...].reshape(tok, heads, mid).astype(BF16)


def body(queries, key_rows, value_rows, log_gate, beta_rate):
    tok, heads, key_dim = queries.shape
    value_dim = value_rows.shape[2]
    wide = key_dim + value_dim
    half = heads // 2
    seq, grp = lax.axis_size("seq"), lax.axis_size("grp")
    chips = seq // 2
    owners = min(chips, half)
    per = half // owners
    place_seq, place_grp = lax.axis_index("seq"), lax.axis_index("grp")
    place = jnp.stack([place_seq % 2, place_seq // 2, place_grp]).astype(jnp.int32)
    f32 = lambda *shape: jax.ShapeDtypeStruct(shape, F32)
    tall = lambda width: pltpu.VMEM((tok * heads, width), F32)
    unit = 2 * tok * key_dim * key_dim
    sibling = [(i, i ^ 1) for i in range(seq)]

    give_map, basis, k_heads, trail, rows = pl.pallas_call(
        basis_kernel,
        out_shape=(
            f32(half, key_dim, wide),
            f32(heads, tok, wide),
            jax.ShapeDtypeStruct((heads, tok, key_dim), BF16),
            f32(half, tok, key_dim),
            f32(2, heads, tok),
        ),
        in_specs=[SMEM_SPEC] + [pl.BlockSpec(memory_space=pltpu.HBM)] * 4,
        out_specs=tuple(vmem(5)),
        scratch_shapes=[
            pltpu.VMEM((tok, heads, key_dim), BF16),
            pltpu.VMEM((tok, heads, value_dim), BF16),
            pltpu.VMEM((heads, tok), F32),
            pltpu.VMEM((heads, tok), F32),
            tall(key_dim),
            tall(value_dim // 2),
            tall(value_dim // 2),
            pltpu.SemaphoreType.DMA((4,)),
        ],
        compiler_params=pltpu.CompilerParams(vmem_limit_bytes=VMEM_LIMIT),
        cost_estimate=pl.CostEstimate(
            flops=50 * heads * unit, bytes_accessed=0, transcendentals=0
        ),
    )(place, key_rows, value_rows, log_gate, beta_rate)
    got_map = lax.ppermute(give_map, "seq", sibling)
    own_map = call(own_map_kernel, f32(half, key_dim, wide), flops=6 * half * unit)(
        place, basis, k_heads, trail, rows
    )
    chip_maps = call(
        functools.partial(chip_kernel, key_dim, per), [f32(per, key_dim, wide)] * chips
    )(place, own_map, got_map)

    def across(parts, to_owner):
        moved = [parts[0]]
        for r in range(1, chips):
            pairs = [
                (i, i ^ (2 * r))
                for i in range(seq)
                if ((i ^ (2 * r)) // 2 if to_owner else i // 2) < owners
            ]
            moved.append(lax.ppermute(parts[r], "seq", pairs))
        return moved

    owned = across(chip_maps, True)
    got_own = lax.ppermute(own_map, "seq", sibling)
    folded = call(
        query_kernel, f32(heads, tok, wide), [tall(key_dim)], flops=20 * heads * unit
    )(place, queries, k_heads, rows, basis, got_map, got_own)
    owned, folded = lax.optimization_barrier((owned, folded))
    total = call(functools.partial(total_kernel, key_dim), f32(per, key_dim, wide))(
        place, *owned
    )
    prefix = call(
        functools.partial(prefix_kernel, key_dim), f32(chips - 1, per, key_dim, wide)
    )(place, *owned)
    level = 0
    while 2 << level <= grp:
        swap = [(i, i ^ (1 << level)) for i in range(grp)]
        if 2 << level == grp:
            if level == 0:
                total = total[:, :, key_dim:]
            got_state = lax.ppermute(total, "grp", swap)
            states = call(
                functools.partial(enter_kernel, key_dim, level),
                [f32(per, key_dim, value_dim)] * chips,
            )(place, got_state, prefix)
        else:
            got = lax.ppermute(total, "grp", swap)
            width = value_dim if 4 << level == grp else wide
            total = call(
                functools.partial(group_total_kernel, key_dim, level), f32(per, key_dim, width)
            )(place, total, got)
            prefix = call(
                functools.partial(before_kernel, key_dim, level),
                f32(chips, per, key_dim, wide),
            )(place, got, prefix)
        level += 1
    arrived = across(states, False)
    others = [lax.ppermute(part, "seq", sibling) for part in arrived]
    return call(
        functools.partial(output_kernel, per, owners),
        jax.ShapeDtypeStruct((tok, heads, value_dim), BF16),
        [tall(value_dim // 2), tall(value_dim // 2)],
    )(place, folded, *arrived, *others)


def solution(mesh):
    return jax.shard_map(
        body,
        mesh=mesh,
        in_specs=(
            P(("grp", "seq"), None, None),
            P(("grp", "seq"), None, None),
            P(("grp", "seq"), None, None),
            P(None, ("grp", "seq")),
            P(None, ("grp", "seq")),
        ),
        out_specs=P(("grp", "seq"), None, None),
        check_vma=False,
    )
```

time: 59.9 us -> 54.6 us (0.912)
  Pallas kernels: 20.1 us -> 16.6 us
  waiting for transfers between devices: 24.3 us -> 20.8 us
  starting transfers between devices: 12.5 us -> 13.5 us
  local copies, waits for them, and re-layouts: 2.63 us -> 3.37 us
    pallas_call x10 -> x9, Pallas kernels: 20.1 us -> 10.5 us  [run(): pl.pallas_call(kernel, out_shape=out_shape, in_specs=[SMEM_SPEC] + vmem(l...]
    pallas_call x0 -> x1, Pallas kernels: none -> 6.06 us  [body(): pl.pallas_call(basis_kernel, out_shape=(f32(half, key_dim, wide), f32(hea...]
    ppermute x6, waiting for transfers between devices: 14.3 us -> 11.5 us  [across(): moved.append(lax.ppermute(parts[r], 'seq', pairs))]
    ppermute x2 -> x6, waiting for transfers between devices: 5.17 us -> 4.11 us  [the longest x1 3.09 us: body(): got_state = lax.ppermute(total, 'grp', swap)]
    ppermute x1, waiting for transfers between devices: 0.01 us -> 0.83 us  [body(): got_map = lax.ppermute(give_map, 'seq', sibling)]
    unnamed x12 -> x10, local copies, waits for them, and re-layouts: 2.62 us -> 3.37 us
    ppermute x2 -> x6, starting transfers between devices: 2.67 us -> 3.3 us  [the longest x1 2.65 us: body(): got_state = lax.ppermute(total, 'grp', swap)]
  transfers between devices with their start and end apart: 10 -> 14, of which waited for: 6 -> 9; matrix products, arithmetic and copies ran while one was open for 0% -> 0% of each run, Pallas kernels for 14% -> 11%
where the time goes in v2:
time: 54.6 us; the launch traced here: 54.4 us
  waiting for transfers between devices  20.8 us (38%)
  Pallas kernels  16.6 us (30%)
  starting transfers between devices  13.5 us (25%)
  local copies, waits for them, and re-layouts  3.37 us (6%)
    ppermute x6, waiting for transfers between devices, across(): moved.append(lax.ppermute(parts[r], 'seq', pairs))  11.5 us
    pallas_call x9, Pallas kernels, run(): pl.pallas_call(kernel, out_shape=out_shape, in_specs=[SMEM_SPEC] + vmem(l...  10.5 us
    ppermute x6, starting transfers between devices, across(): moved.append(lax.ppermute(parts[r], 'seq', pairs))  8.02 us
    pallas_call x1, Pallas kernels, body(): pl.pallas_call(basis_kernel, out_shape=(f32(half, key_dim, wide), f32(hea...  6.06 us
    ppermute x1, waiting for transfers between devices, body(): got = lax.ppermute(total, 'grp', swap)  4.32 us
    unnamed x10, local copies, waits for them, and re-layouts  3.37 us
    ppermute x1, waiting for transfers between devices, body(): got_state = lax.ppermute(total, 'grp', swap)  3.09 us
    ppermute x1, starting transfers between devices, body(): got_state = lax.ppermute(total, 'grp', swap)  2.65 us
  transfers between devices with their start and end apart: 14, of which 9 were waited for; matrix products, arithmetic and copies ran while one was open for 0% of the time, Pallas kernels for 11%

profile of v2, /device:TPU:0, one launch (start us, length us, event | category | flops | bytes accessed | tf_op | source)
XLA Modules:
  0.0 54.4 jit_solution(10002495631314838765)
XLA Ops:
  0.0 0.1 pad_add_fusion.place
  0.1 0.0 copy-start.1
  0.1 1.0 %copy-done.1 = bf16[128,8,256]{2,1,0:T(8,128)(2,1)S(1)} copy-done((bf16[128,8,256]{2,1,0:T(8,128)(2,1)S(1)}, bf16[128,8,256]{2,1,0:T(8,128)(2,1)}, u32[]{:S(2)}) %copy-start.1) | copy-done | bytes 524312
  1.1 0.0 copy-start.2
  1.1 0.9 %copy-done.2 = bf16[128,8,128]{2,1,0:T(8,128)(2,1)S(1)} copy-done((bf16[128,8,128]{2,1,0:T(8,128)(2,1)S(1)}, bf16[128,8,128]{2,1,0:T(8,128)(2,1)}, u32[]{:S(2)}) %copy-start.2) | copy-done | bytes 262168
  2.1 0.0 copy-start.3
  2.1 0.7 %copy-done.3 = f32[8,128]{1,0:T(8,128)S(1)} copy-done((f32[8,128]{1,0:T(8,128)S(1)}, f32[8,128]{1,0:T(8,128)}, u32[]{:S(2)}) %copy-start.3) | copy-done | bytes 4120
  2.8 0.0 copy-start.4
  2.8 0.7 %copy-done.4 = f32[8,128]{1,0:T(8,128)S(1)} copy-done((f32[8,128]{1,0:T(8,128)S(1)}, f32[8,128]{1,0:T(8,128)}, u32[]{:S(2)}) %copy-start.4) | copy-done | bytes 4120
  3.4 6.1 %shard_map.55 = (f32[4,128,384]{2,1,0:T(8,128)S(1)}, f32[8,128,384]{2,1,0:T(8,128)S(1)}, bf16[8,128,128]{2,1,0:T(8,128)(2,1)S(1)}, f32[4,128,128]{2,1,0:T(8,128)S(1)}, f32[2,8,128]{2,1,0:T(8,128)S(1)}) custom-call(s32[3]{0:T(128)S(1)} %pad_add_fusion.place, bf16[128,8,128]{2,1,0:T(8,128)(2,1)S(1)} %copy-done.2, bf16[128,8,256]{2,1,0:T(8,128)(2,1)S(1)} %copy-done.1, ...), custom_call_target="tpu_custom_call" | custom-call | flops 1677721600 | tf_op jit(solution)/shard_map/pallas_call | solution.py:420
  9.5 0.5 collective-permute-start
  10.0 0.9 %shard_map.56.own_ref = f32[4,128,384]{2,1,0:T(8,128)S(1)} custom-call(s32[3]{0:T(128)S(1)} %pad_add_fusion.place, f32[8,128,384]{2,1,0:T(8,128)S(1)} %get-tuple-element.23.r_ref, bf16[8,128,128]{2,1,0:T(8,128)(2,1)S(1)} %get-tuple-element.24.kh_ref, f32[4,128,128]{2,1,0:T(8,128)S(1)} %get-tuple-element.25.trail_ref, f32[2,8,128]{2,1,0:T(8,128)S(1)} %get-tuple-element.26.rows_ref), custom_call_target="tpu_custom_call" | custom-call | flops 100663296 | tf_op jit(solution)/shard_map/pallas_call | solution.py:60
  11.0 0.1 collective-permute-start.4
  11.1 0.8 %collective-permute-done.got_ref = f32[4,128,384]{2,1,0:T(8,128)S(1)} collective-permute-done((f32[4,128,384]{2,1,0:T(8,128)S(1)}, f32[4,128,384]{2,1,0:T(8,128)S(1)}, u32[]{:S(2)}, u32[]{:S(2)}) %collective-permute-start) | collective-permute-done | bytes 786464 | tf_op jit(solution)/shard_map/ppermute | solution.py:446
  11.9 1.0 %shard_map.57 = (f32[1,128,384]{2,1,0:T(8,128)S(1)}, f32[1,128,384]{2,1,0:T(8,128)S(1)}, f32[1,128,384]{2,1,0:T(8,128)S(1)}, f32[1,128,384]{2,1,0:T(8,128)S(1)}) custom-call(s32[3]{0:T(128)S(1)} %pad_add_fusion.place, f32[4,128,384]{2,1,0:T(8,128)S(1)} %shard_map.56.own_ref, f32[4,128,384]{2,1,0:T(8,128)S(1)} %collective-permute-done.got_ref), custom_call_target="tpu_custom_call" | custom-call | tf_op jit(solution)/shard_map/pallas_call | solution.py:60
  12.9 2.9 %collective-permute-start.1 = (f32[1,128,384]{2,1,0:T(8,128)S(1)}, f32[1,128,384]{2,1,0:T(8,128)S(1)}, u32[]{:S(2)}, u32[]{:S(2)}) collective-permute-start(f32[1,128,384]{2,1,0:T(8,128)S(1)} %get-tuple-element.29), channel_id=1, source_target_pairs={{0,8},{4,12},{8,0},{12,4},{16,24},{20,28},{24,16},{28,20},{1,9},{5... | collective-permute-start | bytes 589832 | tf_op jit(solution)/shard_map/ppermute | solution.py:462
  15.9 1.5 %collective-permute-start.2 = (f32[1,128,384]{2,1,0:T(8,128)S(1)}, f32[1,128,384]{2,1,0:T(8,128)S(1)}, u32[]{:S(2)}, u32[]{:S(2)}) collective-permute-start(f32[1,128,384]{2,1,0:T(8,128)S(1)} %get-tuple-element.30), channel_id=1, source_target_pairs={{0,16},{4,20},{8,24},{12,28},{16,0},{20,4},{24,8},{28,12},{1,17},{... | collective-permute-start | bytes 589832 | tf_op jit(solution)/shard_map/ppermute | solution.py:462
  17.4 0.0 collective-permute-start.3
  17.4 0.0 collective-permute-done.4.got_own_ref
  17.4 0.0 copy-done
  17.4 2.4 %shard_map.58.f_ref = f32[8,128,384]{2,1,0:T(8,128)S(1)} custom-call(s32[3]{0:T(128)S(1)} %pad_add_fusion.place, bf16[128,8,128]{2,1,0:T(8,128)(2,1)S(1)} %copy-done, bf16[8,128,128]{2,1,0:T(8,128)(2,1)S(1)} %get-tuple-element.24.kh_ref, f32[2,8,128]{2,1,0:T(8,128)S(1)} %get-tuple-element.26.rows_ref, f32[8,128,384]{2,1,0:T(8,128)S(1)} %get-tuple-element.23.r_ref, ...), custom_call_target="tpu_custom_call" | custom-call | flops 671088640 | tf_op jit(solution)/shard_map/pallas_call | solution.py:60
  19.8 1.8 %collective-permute-done.1.refs_1_ = f32[1,128,384]{2,1,0:T(8,128)S(1)} collective-permute-done((f32[1,128,384]{2,1,0:T(8,128)S(1)}, f32[1,128,384]{2,1,0:T(8,128)S(1)}, u32[]{:S(2)}, u32[]{:S(2)}) %collective-permute-start.1) | collective-permute-done | bytes 196640 | tf_op jit(solution)/shard_map/ppermute | solution.py:462
  21.5 5.2 %collective-permute-done.2.refs_2_ = f32[1,128,384]{2,1,0:T(8,128)S(1)} collective-permute-done((f32[1,128,384]{2,1,0:T(8,128)S(1)}, f32[1,128,384]{2,1,0:T(8,128)S(1)}, u32[]{:S(2)}, u32[]{:S(2)}) %collective-permute-start.2) | collective-permute-done | bytes 196640 | tf_op jit(solution)/shard_map/ppermute | solution.py:462
  26.7 0.0 collective-permute-done.3.refs_3_
  26.7 1.1 %shard_map.59.total_ref = f32[1,128,384]{2,1,0:T(8,128)S(1)} custom-call(s32[3]{0:T(128)S(1)} %pad_add_fusion.place, f32[1,128,384]{2,1,0:T(8,128)S(1)} %get-tuple-element.33.refs_0_, f32[1,128,384]{2,1,0:T(8,128)S(1)} %collective-permute-done.1.refs_1_, f32[1,128,384]{2,1,0:T(8,128)S(1)} %collective-permute-done.2.refs_2_, ...), custom_call_target="tpu_custom_call" | custom-call | tf_op jit(solution)/shard_map/pallas_call | solution.py:60
  27.8 1.6 %collective-permute-start.5 = (f32[1,128,384]{2,1,0:T(8,128)S(1)}, f32[1,128,384]{2,1,0:T(8,128)S(1)}, u32[]{:S(2)}, u32[]{:S(2)}) collective-permute-start(f32[1,128,384]{2,1,0:T(8,128)S(1)} %shard_map.59.total_ref), channel_id=1, source_target_pairs={{0,1},{1,0},{2,3},{3,2},{4,5},{5,4},{6,7},{7,6},{8,9},{9,8},{10,11... | collective-permute-start | bytes 589832 | tf_op jit(solution)/shard_map/ppermute | solution.py:489
  29.4 4.3 %collective-permute-done.5.got_ref = f32[1,128,384]{2,1,0:T(8,128)S(1)} collective-permute-done((f32[1,128,384]{2,1,0:T(8,128)S(1)}, f32[1,128,384]{2,1,0:T(8,128)S(1)}, u32[]{:S(2)}, u32[]{:S(2)}) %collective-permute-start.5) | collective-permute-done | bytes 196640 | tf_op jit(solution)/shard_map/ppermute | solution.py:489
  33.8 0.7 %shard_map.60 = f32[1,128,256]{2,1,0:T(8,128)S(1)} custom-call(s32[3]{0:T(128)S(1)} %pad_add_fusion.place, f32[1,128,384]{2,1,0:T(8,128)S(1)} %shard_map.59.total_ref, f32[1,128,384]{2,1,0:T(8,128)S(1)} %collective-permute-done.5.got_ref), custom_call_target="tpu_custom_call" | custom-call | tf_op jit(solution)/shard_map/pallas_call | solution.py:60
  34.5 2.6 %collective-permute-start.6 = (f32[1,128,256]{2,1,0:T(8,128)S(1)}, f32[1,128,256]{2,1,0:T(8,128)S(1)}, u32[]{:S(2)}, u32[]{:S(2)}) collective-permute-start(f32[1,128,256]{2,1,0:T(8,128)S(1)} %shard_map.60), channel_id=1, source_target_pairs={{0,2},{1,3},{2,0},{3,1},{4,6},{5,7},{6,4},{7,5},{8,10},{9,11},{10,... | collective-permute-start | bytes 393224 | tf_op jit(solution)/shard_map/ppermute | solution.py:483
  37.2 1.0 %shard_map.61.prefix_ref = f32[3,1,128,384]{3,2,1,0:T(8,128)S(1)} custom-call(s32[3]{0:T(128)S(1)} %pad_add_fusion.place, f32[1,128,384]{2,1,0:T(8,128)S(1)} %get-tuple-element.33.refs_0_, f32[1,128,384]{2,1,0:T(8,128)S(1)} %collective-permute-done.1.refs_1_, f32[1,128,384]{2,1,0:T(8,128)S(1)} %collective-permute-done.2.refs_2_, ...), custom_call_target="tpu_custom_call" | custom-call | tf_op jit(solution)/shard_map/pallas_call | solution.py:60
  38.2 0.6 %shard_map.62.prefix_ref = f32[4,1,128,384]{3,2,1,0:T(8,128)S(1)} custom-call(s32[3]{0:T(128)S(1)} %pad_add_fusion.place, f32[1,128,384]{2,1,0:T(8,128)S(1)} %collective-permute-done.5.got_ref, f32[3,1,128,384]{3,2,1,0:T(8,128)S(1)} %shard_map.61.prefix_ref), custom_call_target="tpu_custom_call" | custom-call | tf_op jit(solution)/shard_map/pallas_call | solution.py:60
  38.8 3.1 %collective-permute-done.6.got_ref = f32[1,128,256]{2,1,0:T(8,128)S(1)} collective-permute-done((f32[1,128,256]{2,1,0:T(8,128)S(1)}, f32[1,128,256]{2,1,0:T(8,128)S(1)}, u32[]{:S(2)}, u32[]{:S(2)}) %collective-permute-start.6) | collective-permute-done | bytes 131104 | tf_op jit(solution)/shard_map/ppermute | solution.py:483
  41.9 0.8 %shard_map.63 = (f32[1,128,256]{2,1,0:T(8,128)S(1)}, f32[1,128,256]{2,1,0:T(8,128)S(1)}, f32[1,128,256]{2,1,0:T(8,128)S(1)}, f32[1,128,256]{2,1,0:T(8,128)S(1)}) custom-call(s32[3]{0:T(128)S(1)} %pad_add_fusion.place, f32[1,128,256]{2,1,0:T(8,128)S(1)} %collective-permute-done.6.got_ref, f32[4,1,128,384]{3,2,1,0:T(8,128)S(1)} %shard_map.62.prefix_ref), custom_call_target="tpu_custom_call" | custom-call | tf_op jit(solution)/shard_map/pallas_call | solution.py:60
  42.7 1.7 %collective-permute-start.7 = (f32[1,128,256]{2,1,0:T(8,128)S(1)}, f32[1,128,256]{2,1,0:T(8,128)S(1)}, u32[]{:S(2)}, u32[]{:S(2)}) collective-permute-start(f32[1,128,256]{2,1,0:T(8,128)S(1)} %get-tuple-element.38), channel_id=1, source_target_pairs={{0,8},{4,12},{8,0},{12,4},{16,24},{20,28},{24,16},{28,20},{1,9},{5... | collective-permute-start | bytes 393224 | tf_op jit(solution)/shard_map/ppermute | solution.py:462
  44.4 0.3 collective-permute-start.8
  44.7 1.5 %collective-permute-start.9 = (f32[1,128,256]{2,1,0:T(8,128)S(1)}, f32[1,128,256]{2,1,0:T(8,128)S(1)}, u32[]{:S(2)}, u32[]{:S(2)}) collective-permute-start(f32[1,128,256]{2,1,0:T(8,128)S(1)} %get-tuple-element.40), channel_id=1, source_target_pairs={{0,24},{4,28},{8,16},{12,20},{16,8},{20,12},{24,0},{28,4},{1,25},{... | collective-permute-start | bytes 393224 | tf_op jit(solution)/shard_map/ppermute | solution.py:462
  46.2 0.0 collective-permute-start.10
  46.2 1.9 %collective-permute-done.7.refs_1_ = f32[1,128,256]{2,1,0:T(8,128)S(1)} collective-permute-done((f32[1,128,256]{2,1,0:T(8,128)S(1)}, f32[1,128,256]{2,1,0:T(8,128)S(1)}, u32[]{:S(2)}, u32[]{:S(2)}) %collective-permute-start.7) | collective-permute-done | bytes 131104 | tf_op jit(solution)/shard_map/ppermute | solution.py:462
  48.2 0.0 collective-permute-start.11
  48.2 2.6 %collective-permute-done.8.refs_2_ = f32[1,128,256]{2,1,0:T(8,128)S(1)} collective-permute-done((f32[1,128,256]{2,1,0:T(8,128)S(1)}, f32[1,128,256]{2,1,0:T(8,128)S(1)}, u32[]{:S(2)}, u32[]{:S(2)}) %collective-permute-start.8) | collective-permute-done | bytes 131104 | tf_op jit(solution)/shard_map/ppermute | solution.py:462
  50.8 0.0 collective-permute-start.12
  50.8 0.0 collective-permute-done.9.refs_3_
  50.8 0.5 collective-permute-start.13
  51.3 0.0 collective-permute-done.10.refs_4_
  51.3 0.0 collective-permute-done.11.refs_5_
  51.3 0.8 %collective-permute-done.12.refs_6_ = f32[1,128,256]{2,1,0:T(8,128)S(1)} collective-permute-done((f32[1,128,256]{2,1,0:T(8,128)S(1)}, f32[1,128,256]{2,1,0:T(8,128)S(1)}, u32[]{:S(2)}, u32[]{:S(2)}) %collective-permute-start.12) | collective-permute-done | bytes 131104 | tf_op jit(solution)/shard_map/ppermute | solution.py:500
  52.1 0.2 collective-permute-done.13.refs_7_
  52.3 2.0 %shard_map.64 = bf16[128,8,256]{2,1,0:T(8,128)(2,1)} custom-call(s32[3]{0:T(128)S(1)} %pad_add_fusion.place, f32[8,128,384]{2,1,0:T(8,128)S(1)} %shard_map.58.f_ref, f32[1,128,256]{2,1,0:T(8,128)S(1)} %get-tuple-element.37.refs_0_, f32[1,128,256]{2,1,0:T(8,128)S(1)} %collective-permute-done.7.refs_1_, f32[1,128,256]{2,1,0:T(8,128)S(1)} %collective-permute-done.8.refs_2_, ...), custom_call_target="tpu_custom_call" | custom-call | tf_op jit(solution)/shard_map/pallas_call | solution.py:60
  (1 shorter events, 0.0 us)
Async XLA Ops:
  0.1 1.0 %copy-start.1 = (bf16[128,8,256]{2,1,0:T(8,128)(2,1)S(1)}, bf16[128,8,256]{2,1,0:T(8,128)(2,1)}, u32[]{:S(2)}) copy-start(bf16[128,8,256]{2,1,0:T(8,128)(2,1)} %v_hbm.1) | copy-start | bytes 1572868
  1.1 0.9 %copy-start.2 = (bf16[128,8,128]{2,1,0:T(8,128)(2,1)S(1)}, bf16[128,8,128]{2,1,0:T(8,128)(2,1)}, u32[]{:S(2)}) copy-start(bf16[128,8,128]{2,1,0:T(8,128)(2,1)} %k_hbm.1) | copy-start | bytes 786436
  2.1 0.7 %copy-start.3 = (f32[8,128]{1,0:T(8,128)S(1)}, f32[8,128]{1,0:T(8,128)}, u32[]{:S(2)}) copy-start(f32[8,128]{1,0:T(8,128)} %g_hbm.1) | copy-start | bytes 12292
  2.8 0.7 %copy-start.4 = (f32[8,128]{1,0:T(8,128)S(1)}, f32[8,128]{1,0:T(8,128)}, u32[]{:S(2)}) copy-start(f32[8,128]{1,0:T(8,128)} %b_hbm.1) | copy-start | bytes 12292
  9.5 2.4 %collective-permute-start = (f32[4,128,384]{2,1,0:T(8,128)S(1)}, f32[4,128,384]{2,1,0:T(8,128)S(1)}, u32[]{:S(2)}, u32[]{:S(2)}) collective-permute-start(f32[4,128,384]{2,1,0:T(8,128)S(1)} %get-tuple-element.27), channel_id=1, source_target_pairs={{0,4},{4,0},{8,12},{12,8},{16,20},{20,16},{24,28},{28,24},{1,5},{5... | collective-permute-start | bytes 2359304 | tf_op jit(solution)/shard_map/ppermute | solution.py:446
  10.0 7.4 %copy-start = (bf16[128,8,128]{2,1,0:T(8,128)(2,1)S(1)}, bf16[128,8,128]{2,1,0:T(8,128)(2,1)}, u32[]{:S(2)}) copy-start(bf16[128,8,128]{2,1,0:T(8,128)(2,1)} %q_ref.1) | copy-start | bytes 786436
  11.0 6.4 %collective-permute-start.4 = (f32[4,128,384]{2,1,0:T(8,128)S(1)}, f32[4,128,384]{2,1,0:T(8,128)S(1)}, u32[]{:S(2)}, u32[]{:S(2)}) collective-permute-start(f32[4,128,384]{2,1,0:T(8,128)S(1)} %shard_map.56.own_ref), channel_id=1, source_target_pairs={{0,4},{4,0},{8,12},{12,8},{16,20},{20,16},{24,28},{28,24},{1,5},{5... | collective-permute-start | bytes 2359304 | tf_op jit(solution)/shard_map/ppermute | solution.py:466
  12.9 8.6 %collective-permute-start.1 = (f32[1,128,384]{2,1,0:T(8,128)S(1)}, f32[1,128,384]{2,1,0:T(8,128)S(1)}, u32[]{:S(2)}, u32[]{:S(2)}) collective-permute-start(f32[1,128,384]{2,1,0:T(8,128)S(1)} %get-tuple-element.29), channel_id=1, source_target_pairs={{0,8},{4,12},{8,0},{12,4},{16,24},{20,28},{24,16},{28,20},{1,9},{5... | collective-permute-start | bytes 589832 | tf_op jit(solution)/shard_map/ppermute | solution.py:462
  15.9 10.9 %collective-permute-start.2 = (f32[1,128,384]{2,1,0:T(8,128)S(1)}, f32[1,128,384]{2,1,0:T(8,128)S(1)}, u32[]{:S(2)}, u32[]{:S(2)}) collective-permute-start(f32[1,128,384]{2,1,0:T(8,128)S(1)} %get-tuple-element.30), channel_id=1, source_target_pairs={{0,16},{4,20},{8,24},{12,28},{16,0},{20,4},{24,8},{28,12},{1,17},{... | collective-permute-start | bytes 589832 | tf_op jit(solution)/shard_map/ppermute | solution.py:462
  17.4 9.4 %collective-permute-start.3 = (f32[1,128,384]{2,1,0:T(8,128)S(1)}, f32[1,128,384]{2,1,0:T(8,128)S(1)}, u32[]{:S(2)}, u32[]{:S(2)}) collective-permute-start(f32[1,128,384]{2,1,0:T(8,128)S(1)} %get-tuple-element.31), channel_id=1, source_target_pairs={{0,24},{4,28},{8,16},{12,20},{16,8},{20,12},{24,0},{28,4},{1,25},{... | collective-permute-start | bytes 589832 | tf_op jit(solution)/shard_map/ppermute | solution.py:462
  27.8 6.0 %collective-permute-start.5 = (f32[1,128,384]{2,1,0:T(8,128)S(1)}, f32[1,128,384]{2,1,0:T(8,128)S(1)}, u32[]{:S(2)}, u32[]{:S(2)}) collective-permute-start(f32[1,128,384]{2,1,0:T(8,128)S(1)} %shard_map.59.total_ref), channel_id=1, source_target_pairs={{0,1},{1,0},{2,3},{3,2},{4,5},{5,4},{6,7},{7,6},{8,9},{9,8},{10,11... | collective-permute-start | bytes 589832 | tf_op jit(solution)/shard_map/ppermute | solution.py:489
  34.5 7.3 %collective-permute-start.6 = (f32[1,128,256]{2,1,0:T(8,128)S(1)}, f32[1,128,256]{2,1,0:T(8,128)S(1)}, u32[]{:S(2)}, u32[]{:S(2)}) collective-permute-start(f32[1,128,256]{2,1,0:T(8,128)S(1)} %shard_map.60), channel_id=1, source_target_pairs={{0,2},{1,3},{2,0},{3,1},{4,6},{5,7},{6,4},{7,5},{8,10},{9,11},{10,... | collective-permute-start | bytes 393224 | tf_op jit(solution)/shard_map/ppermute | solution.py:483
  42.7 5.5 %collective-permute-start.7 = (f32[1,128,256]{2,1,0:T(8,128)S(1)}, f32[1,128,256]{2,1,0:T(8,128)S(1)}, u32[]{:S(2)}, u32[]{:S(2)}) collective-permute-start(f32[1,128,256]{2,1,0:T(8,128)S(1)} %get-tuple-element.38), channel_id=1, source_target_pairs={{0,8},{4,12},{8,0},{12,4},{16,24},{20,28},{24,16},{28,20},{1,9},{5... | collective-permute-start | bytes 393224 | tf_op jit(solution)/shard_map/ppermute | solution.py:462
  44.4 6.4 %collective-permute-start.8 = (f32[1,128,256]{2,1,0:T(8,128)S(1)}, f32[1,128,256]{2,1,0:T(8,128)S(1)}, u32[]{:S(2)}, u32[]{:S(2)}) collective-permute-start(f32[1,128,256]{2,1,0:T(8,128)S(1)} %get-tuple-element.39), channel_id=1, source_target_pairs={{0,16},{4,20},{8,24},{12,28},{16,0},{20,4},{24,8},{28,12},{1,17},{... | collective-permute-start | bytes 393224 | tf_op jit(solution)/shard_map/ppermute | solution.py:462
  44.7 6.1 %collective-permute-start.9 = (f32[1,128,256]{2,1,0:T(8,128)S(1)}, f32[1,128,256]{2,1,0:T(8,128)S(1)}, u32[]{:S(2)}, u32[]{:S(2)}) collective-permute-start(f32[1,128,256]{2,1,0:T(8,128)S(1)} %get-tuple-element.40), channel_id=1, source_target_pairs={{0,24},{4,28},{8,16},{12,20},{16,8},{20,12},{24,0},{28,4},{1,25},{... | collective-permute-start | bytes 393224 | tf_op jit(solution)/shard_map/ppermute | solution.py:462
  46.2 5.1 %collective-permute-start.10 = (f32[1,128,256]{2,1,0:T(8,128)S(1)}, f32[1,128,256]{2,1,0:T(8,128)S(1)}, u32[]{:S(2)}, u32[]{:S(2)}) collective-permute-start(f32[1,128,256]{2,1,0:T(8,128)S(1)} %get-tuple-element.37.refs_0_), channel_id=1, source_target_pairs={{0,4},{4,0},{8,12},{12,8},{16,20},{20,16},{24,28},{28,24},{1,5},{5... | collective-permute-start | bytes 393224 | tf_op jit(solution)/shard_map/ppermute | solution.py:500
  48.2 3.1 %collective-permute-start.11 = (f32[1,128,256]{2,1,0:T(8,128)S(1)}, f32[1,128,256]{2,1,0:T(8,128)S(1)}, u32[]{:S(2)}, u32[]{:S(2)}) collective-permute-start(f32[1,128,256]{2,1,0:T(8,128)S(1)} %collective-permute-done.7.refs_1_), channel_id=1, source_target_pairs={{0,4},{4,0},{8,12},{12,8},{16,20},{20,16},{24,28},{28,24},{1,5},{5... | collective-permute-start | bytes 393224 | tf_op jit(solution)/shard_map/ppermute | solution.py:500
  50.8 1.3 %collective-permute-start.12 = (f32[1,128,256]{2,1,0:T(8,128)S(1)}, f32[1,128,256]{2,1,0:T(8,128)S(1)}, u32[]{:S(2)}, u32[]{:S(2)}) collective-permute-start(f32[1,128,256]{2,1,0:T(8,128)S(1)} %collective-permute-done.8.refs_2_), channel_id=1, source_target_pairs={{0,4},{4,0},{8,12},{12,8},{16,20},{20,16},{24,28},{28,24},{1,5},{5... | collective-permute-start | bytes 393224 | tf_op jit(solution)/shard_map/ppermute | solution.py:500
  50.8 1.5 %collective-permute-start.13 = (f32[1,128,256]{2,1,0:T(8,128)S(1)}, f32[1,128,256]{2,1,0:T(8,128)S(1)}, u32[]{:S(2)}, u32[]{:S(2)}) collective-permute-start(f32[1,128,256]{2,1,0:T(8,128)S(1)} %collective-permute-done.9.refs_3_), channel_id=1, source_target_pairs={{0,4},{4,0},{8,12},{12,8},{16,20},{20,16},{24,28},{28,24},{1,5},{5... | collective-permute-start | bytes 393224 | tf_op jit(solution)/shard_map/ppermute | solution.py:500

commit v3 on v2

--- a/solution.py
+++ b/solution.py
@@ -95,28 +95,79 @@
     return jnp.where(flip, jnp.concatenate([a[half:], a[:half]], axis=0), a)
 
 
-def block_inverse(strict, rows, cols):
-    size = rows.shape[0]
+def mm3_packed(lhs, rhs):
+    rows = lhs.shape[0]
+    width = rhs.shape[1] // 2
+    high, low = split2(lhs)
+    out = mm(jnp.concatenate([high, low], axis=0), rhs)
+    return out[:rows, :width] + (out[:rows, width:] + out[rows:, :width])
+
+
+def block_inverse(strict):
+    size = strict[0].shape[0]
     base = min(16, size)
-    eye = rows == cols
-    within = (rows // base) == (cols // base)
-    power = [jnp.where(within, -a, 0.0) for a in strict]
-    inverse = [jnp.where(eye, 1.0, a) for a in power]
+    rows = lax.broadcasted_iota(jnp.int32, (size, size), 0)
+    cols = lax.broadcasted_iota(jnp.int32, (size, size), 1)
+
+    def ones_where(mask):
+        return jnp.where(mask, 1.0, 0.0).astype(BF16)
+
+    def spread(compact, mask):
+        count = size // compact.shape[0]
+        return jnp.concatenate(
+            [jnp.concatenate([part] * count, axis=0) * mask for part in split2(compact)], axis=1
+        )
+
+    lane = lax.broadcasted_iota(jnp.int32, (base, size), 1)
+    line = lax.broadcasted_iota(jnp.int32, (base, size), 0)
+    power, inverse = [], []
+    for a in strict:
+        compact = jnp.zeros((base, size), F32)
+        for n in range(size // base):
+            compact = jnp.where(lane // base == n, -a[n * base : (n + 1) * base, :], compact)
+        power.append(compact)
+        inverse.append(jnp.where(lane % base == line, 1.0, compact))
+    mask = ones_where(rows // base == cols // base)
+    wide = [spread(p, mask) for p in power]
+    power = [mm3_packed(p, w) for p, w in zip(power, wide)]
     span = 2
     while span < base:
-        power = [mm3(a, a) for a in power]
-        inverse = [x + mm3(x, a) for x, a in zip(inverse, power)]
+        wide = [spread(p, mask) for p in power]
+        if span * 2 < base:
+            both = [
+                mm3_packed(jnp.concatenate([p, x], axis=0), w)
+                for p, x, w in zip(power, inverse, wide)
+            ]
+            power = [a[:base] for a in both]
+            inverse = [x + a[base:] for x, a in zip(inverse, both)]
+        else:
+            inverse = [x + mm3_packed(x, w) for x, w in zip(inverse, wide)]
         span *= 2
+    parts = [split2(a) for a in strict]
     span = base
     while span < size:
-        joint = ((rows // (2 * span)) == (cols // (2 * span))) & (
-            (rows // span) != (cols // span)
+        joint = ones_where(
+            (rows // (2 * span) == cols // (2 * span)) & (rows // span != cols // span)
         )
-        off = [jnp.where(joint, a, 0.0) for a in strict]
-        first = [mm3(x, o) for x, o in zip(inverse, off)]
-        inverse = [x - mm3(f, x) for f, x in zip(first, inverse)]
+        mask = ones_where(rows // span == cols // span)
+        even = (
+            (lax.broadcasted_iota(jnp.int32, (span, size), 1) // span) % 2
+        ) == 0
+        off = [jnp.concatenate([h * joint, l * joint], axis=1) for h, l in parts]
+        first = [mm3_packed(x, o) for x, o in zip(inverse, off)]
+        second = [mm3_packed(f, spread(x, mask)) for f, x in zip(first, inverse)]
+        inverse = [
+            jnp.concatenate([jnp.where(even, x, 0.0), jnp.where(even, -y, x)], axis=0)
+            for x, y in zip(inverse, second)
+        ]
         span *= 2
     return inverse
+
+
+def updates_basis(inverse, k_raw, v_raw, beta, key_scale):
+    key_part = mm_exact_right(inverse * key_scale, k_raw)
+    value_part = mm_exact_right(inverse * beta, v_raw)
+    return jnp.concatenate([key_part, value_part], axis=1)
 
 
 def trailing_map(basis, trail, k_raw, last, eye_key, key_dim):
@@ -136,7 +187,7 @@
 
 
 def basis_kernel(
-    place, k_hbm, v_hbm, g_hbm, b_hbm, m_ref, r_ref, kh_ref, trail_ref, rows_ref,
+    place, k_hbm, v_hbm, g_hbm, b_hbm, m_ref, r_ref, kh_ref, trail_ref, rows_ref, inverse_ref, v_own_ref,
     k_ref, v_ref, g_ref, b_ref, ks, vs0, vs1, sems,
 ):
     copies = [
@@ -186,43 +237,50 @@
         decay = jnp.exp(jnp.where(lower, gap, 0.0))
         left = beta_col[:, i : i + 1] * inv_col[i]
         strict.append(jnp.where(lower, gram[i] * decay * left * inv_row[i], 0.0))
-    inverse = block_inverse(strict, rows, cols)
+    inverse = block_inverse(strict)
     copies[3].wait()
     wide = v_ref[...].astype(F32)
     vs0[...] = wide[:, :, : value_dim // 2].reshape(vs0.shape)
     vs1[...] = wide[:, :, value_dim // 2 :].reshape(vs1.shape)
     rows_ref[0] = jnp.concatenate(inv_row, axis=0)
     rows_ref[1] = cum_row
+    rows_ref[2] = beta_row
+    rows_ref[3] = -(decay_row * beta_row * jnp.concatenate(inv_row, axis=0))
     for i in every:
         v_raw = jnp.concatenate(
             [head_rows(vs0, order[i], heads), head_rows(vs1, order[i], heads)], axis=1
         ).astype(BF16)
-        beta_i = beta_row[i : i + 1, :]
-        key_scale = -(decay_row[i : i + 1, :] * beta_i * inv_row[i])
-        key_part = mm_exact_right(inverse[i] * key_scale, k_raw[i])
-        value_part = mm_exact_right(inverse[i] * beta_i, v_raw)
-        basis = jnp.concatenate([key_part, value_part], axis=1)
-        r_ref[i] = basis
         trail = trail_col[:, i : i + 1] * inv_col[i]
         if i < half:
+            beta_i = beta_row[i : i + 1, :]
+            key_scale = -(decay_row[i : i + 1, :] * beta_i * inv_row[i])
+            basis = updates_basis(inverse[i], k_raw[i], v_raw, beta_i, key_scale)
+            r_ref[i] = basis
             m_ref[i] = trailing_map(
                 basis, trail, k_raw[i], jnp.exp(last_row[i : i + 1, :]), eye_key, key_dim
             )
         else:
             trail_ref[i - half] = jnp.broadcast_to(trail, (tok, key_dim))
-
-
-def own_map_kernel(place, r_ref, kh_ref, trail_ref, rows_ref, m_ref):
+            inverse_ref[i - half] = inverse[i]
+            v_own_ref[i - half] = v_raw
+
+
+def own_map_kernel(place, inverse_ref, kh_ref, v_ref, trail_ref, rows_ref, m_ref, r_ref):
     half, key_dim, wide = m_ref.shape
     tok = r_ref.shape[1]
     eye_key = eye_mask(key_dim)
     for i in range(half):
-        trail = trail_ref[i][:, :1]
-        last = jnp.exp(rows_ref[1, half + i : half + i + 1, tok - 1 :])
-        m_ref[i] = trailing_map(r_ref[half + i], trail, kh_ref[half + i], last, eye_key, key_dim)
-
-
-def query_kernel(place, q_ref, kh_ref, rows_ref, r_ref, got_ref, got_own_ref, f_ref, qs):
+        at = slice(half + i, half + i + 1)
+        k_raw = kh_ref[half + i]
+        basis = updates_basis(
+            inverse_ref[i], k_raw, v_ref[i], rows_ref[2, at, :], rows_ref[3, at, :]
+        )
+        r_ref[i] = basis
+        last = jnp.exp(rows_ref[1, at, tok - 1 :])
+        m_ref[i] = trailing_map(basis, trail_ref[i][:, :1], k_raw, last, eye_key, key_dim)
+
+
+def query_kernel(place, q_ref, kh_ref, rows_ref, r_give, r_own, got_ref, got_own_ref, f_ref, qs):
     heads, tok, key_dim = kh_ref.shape
     half = heads // 2
     core = place[0]
@@ -240,7 +298,7 @@
         gap = cum_col[:, i : i + 1] - cum_row[i : i + 1, :]
         decay = jnp.exp(jnp.where(lower, gap, 0.0))
         scores = jnp.where(lower, dots * decay * q_inv * rows_ref[0, i : i + 1, :], 0.0)
-        folded = mm3(scores, r_ref[i])
+        folded = mm3(scores, r_give[i] if i < half else r_own[i - half])
         gated = q_wide * (q_inv * jnp.exp(cum_col[:, i : i + 1]))
         f_ref[i] = jnp.concatenate(
             [folded[:, :key_dim] + gated, folded[:, key_dim:]], axis=1
@@ -368,19 +426,41 @@
             out[j] = moved + one[:, key_dim:]
 
 
-def output_kernel(per, owners, place, f_ref, *refs):
+def read_out(folded, state):
+    key_dim = state.shape[0]
+    return mm3(folded[:, :key_dim], state) + folded[:, key_dim:]
+
+
+def early_kernel(per, owners, first, chips, place, f_ref, *refs):
+    parts, out_ref = refs[:-1], refs[-1]
+    half = f_ref.shape[0] // 2
+    chip = place[1]
+    count = len(parts) // 2
+    for n in range(count):
+        owner = jnp.bitwise_xor(chip, first + n)
+
+        def both(owner=owner, n=n):
+            for j in range(per):
+                head = owner * per + j
+                out_ref[n, 0, j] = read_out(f_ref[half + head], parts[n][j])
+                out_ref[n, 1, j] = read_out(f_ref[head], parts[count + n][j])
+
+        if owners < chips:
+            pl.when(owner < owners)(both)
+        else:
+            both()
+
+
+def output_kernel(per, owners, first, chips, place, f_ref, early_ref, *refs):
     o_ref, os0, os1 = refs[-3:]
     parts = refs[:-3]
-    chips = len(parts) // 2
+    count = len(parts) // 2
     heads, tok, wide = f_ref.shape
     half = heads // 2
-    key_dim = wide - o_ref.shape[2]
     core, chip = place[0], place[1]
     mid = o_ref.shape[2] // 2
 
-    def one(index, state, head):
-        folded = f_ref[index]
-        out = mm3(folded[:, :key_dim], state) + folded[:, key_dim:]
+    def put(head, out):
         os0[pl.ds(head, tok, stride=heads), :] = out[:, :mid]
         os1[pl.ds(head, tok, stride=heads), :] = out[:, mid:]
 
@@ -390,8 +470,13 @@
         def both(owner=owner, r=r):
             for j in range(per):
                 head = owner * per + j
-                one(half + head, parts[r][j], core * half + head)
-                one(head, parts[chips + r][j], (1 - core) * half + head)
+                if r < first:
+                    own, other = early_ref[r, 0, j], early_ref[r, 1, j]
+                else:
+                    own = read_out(f_ref[half + head], parts[r - first][j])
+                    other = read_out(f_ref[head], parts[count + r - first][j])
+                put(core * half + head, own)
+                put((1 - core) * half + head, other)
 
         if owners < chips:
             pl.when(owner < owners)(both)
@@ -417,17 +502,19 @@
     unit = 2 * tok * key_dim * key_dim
     sibling = [(i, i ^ 1) for i in range(seq)]
 
-    give_map, basis, k_heads, trail, rows = pl.pallas_call(
+    give_map, give_basis, k_heads, trail, rows, inverse, v_own = pl.pallas_call(
         basis_kernel,
         out_shape=(
             f32(half, key_dim, wide),
-            f32(heads, tok, wide),
+            f32(half, tok, wide),
             jax.ShapeDtypeStruct((heads, tok, key_dim), BF16),
             f32(half, tok, key_dim),
-            f32(2, heads, tok),
+            f32(4, heads, tok),
+            f32(half, tok, tok),
+            jax.ShapeDtypeStruct((half, tok, value_dim), BF16),
         ),
         in_specs=[SMEM_SPEC] + [pl.BlockSpec(memory_space=pltpu.HBM)] * 4,
-        out_specs=tuple(vmem(5)),
+        out_specs=tuple(vmem(7)),
         scratch_shapes=[
             pltpu.VMEM((tok, heads, key_dim), BF16),
             pltpu.VMEM((tok, heads, value_dim), BF16),
@@ -442,11 +529,13 @@
         cost_estimate=pl.CostEstimate(
             flops=50 * heads * unit, bytes_accessed=0, transcendentals=0
         ),
-    )(place, key_rows, value_rows, log_gate, beta_rate)
+    )(place, *(pltpu.with_memory_space_constraint(a, pltpu.HBM) for a in (key_rows, value_rows, log_gate, beta_rate)))
     got_map = lax.ppermute(give_map, "seq", sibling)
-    own_map = call(own_map_kernel, f32(half, key_dim, wide), flops=6 * half * unit)(
-        place, basis, k_heads, trail, rows
-    )
+    own_map, own_basis = call(
+        own_map_kernel,
+        (f32(half, key_dim, wide), f32(half, tok, wide)),
+        flops=12 * half * unit,
+    )(place, inverse, k_heads, v_own, trail, rows)
     chip_maps = call(
         functools.partial(chip_kernel, key_dim, per), [f32(per, key_dim, wide)] * chips
     )(place, own_map, got_map)
@@ -466,7 +555,7 @@
     got_own = lax.ppermute(own_map, "seq", sibling)
     folded = call(
         query_kernel, f32(heads, tok, wide), [tall(key_dim)], flops=20 * heads * unit
-    )(place, queries, k_heads, rows, basis, got_map, got_own)
+    )(place, queries, k_heads, rows, give_basis, own_basis, got_map, got_own)
     owned, folded = lax.optimization_barrier((owned, folded))
     total = call(functools.partial(total_kernel, key_dim), f32(per, key_dim, wide))(
         place, *owned
@@ -498,11 +587,17 @@
         level += 1
     arrived = across(states, False)
     others = [lax.ppermute(part, "seq", sibling) for part in arrived]
+    first = max(chips // 2, 1)
+    early = call(
+        functools.partial(early_kernel, per, owners, 0, chips),
+        f32(first, 2, per, tok, value_dim),
+        flops=6 * first * per * unit,
+    )(place, folded, *arrived[:first], *others[:first])
     return call(
-        functools.partial(output_kernel, per, owners),
+        functools.partial(output_kernel, per, owners, first, chips),
         jax.ShapeDtypeStruct((tok, heads, value_dim), BF16),
         [tall(value_dim // 2), tall(value_dim // 2)],
-    )(place, folded, *arrived, *others)
+    )(place, folded, early, *arrived[first:], *others[first:])
 
 
 def solution(mesh):

time: 54.6 us -> 50.5 us (0.925)
  local copies, waits for them, and re-layouts: 3.37 us -> 0.01 us
  waiting for transfers between devices: 20.8 us -> 19.3 us
  Pallas kernels: 16.6 us -> 17.3 us
    unnamed x10 -> x2, local copies, waits for them, and re-layouts: 3.37 us -> 0.01 us
    pallas_call x9 -> x10, Pallas kernels: 10.5 us -> 11.8 us  [run(): pl.pallas_call(kernel, out_shape=out_shape, in_specs=[SMEM_SPEC] + vmem(l...]
    ppermute x4, waiting for transfers between devices: 1.02 us -> 0.16 us  [body(): others = [lax.ppermute(part, 'seq', sibling) for part in arrived]]
    ppermute x1, waiting for transfers between devices: 0.83 us -> 0.24 us  [body(): got_map = lax.ppermute(give_map, 'seq', sibling)]
  transfers between devices with their start and end apart: 14 -> 14, of which waited for: 9 -> 8; matrix products, arithmetic and copies ran while one was open for 0% -> 0% of each run, Pallas kernels for 11% -> 15%
where the time goes in v3:
time: 50.5 us; the launch traced here: 50.3 us
  waiting for transfers between devices  19.3 us (38%)
  Pallas kernels  17.3 us (34%)
  starting transfers between devices  13.5 us (27%)
    pallas_call x10, Pallas kernels, run(): pl.pallas_call(kernel, out_shape=out_shape, in_specs=[SMEM_SPEC] + vmem(l...  11.8 us
    ppermute x6, waiting for transfers between devices, across(): moved.append(lax.ppermute(parts[r], 'seq', pairs))  11.5 us
    ppermute x6, starting transfers between devices, across(): moved.append(lax.ppermute(parts[r], 'seq', pairs))  8.02 us
    pallas_call x1, Pallas kernels, body(): pl.pallas_call(basis_kernel, out_shape=(f32(half, key_dim, wide), f32(hal...  5.55 us
    ppermute x1, waiting for transfers between devices, body(): got = lax.ppermute(total, 'grp', swap)  4.32 us
    ppermute x1, waiting for transfers between devices, body(): got_state = lax.ppermute(total, 'grp', swap)  3.07 us
    ppermute x1, starting transfers between devices, body(): got_state = lax.ppermute(total, 'grp', swap)  2.66 us
    ppermute x1, starting transfers between devices, body(): got = lax.ppermute(total, 'grp', swap)  1.64 us
  transfers between devices with their start and end apart: 14, of which 8 were waited for; matrix products, arithmetic and copies ran while one was open for 0% of the time, Pallas kernels for 15%

profile of v3, /device:TPU:0, one launch (start us, length us, event | category | flops | bytes accessed | tf_op | source)
XLA Modules:
  0.0 50.3 jit_solution(4170421880792537548)
XLA Ops:
  0.0 0.1 pad_add_fusion.place
  0.1 5.5 %shard_map.55 = (f32[4,128,384]{2,1,0:T(8,128)S(1)}, f32[4,128,384]{2,1,0:T(8,128)S(1)}, bf16[8,128,128]{2,1,0:T(8,128)(2,1)S(1)}, f32[4,128,128]{2,1,0:T(8,128)...) custom-call(s32[3]{0:T(128)S(1)} %pad_add_fusion.place, ...), custom_call_target="tpu_custom_call" | custom-call | flops 1677721600 | tf_op jit(solution)/shard_map/pallas_call | solution.py:505
  5.6 0.0 copy-start
  5.6 0.5 %collective-permute-start = (f32[4,128,384]{2,1,0:T(8,128)S(1)}, f32[4,128,384]{2,1,0:T(8,128)S(1)}, u32[]{:S(2)}, u32[]{:S(2)}) collective-permute-start(f32[4,128,384]{2,1,0:T(8,128)S(1)} %get-tuple-element.33), channel_id=1, source_target_pairs={{0,4},{4,0},{8,12},{12,8},{16,20},{20,16},{24,28},{28,24},{1,5},{5... | collective-permute-start | bytes 2359304 | tf_op jit(solution)/shard_map/ppermute | solution.py:533
  6.2 1.5 %shard_map.56 = (f32[4,128,384]{2,1,0:T(8,128)S(1)}, f32[4,128,384]{2,1,0:T(8,128)S(1)}) custom-call(s32[3]{0:T(128)S(1)} %pad_add_fusion.place, f32[4,128,128]{2,1,0:T(8,128)S(1)} %get-tuple-element.27.inverse_ref, bf16[8,128,128]{2,1,0:T(8,128)(2,1)S(1)} %get-tuple-element.28.kh_ref, bf16[4,128,256]{2,1,0:T(8,128)(2,1)S(1)} %get-tuple-element.29.v_ref, ...), custom_call_target="tpu_custom_call" | custom-call | flops 201326592 | tf_op jit(solution)/shard_map/pallas_call | solution.py:60
  7.7 0.1 collective-permute-start.4
  7.8 0.2 collective-permute-done.got_ref
  8.1 1.0 %shard_map.57 = (f32[1,128,384]{2,1,0:T(8,128)S(1)}, f32[1,128,384]{2,1,0:T(8,128)S(1)}, f32[1,128,384]{2,1,0:T(8,128)S(1)}, f32[1,128,384]{2,1,0:T(8,128)S(1)}) custom-call(s32[3]{0:T(128)S(1)} %pad_add_fusion.place, f32[4,128,384]{2,1,0:T(8,128)S(1)} %get-tuple-element.32.own_ref, f32[4,128,384]{2,1,0:T(8,128)S(1)} %collective-permute-done.got_ref), custom_call_target="tpu_custom_call" | custom-call | tf_op jit(solution)/shard_map/pallas_call | solution.py:60
  9.1 2.9 %collective-permute-start.1 = (f32[1,128,384]{2,1,0:T(8,128)S(1)}, f32[1,128,384]{2,1,0:T(8,128)S(1)}, u32[]{:S(2)}, u32[]{:S(2)}) collective-permute-start(f32[1,128,384]{2,1,0:T(8,128)S(1)} %get-tuple-element.35), channel_id=1, source_target_pairs={{0,8},{4,12},{8,0},{12,4},{16,24},{20,28},{24,16},{28,20},{1,9},{5... | collective-permute-start | bytes 589832 | tf_op jit(solution)/shard_map/ppermute | solution.py:551
  12.0 1.5 %collective-permute-start.2 = (f32[1,128,384]{2,1,0:T(8,128)S(1)}, f32[1,128,384]{2,1,0:T(8,128)S(1)}, u32[]{:S(2)}, u32[]{:S(2)}) collective-permute-start(f32[1,128,384]{2,1,0:T(8,128)S(1)} %get-tuple-element.36), channel_id=1, source_target_pairs={{0,16},{4,20},{8,24},{12,28},{16,0},{20,4},{24,8},{28,12},{1,17},{... | collective-permute-start | bytes 589832 | tf_op jit(solution)/shard_map/ppermute | solution.py:551
  13.5 0.0 collective-permute-start.3
  13.5 0.0 collective-permute-done.4.got_own_ref
  13.5 0.0 copy-done
  13.5 2.4 %shard_map.58.f_ref = f32[8,128,384]{2,1,0:T(8,128)S(1)} custom-call(s32[3]{0:T(128)S(1)} %pad_add_fusion.place, bf16[128,8,128]{2,1,0:T(8,128)(2,1)S(1)} %copy-done, bf16[8,128,128]{2,1,0:T(8,128)(2,1)S(1)} %get-tuple-element.28.kh_ref, f32[4,8,128]{2,1,0:T(8,128)S(1)} %get-tuple-element.31.rows_ref, f32[4,128,384]{2,1,0:T(8,128)S(1)} %get-tuple-element.38.r_give, ...), custom_call_target="tpu_custom_call" | custom-call | flops 671088640 | tf_op jit(solution)/shard_map/pallas_call | solution.py:60
  15.9 1.8 %collective-permute-done.1.refs_1_ = f32[1,128,384]{2,1,0:T(8,128)S(1)} collective-permute-done((f32[1,128,384]{2,1,0:T(8,128)S(1)}, f32[1,128,384]{2,1,0:T(8,128)S(1)}, u32[]{:S(2)}, u32[]{:S(2)}) %collective-permute-start.1) | collective-permute-done | bytes 196640 | tf_op jit(solution)/shard_map/ppermute | solution.py:551
  17.7 5.2 %collective-permute-done.2.refs_2_ = f32[1,128,384]{2,1,0:T(8,128)S(1)} collective-permute-done((f32[1,128,384]{2,1,0:T(8,128)S(1)}, f32[1,128,384]{2,1,0:T(8,128)S(1)}, u32[]{:S(2)}, u32[]{:S(2)}) %collective-permute-start.2) | collective-permute-done | bytes 196640 | tf_op jit(solution)/shard_map/ppermute | solution.py:551
  22.9 0.0 collective-permute-done.3.refs_3_
  22.9 1.1 %shard_map.59.total_ref = f32[1,128,384]{2,1,0:T(8,128)S(1)} custom-call(s32[3]{0:T(128)S(1)} %pad_add_fusion.place, f32[1,128,384]{2,1,0:T(8,128)S(1)} %get-tuple-element.41.refs_0_, f32[1,128,384]{2,1,0:T(8,128)S(1)} %collective-permute-done.1.refs_1_, f32[1,128,384]{2,1,0:T(8,128)S(1)} %collective-permute-done.2.refs_2_, ...), custom_call_target="tpu_custom_call" | custom-call | tf_op jit(solution)/shard_map/pallas_call | solution.py:60
  23.9 1.6 %collective-permute-start.5 = (f32[1,128,384]{2,1,0:T(8,128)S(1)}, f32[1,128,384]{2,1,0:T(8,128)S(1)}, u32[]{:S(2)}, u32[]{:S(2)}) collective-permute-start(f32[1,128,384]{2,1,0:T(8,128)S(1)} %shard_map.59.total_ref), channel_id=1, source_target_pairs={{0,1},{1,0},{2,3},{3,2},{4,5},{5,4},{6,7},{7,6},{8,9},{9,8},{10,11... | collective-permute-start | bytes 589832 | tf_op jit(solution)/shard_map/ppermute | solution.py:578
  25.6 4.3 %collective-permute-done.5.got_ref = f32[1,128,384]{2,1,0:T(8,128)S(1)} collective-permute-done((f32[1,128,384]{2,1,0:T(8,128)S(1)}, f32[1,128,384]{2,1,0:T(8,128)S(1)}, u32[]{:S(2)}, u32[]{:S(2)}) %collective-permute-start.5) | collective-permute-done | bytes 196640 | tf_op jit(solution)/shard_map/ppermute | solution.py:578
  29.9 0.7 %shard_map.60 = f32[1,128,256]{2,1,0:T(8,128)S(1)} custom-call(s32[3]{0:T(128)S(1)} %pad_add_fusion.place, f32[1,128,384]{2,1,0:T(8,128)S(1)} %shard_map.59.total_ref, f32[1,128,384]{2,1,0:T(8,128)S(1)} %collective-permute-done.5.got_ref), custom_call_target="tpu_custom_call" | custom-call | tf_op jit(solution)/shard_map/pallas_call | solution.py:60
  30.6 2.7 %collective-permute-start.6 = (f32[1,128,256]{2,1,0:T(8,128)S(1)}, f32[1,128,256]{2,1,0:T(8,128)S(1)}, u32[]{:S(2)}, u32[]{:S(2)}) collective-permute-start(f32[1,128,256]{2,1,0:T(8,128)S(1)} %shard_map.60), channel_id=1, source_target_pairs={{0,2},{1,3},{2,0},{3,1},{4,6},{5,7},{6,4},{7,5},{8,10},{9,11},{10,... | collective-permute-start | bytes 393224 | tf_op jit(solution)/shard_map/ppermute | solution.py:572
  33.3 1.0 %shard_map.61.prefix_ref = f32[3,1,128,384]{3,2,1,0:T(8,128)S(1)} custom-call(s32[3]{0:T(128)S(1)} %pad_add_fusion.place, f32[1,128,384]{2,1,0:T(8,128)S(1)} %get-tuple-element.41.refs_0_, f32[1,128,384]{2,1,0:T(8,128)S(1)} %collective-permute-done.1.refs_1_, f32[1,128,384]{2,1,0:T(8,128)S(1)} %collective-permute-done.2.refs_2_, ...), custom_call_target="tpu_custom_call" | custom-call | tf_op jit(solution)/shard_map/pallas_call | solution.py:60
  34.3 0.6 %shard_map.62.prefix_ref = f32[4,1,128,384]{3,2,1,0:T(8,128)S(1)} custom-call(s32[3]{0:T(128)S(1)} %pad_add_fusion.place, f32[1,128,384]{2,1,0:T(8,128)S(1)} %collective-permute-done.5.got_ref, f32[3,1,128,384]{3,2,1,0:T(8,128)S(1)} %shard_map.61.prefix_ref), custom_call_target="tpu_custom_call" | custom-call | tf_op jit(solution)/shard_map/pallas_call | solution.py:60
  34.9 3.1 %collective-permute-done.6.got_ref = f32[1,128,256]{2,1,0:T(8,128)S(1)} collective-permute-done((f32[1,128,256]{2,1,0:T(8,128)S(1)}, f32[1,128,256]{2,1,0:T(8,128)S(1)}, u32[]{:S(2)}, u32[]{:S(2)}) %collective-permute-start.6) | collective-permute-done | bytes 131104 | tf_op jit(solution)/shard_map/ppermute | solution.py:572
  37.9 0.8 %shard_map.63 = (f32[1,128,256]{2,1,0:T(8,128)S(1)}, f32[1,128,256]{2,1,0:T(8,128)S(1)}, f32[1,128,256]{2,1,0:T(8,128)S(1)}, f32[1,128,256]{2,1,0:T(8,128)S(1)}) custom-call(s32[3]{0:T(128)S(1)} %pad_add_fusion.place, f32[1,128,256]{2,1,0:T(8,128)S(1)} %collective-permute-done.6.got_ref, f32[4,1,128,384]{3,2,1,0:T(8,128)S(1)} %shard_map.62.prefix_ref), custom_call_target="tpu_custom_call" | custom-call | tf_op jit(solution)/shard_map/pallas_call | solution.py:60
  38.8 1.7 %collective-permute-start.7 = (f32[1,128,256]{2,1,0:T(8,128)S(1)}, f32[1,128,256]{2,1,0:T(8,128)S(1)}, u32[]{:S(2)}, u32[]{:S(2)}) collective-permute-start(f32[1,128,256]{2,1,0:T(8,128)S(1)} %get-tuple-element.46), channel_id=1, source_target_pairs={{0,8},{4,12},{8,0},{12,4},{16,24},{20,28},{24,16},{28,20},{1,9},{5... | collective-permute-start | bytes 393224 | tf_op jit(solution)/shard_map/ppermute | solution.py:551
  40.5 0.3 collective-permute-start.10
  40.9 1.5 %collective-permute-start.11 = (f32[1,128,256]{2,1,0:T(8,128)S(1)}, f32[1,128,256]{2,1,0:T(8,128)S(1)}, u32[]{:S(2)}, u32[]{:S(2)}) collective-permute-start(f32[1,128,256]{2,1,0:T(8,128)S(1)} %get-tuple-element.48), channel_id=1, source_target_pairs={{0,24},{4,28},{8,16},{12,20},{16,8},{20,12},{24,0},{28,4},{1,25},{... | collective-permute-start | bytes 393224 | tf_op jit(solution)/shard_map/ppermute | solution.py:551
  42.3 0.0 collective-permute-start.8
  42.3 1.9 %collective-permute-done.7.refs_1_ = f32[1,128,256]{2,1,0:T(8,128)S(1)} collective-permute-done((f32[1,128,256]{2,1,0:T(8,128)S(1)}, f32[1,128,256]{2,1,0:T(8,128)S(1)}, u32[]{:S(2)}, u32[]{:S(2)}) %collective-permute-start.7) | collective-permute-done | bytes 131104 | tf_op jit(solution)/shard_map/ppermute | solution.py:551
  44.3 0.0 collective-permute-start.9
  44.3 2.6 %collective-permute-done.10.refs_0_ = f32[1,128,256]{2,1,0:T(8,128)S(1)} collective-permute-done((f32[1,128,256]{2,1,0:T(8,128)S(1)}, f32[1,128,256]{2,1,0:T(8,128)S(1)}, u32[]{:S(2)}, u32[]{:S(2)}) %collective-permute-start.10) | collective-permute-done | bytes 131104 | tf_op jit(solution)/shard_map/ppermute | solution.py:551
  46.9 0.0 collective-permute-start.12
  46.9 0.0 collective-permute-done.11.refs_1_
  46.9 0.5 %collective-permute-start.13 = (f32[1,128,256]{2,1,0:T(8,128)S(1)}, f32[1,128,256]{2,1,0:T(8,128)S(1)}, u32[]{:S(2)}, u32[]{:S(2)}) collective-permute-start(f32[1,128,256]{2,1,0:T(8,128)S(1)} %collective-permute-done.11.refs_1_), channel_id=1, source_target_pairs={{0,4},{4,0},{8,12},{12,8},{16,20},{20,16},{24,28},{28,24},{1,5},{5... | collective-permute-start | bytes 393224 | tf_op jit(solution)/shard_map/ppermute | solution.py:589
  47.4 0.0 collective-permute-done.8.refs_2_
  47.4 0.0 collective-permute-done.9.refs_3_
  47.4 0.8 %shard_map.64.early_ref = f32[2,2,1,128,256]{4,3,2,1,0:T(8,128)S(1)} custom-call(s32[3]{0:T(128)S(1)} %pad_add_fusion.place, f32[8,128,384]{2,1,0:T(8,128)S(1)} %shard_map.58.f_ref, f32[1,128,256]{2,1,0:T(8,128)S(1)} %get-tuple-element.45.refs_0_, f32[1,128,256]{2,1,0:T(8,128)S(1)} %collective-permute-done.7.refs_1_, ...), custom_call_target="tpu_custom_call" | custom-call | flops 50331648 | tf_op jit(solution)/shard_map/pallas_call | solution.py:60
  48.3 0.0 collective-permute-done.12.refs_2_
  48.3 0.2 collective-permute-done.13.refs_3_
  48.4 1.9 %shard_map.65 = bf16[128,8,256]{2,1,0:T(8,128)(2,1)} custom-call(s32[3]{0:T(128)S(1)} %pad_add_fusion.place, f32[8,128,384]{2,1,0:T(8,128)S(1)} %shard_map.58.f_ref, f32[2,2,1,128,256]{4,3,2,1,0:T(8,128)S(1)} %shard_map.64.early_ref, f32[1,128,256]{2,1,0:T(8,128)S(1)} %collective-permute-done.10.refs_0_, f32[1,128,256]{2,1,0:T(8,128)S(1)} %collective-permute-done.11.refs_1_, ...), custom_call_target="tpu_custom_call" | custom-call | tf_op jit(solution)/shard_map/pallas_call | solution.py:60
Async XLA Ops:
  5.6 7.9 %copy-start = (bf16[128,8,128]{2,1,0:T(8,128)(2,1)S(1)}, bf16[128,8,128]{2,1,0:T(8,128)(2,1)}, u32[]{:S(2)}) copy-start(bf16[128,8,128]{2,1,0:T(8,128)(2,1)} %q_ref.1) | copy-start | bytes 786436
  5.6 2.4 %collective-permute-start = (f32[4,128,384]{2,1,0:T(8,128)S(1)}, f32[4,128,384]{2,1,0:T(8,128)S(1)}, u32[]{:S(2)}, u32[]{:S(2)}) collective-permute-start(f32[4,128,384]{2,1,0:T(8,128)S(1)} %get-tuple-element.33), channel_id=1, source_target_pairs={{0,4},{4,0},{8,12},{12,8},{16,20},{20,16},{24,28},{28,24},{1,5},{5... | collective-permute-start | bytes 2359304 | tf_op jit(solution)/shard_map/ppermute | solution.py:533
  7.7 5.8 %collective-permute-start.4 = (f32[4,128,384]{2,1,0:T(8,128)S(1)}, f32[4,128,384]{2,1,0:T(8,128)S(1)}, u32[]{:S(2)}, u32[]{:S(2)}) collective-permute-start(f32[4,128,384]{2,1,0:T(8,128)S(1)} %get-tuple-element.32.own_ref), channel_id=1, source_target_pairs={{0,4},{4,0},{8,12},{12,8},{16,20},{20,16},{24,28},{28,24},{1,5},{5... | collective-permute-start | bytes 2359304 | tf_op jit(solution)/shard_map/ppermute | solution.py:555
  9.1 8.6 %collective-permute-start.1 = (f32[1,128,384]{2,1,0:T(8,128)S(1)}, f32[1,128,384]{2,1,0:T(8,128)S(1)}, u32[]{:S(2)}, u32[]{:S(2)}) collective-permute-start(f32[1,128,384]{2,1,0:T(8,128)S(1)} %get-tuple-element.35), channel_id=1, source_target_pairs={{0,8},{4,12},{8,0},{12,4},{16,24},{20,28},{24,16},{28,20},{1,9},{5... | collective-permute-start | bytes 589832 | tf_op jit(solution)/shard_map/ppermute | solution.py:551
  12.0 10.9 %collective-permute-start.2 = (f32[1,128,384]{2,1,0:T(8,128)S(1)}, f32[1,128,384]{2,1,0:T(8,128)S(1)}, u32[]{:S(2)}, u32[]{:S(2)}) collective-permute-start(f32[1,128,384]{2,1,0:T(8,128)S(1)} %get-tuple-element.36), channel_id=1, source_target_pairs={{0,16},{4,20},{8,24},{12,28},{16,0},{20,4},{24,8},{28,12},{1,17},{... | collective-permute-start | bytes 589832 | tf_op jit(solution)/shard_map/ppermute | solution.py:551
  13.5 9.4 %collective-permute-start.3 = (f32[1,128,384]{2,1,0:T(8,128)S(1)}, f32[1,128,384]{2,1,0:T(8,128)S(1)}, u32[]{:S(2)}, u32[]{:S(2)}) collective-permute-start(f32[1,128,384]{2,1,0:T(8,128)S(1)} %get-tuple-element.37), channel_id=1, source_target_pairs={{0,24},{4,28},{8,16},{12,20},{16,8},{20,12},{24,0},{28,4},{1,25},{... | collective-permute-start | bytes 589832 | tf_op jit(solution)/shard_map/ppermute | solution.py:551
  23.9 6.0 %collective-permute-start.5 = (f32[1,128,384]{2,1,0:T(8,128)S(1)}, f32[1,128,384]{2,1,0:T(8,128)S(1)}, u32[]{:S(2)}, u32[]{:S(2)}) collective-permute-start(f32[1,128,384]{2,1,0:T(8,128)S(1)} %shard_map.59.total_ref), channel_id=1, source_target_pairs={{0,1},{1,0},{2,3},{3,2},{4,5},{5,4},{6,7},{7,6},{8,9},{9,8},{10,11... | collective-permute-start | bytes 589832 | tf_op jit(solution)/shard_map/ppermute | solution.py:578
  30.6 7.3 %collective-permute-start.6 = (f32[1,128,256]{2,1,0:T(8,128)S(1)}, f32[1,128,256]{2,1,0:T(8,128)S(1)}, u32[]{:S(2)}, u32[]{:S(2)}) collective-permute-start(f32[1,128,256]{2,1,0:T(8,128)S(1)} %shard_map.60), channel_id=1, source_target_pairs={{0,2},{1,3},{2,0},{3,1},{4,6},{5,7},{6,4},{7,5},{8,10},{9,11},{10,... | collective-permute-start | bytes 393224 | tf_op jit(solution)/shard_map/ppermute | solution.py:572
  38.8 5.5 %collective-permute-start.7 = (f32[1,128,256]{2,1,0:T(8,128)S(1)}, f32[1,128,256]{2,1,0:T(8,128)S(1)}, u32[]{:S(2)}, u32[]{:S(2)}) collective-permute-start(f32[1,128,256]{2,1,0:T(8,128)S(1)} %get-tuple-element.46), channel_id=1, source_target_pairs={{0,8},{4,12},{8,0},{12,4},{16,24},{20,28},{24,16},{28,20},{1,9},{5... | collective-permute-start | bytes 393224 | tf_op jit(solution)/shard_map/ppermute | solution.py:551
  40.5 6.4 %collective-permute-start.10 = (f32[1,128,256]{2,1,0:T(8,128)S(1)}, f32[1,128,256]{2,1,0:T(8,128)S(1)}, u32[]{:S(2)}, u32[]{:S(2)}) collective-permute-start(f32[1,128,256]{2,1,0:T(8,128)S(1)} %get-tuple-element.47), channel_id=1, source_target_pairs={{0,16},{4,20},{8,24},{12,28},{16,0},{20,4},{24,8},{28,12},{1,17},{... | collective-permute-start | bytes 393224 | tf_op jit(solution)/shard_map/ppermute | solution.py:551
  40.9 6.0 %collective-permute-start.11 = (f32[1,128,256]{2,1,0:T(8,128)S(1)}, f32[1,128,256]{2,1,0:T(8,128)S(1)}, u32[]{:S(2)}, u32[]{:S(2)}) collective-permute-start(f32[1,128,256]{2,1,0:T(8,128)S(1)} %get-tuple-element.48), channel_id=1, source_target_pairs={{0,24},{4,28},{8,16},{12,20},{16,8},{20,12},{24,0},{28,4},{1,25},{... | collective-permute-start | bytes 393224 | tf_op jit(solution)/shard_map/ppermute | solution.py:551
  42.3 5.1 %collective-permute-start.8 = (f32[1,128,256]{2,1,0:T(8,128)S(1)}, f32[1,128,256]{2,1,0:T(8,128)S(1)}, u32[]{:S(2)}, u32[]{:S(2)}) collective-permute-start(f32[1,128,256]{2,1,0:T(8,128)S(1)} %get-tuple-element.45.refs_0_), channel_id=1, source_target_pairs={{0,4},{4,0},{8,12},{12,8},{16,20},{20,16},{24,28},{28,24},{1,5},{5... | collective-permute-start | bytes 393224 | tf_op jit(solution)/shard_map/ppermute | solution.py:589
  44.3 3.1 %collective-permute-start.9 = (f32[1,128,256]{2,1,0:T(8,128)S(1)}, f32[1,128,256]{2,1,0:T(8,128)S(1)}, u32[]{:S(2)}, u32[]{:S(2)}) collective-permute-start(f32[1,128,256]{2,1,0:T(8,128)S(1)} %collective-permute-done.7.refs_1_), channel_id=1, source_target_pairs={{0,4},{4,0},{8,12},{12,8},{16,20},{20,16},{24,28},{28,24},{1,5},{5... | collective-permute-start | bytes 393224 | tf_op jit(solution)/shard_map/ppermute | solution.py:589
  46.9 1.4 %collective-permute-start.12 = (f32[1,128,256]{2,1,0:T(8,128)S(1)}, f32[1,128,256]{2,1,0:T(8,128)S(1)}, u32[]{:S(2)}, u32[]{:S(2)}) collective-permute-start(f32[1,128,256]{2,1,0:T(8,128)S(1)} %collective-permute-done.10.refs_0_), channel_id=1, source_target_pairs={{0,4},{4,0},{8,12},{12,8},{16,20},{20,16},{24,28},{28,24},{1,5},{5... | collective-permute-start | bytes 393224 | tf_op jit(solution)/shard_map/ppermute | solution.py:589
  46.9 1.5 %collective-permute-start.13 = (f32[1,128,256]{2,1,0:T(8,128)S(1)}, f32[1,128,256]{2,1,0:T(8,128)S(1)}, u32[]{:S(2)}, u32[]{:S(2)}) collective-permute-start(f32[1,128,256]{2,1,0:T(8,128)S(1)} %collective-permute-done.11.refs_1_), channel_id=1, source_target_pairs={{0,4},{4,0},{8,12},{12,8},{16,20},{20,16},{24,28},{28,24},{1,5},{5... | collective-permute-start | bytes 393224 | tf_op jit(solution)/shard_map/ppermute | solution.py:589

commit v4 on v3

--- a/solution.py
+++ b/solution.py
@@ -52,20 +52,25 @@
     return [pl.BlockSpec(memory_space=pltpu.VMEM)] * count
 
 
-SMEM_SPEC = pl.BlockSpec(memory_space=pltpu.SMEM)
+def placed(kernel):
+    def run(*refs):
+        seq = lax.axis_index("seq")
+        kernel((lax.rem(seq, 2), lax.div(seq, 2), lax.axis_index("grp")), *refs)
+
+    return run
 
 
 def call(kernel, out_shape, scratch=(), flops=0, nbytes=0):
-    def run(place, *arrays):
+    def run(*arrays):
         return pl.pallas_call(
-            kernel,
+            placed(kernel),
             out_shape=out_shape,
-            in_specs=[SMEM_SPEC] + vmem(len(arrays)),
+            in_specs=vmem(len(arrays)),
             out_specs=jax.tree.map(lambda _: pl.BlockSpec(memory_space=pltpu.VMEM), out_shape),
             scratch_shapes=list(scratch),
             compiler_params=pltpu.CompilerParams(vmem_limit_bytes=VMEM_LIMIT),
             cost_estimate=pl.CostEstimate(flops=flops, bytes_accessed=nbytes, transcendentals=0),
-        )(place, *arrays)
+        )(*arrays)
 
     return run
 
@@ -237,24 +242,29 @@
         decay = jnp.exp(jnp.where(lower, gap, 0.0))
         left = beta_col[:, i : i + 1] * inv_col[i]
         strict.append(jnp.where(lower, gram[i] * decay * left * inv_row[i], 0.0))
-    inverse = block_inverse(strict)
     copies[3].wait()
     wide = v_ref[...].astype(F32)
     vs0[...] = wide[:, :, : value_dim // 2].reshape(vs0.shape)
     vs1[...] = wide[:, :, value_dim // 2 :].reshape(vs1.shape)
+    v_raw = [
+        jnp.concatenate(
+            [head_rows(vs0, h, heads), head_rows(vs1, h, heads)], axis=1
+        ).astype(BF16)
+        for h in order
+    ]
+    for i in range(half):
+        v_own_ref[i] = v_raw[half + i]
+    inverse = block_inverse(strict)
     rows_ref[0] = jnp.concatenate(inv_row, axis=0)
     rows_ref[1] = cum_row
     rows_ref[2] = beta_row
     rows_ref[3] = -(decay_row * beta_row * jnp.concatenate(inv_row, axis=0))
     for i in every:
-        v_raw = jnp.concatenate(
-            [head_rows(vs0, order[i], heads), head_rows(vs1, order[i], heads)], axis=1
-        ).astype(BF16)
         trail = trail_col[:, i : i + 1] * inv_col[i]
         if i < half:
             beta_i = beta_row[i : i + 1, :]
             key_scale = -(decay_row[i : i + 1, :] * beta_i * inv_row[i])
-            basis = updates_basis(inverse[i], k_raw[i], v_raw, beta_i, key_scale)
+            basis = updates_basis(inverse[i], k_raw[i], v_raw[i], beta_i, key_scale)
             r_ref[i] = basis
             m_ref[i] = trailing_map(
                 basis, trail, k_raw[i], jnp.exp(last_row[i : i + 1, :]), eye_key, key_dim
@@ -262,7 +272,6 @@
         else:
             trail_ref[i - half] = jnp.broadcast_to(trail, (tok, key_dim))
             inverse_ref[i - half] = inverse[i]
-            v_own_ref[i - half] = v_raw
 
 
 def own_map_kernel(place, inverse_ref, kh_ref, v_ref, trail_ref, rows_ref, m_ref, r_ref):
@@ -495,15 +504,13 @@
     chips = seq // 2
     owners = min(chips, half)
     per = half // owners
-    place_seq, place_grp = lax.axis_index("seq"), lax.axis_index("grp")
-    place = jnp.stack([place_seq % 2, place_seq // 2, place_grp]).astype(jnp.int32)
     f32 = lambda *shape: jax.ShapeDtypeStruct(shape, F32)
     tall = lambda width: pltpu.VMEM((tok * heads, width), F32)
     unit = 2 * tok * key_dim * key_dim
     sibling = [(i, i ^ 1) for i in range(seq)]
 
     give_map, give_basis, k_heads, trail, rows, inverse, v_own = pl.pallas_call(
-        basis_kernel,
+        placed(basis_kernel),
         out_shape=(
             f32(half, key_dim, wide),
             f32(half, tok, wide),
@@ -513,7 +520,7 @@
             f32(half, tok, tok),
             jax.ShapeDtypeStruct((half, tok, value_dim), BF16),
         ),
-        in_specs=[SMEM_SPEC] + [pl.BlockSpec(memory_space=pltpu.HBM)] * 4,
+        in_specs=[pl.BlockSpec(memory_space=pltpu.HBM)] * 4,
         out_specs=tuple(vmem(7)),
         scratch_shapes=[
             pltpu.VMEM((tok, heads, key_dim), BF16),
@@ -529,16 +536,16 @@
         cost_estimate=pl.CostEstimate(
             flops=50 * heads * unit, bytes_accessed=0, transcendentals=0
         ),
-    )(place, *(pltpu.with_memory_space_constraint(a, pltpu.HBM) for a in (key_rows, value_rows, log_gate, beta_rate)))
+    )(*(pltpu.with_memory_space_constraint(a, pltpu.HBM) for a in (key_rows, value_rows, log_gate, beta_rate)))
     got_map = lax.ppermute(give_map, "seq", sibling)
     own_map, own_basis = call(
         own_map_kernel,
         (f32(half, key_dim, wide), f32(half, tok, wide)),
         flops=12 * half * unit,
-    )(place, inverse, k_heads, v_own, trail, rows)
+    )(inverse, k_heads, v_own, trail, rows)
     chip_maps = call(
         functools.partial(chip_kernel, key_dim, per), [f32(per, key_dim, wide)] * chips
-    )(place, own_map, got_map)
+    )(own_map, got_map)
 
     def across(parts, to_owner):
         moved = [parts[0]]
@@ -555,14 +562,14 @@
     got_own = lax.ppermute(own_map, "seq", sibling)
     folded = call(
         query_kernel, f32(heads, tok, wide), [tall(key_dim)], flops=20 * heads * unit
-    )(place, queries, k_heads, rows, give_basis, own_basis, got_map, got_own)
+    )(queries, k_heads, rows, give_basis, own_basis, got_map, got_own)
     owned, folded = lax.optimization_barrier((owned, folded))
     total = call(functools.partial(total_kernel, key_dim), f32(per, key_dim, wide))(
-        place, *owned
+        *owned
     )
     prefix = call(
         functools.partial(prefix_kernel, key_dim), f32(chips - 1, per, key_dim, wide)
-    )(place, *owned)
+    )(*owned)
     level = 0
     while 2 << level <= grp:
         swap = [(i, i ^ (1 << level)) for i in range(grp)]
@@ -573,17 +580,17 @@
             states = call(
                 functools.partial(enter_kernel, key_dim, level),
                 [f32(per, key_dim, value_dim)] * chips,
-            )(place, got_state, prefix)
+            )(got_state, prefix)
         else:
             got = lax.ppermute(total, "grp", swap)
             width = value_dim if 4 << level == grp else wide
             total = call(
                 functools.partial(group_total_kernel, key_dim, level), f32(per, key_dim, width)
-            )(place, total, got)
+            )(total, got)
             prefix = call(
                 functools.partial(before_kernel, key_dim, level),
                 f32(chips, per, key_dim, wide),
-            )(place, got, prefix)
+            )(got, prefix)
         level += 1
     arrived = across(states, False)
     others = [lax.ppermute(part, "seq", sibling) for part in arrived]
@@ -592,12 +599,12 @@
         functools.partial(early_kernel, per, owners, 0, chips),
         f32(first, 2, per, tok, value_dim),
         flops=6 * first * per * unit,
-    )(place, folded, *arrived[:first], *others[:first])
+    )(folded, *arrived[:first], *others[:first])
     return call(
         functools.partial(output_kernel, per, owners, first, chips),
         jax.ShapeDtypeStruct((tok, heads, value_dim), BF16),
         [tall(value_dim // 2), tall(value_dim // 2)],
-    )(place, folded, early, *arrived[first:], *others[first:])
+    )(folded, early, *arrived[first:], *others[first:])
 
 
 def solution(mesh):

time: 50.5 us -> 46.9 us (0.929)
  Pallas kernels: 17.3 us -> 11.1 us
  waiting for transfers between devices: 19.3 us -> 22 us
    pallas_call x11, Pallas kernels: 17.3 us -> 11.1 us  [the longest x10 6.37 us: run(): pl.pallas_call(placed(kernel), out_shape=out_shape, in_specs=vmem(len(arr...]
    ppermute x1, waiting for transfers between devices: 3.07 us -> 4.15 us  [body(): got_state = lax.ppermute(total, 'grp', swap)]
    ppermute x4, waiting for transfers between devices: 0.16 us -> 0.71 us  [body(): others = [lax.ppermute(part, 'seq', sibling) for part in arrived]]
    ppermute x1, waiting for transfers between devices: 0.24 us -> 0.78 us  [body(): got_map = lax.ppermute(give_map, 'seq', sibling)]
  transfers between devices with their start and end apart: 14 -> 14, of which waited for: 8 -> 9; matrix products, arithmetic and copies ran while one was open for 0% -> 0% of each run, Pallas kernels for 15% -> 9%
where the time goes in v4:
time: 46.9 us; the launch traced here: 46.7 us
  waiting for transfers between devices  22 us (47%)
  starting transfers between devices  13.5 us (29%)
  Pallas kernels  11.1 us (24%)
    ppermute x6, waiting for transfers between devices, across(): moved.append(lax.ppermute(parts[r], 'seq', pairs))  12 us
    ppermute x6, starting transfers between devices, across(): moved.append(lax.ppermute(parts[r], 'seq', pairs))  8.02 us
    pallas_call x10, Pallas kernels, run(): pl.pallas_call(placed(kernel), out_shape=out_shape, in_specs=vmem(len(arr...  6.37 us
    pallas_call x1, Pallas kernels, body(): pl.pallas_call(placed(basis_kernel), out_shape=(f32(half, key_dim, wide),...  4.77 us
    ppermute x1, waiting for transfers between devices, body(): got = lax.ppermute(total, 'grp', swap)  4.31 us
    ppermute x1, waiting for transfers between devices, body(): got_state = lax.ppermute(total, 'grp', swap)  4.15 us
    ppermute x1, starting transfers between devices, body(): got_state = lax.ppermute(total, 'grp', swap)  2.65 us
    ppermute x1, starting transfers between devices, body(): got = lax.ppermute(total, 'grp', swap)  1.64 us
  transfers between devices with their start and end apart: 14, of which 9 were waited for; matrix products, arithmetic and copies ran while one was open for 0% of the time, Pallas kernels for 9%

profile of v4, /device:TPU:0, one launch (start us, length us, event | category | flops | bytes accessed | tf_op | source)
XLA Modules:
  0.0 46.7 jit_solution(4700754597111384283)
XLA Ops:
  0.0 4.8 %shard_map.55 = (f32[4,128,384]{2,1,0:T(8,128)S(1)}, f32[4,128,384]{2,1,0:T(8,128)S(1)}, bf16[8,128,128]{2,1,0:T(8,128)(2,1)S(1)}, f32[4,128,128]{2,1,0:T(8,128)...) custom-call(bf16[128,8,128]{2,1,0:T(8,128)(2,1)} %refs_0_.2, ...), custom_call_target="tpu_custom_call" | custom-call | flops 1677721600 | tf_op jit(solution)/shard_map/pallas_call | solution.py:512
  4.8 0.0 copy-start
  4.8 0.5 %collective-permute-start = (f32[4,128,384]{2,1,0:T(8,128)S(1)}, f32[4,128,384]{2,1,0:T(8,128)S(1)}, u32[]{:S(2)}, u32[]{:S(2)}) collective-permute-start(f32[4,128,384]{2,1,0:T(8,128)S(1)} %get-tuple-element.33), channel_id=1, source_target_pairs={{0,4},{4,0},{8,12},{12,8},{16,20},{20,16},{24,28},{28,24},{1,5},{5... | collective-permute-start | bytes 2359304 | tf_op jit(solution)/shard_map/ppermute | solution.py:540
  5.3 1.0 %shard_map.56 = (f32[4,128,384]{2,1,0:T(8,128)S(1)}, f32[4,128,384]{2,1,0:T(8,128)S(1)}) custom-call(f32[4,128,128]{2,1,0:T(8,128)S(1)} %get-tuple-element.27.refs_0_, bf16[8,128,128]{2,1,0:T(8,128)(2,1)S(1)} %get-tuple-element.28.refs_1_, bf16[4,128,256]{2,1,0:T(8,128)(2,1)S(1)} %get-tuple-element.29.refs_2_, f32[4,128,128]{2,1,0:T(8,128)S(1)} %get-tuple-element.30.refs_3_, ...), custom_call_target="tpu_custom_call" | custom-call | flops 201326592 | tf_op jit(solution)/shard_map/pallas_call | solution.py:65
  6.3 0.1 collective-permute-start.4
  6.4 0.8 %collective-permute-done.refs_1_.refs_5_ = f32[4,128,384]{2,1,0:T(8,128)S(1)} collective-permute-done((f32[4,128,384]{2,1,0:T(8,128)S(1)}, f32[4,128,384]{2,1,0:T(8,128)S(1)}, u32[]{:S(2)}, u32[]{:S(2)}) %collective-permute-start) | collective-permute-done | bytes 786464 | tf_op jit(solution)/shard_map/ppermute | solution.py:540
  7.2 0.4 shard_map.57
  7.6 2.9 %collective-permute-start.1 = (f32[1,128,384]{2,1,0:T(8,128)S(1)}, f32[1,128,384]{2,1,0:T(8,128)S(1)}, u32[]{:S(2)}, u32[]{:S(2)}) collective-permute-start(f32[1,128,384]{2,1,0:T(8,128)S(1)} %get-tuple-element.35), channel_id=1, source_target_pairs={{0,8},{4,12},{8,0},{12,4},{16,24},{20,28},{24,16},{28,20},{1,9},{5... | collective-permute-start | bytes 589832 | tf_op jit(solution)/shard_map/ppermute | solution.py:558
  10.6 1.5 %collective-permute-start.2 = (f32[1,128,384]{2,1,0:T(8,128)S(1)}, f32[1,128,384]{2,1,0:T(8,128)S(1)}, u32[]{:S(2)}, u32[]{:S(2)}) collective-permute-start(f32[1,128,384]{2,1,0:T(8,128)S(1)} %get-tuple-element.36), channel_id=1, source_target_pairs={{0,16},{4,20},{8,24},{12,28},{16,0},{20,4},{24,8},{28,12},{1,17},{... | collective-permute-start | bytes 589832 | tf_op jit(solution)/shard_map/ppermute | solution.py:558
  12.1 0.0 collective-permute-start.3
  12.1 0.0 collective-permute-done.4.refs_6_
  12.1 0.0 copy-done
  12.1 1.8 %shard_map.58.refs_0_ = f32[8,128,384]{2,1,0:T(8,128)S(1)} custom-call(bf16[128,8,128]{2,1,0:T(8,128)(2,1)S(1)} %copy-done, bf16[8,128,128]{2,1,0:T(8,128)(2,1)S(1)} %get-tuple-element.28.refs_1_, f32[4,8,128]{2,1,0:T(8,128)S(1)} %get-tuple-element.31.refs_4_.refs_2_, f32[4,128,384]{2,1,0:T(8,128)S(1)} %get-tuple-element.38.refs_3_, ...), custom_call_target="tpu_custom_call" | custom-call | flops 671088640 | tf_op jit(solution)/shard_map/pallas_call | solution.py:65
  14.0 2.3 %collective-permute-done.1.refs_1_ = f32[1,128,384]{2,1,0:T(8,128)S(1)} collective-permute-done((f32[1,128,384]{2,1,0:T(8,128)S(1)}, f32[1,128,384]{2,1,0:T(8,128)S(1)}, u32[]{:S(2)}, u32[]{:S(2)}) %collective-permute-start.1) | collective-permute-done | bytes 196640 | tf_op jit(solution)/shard_map/ppermute | solution.py:558
  16.3 5.2 %collective-permute-done.2.refs_2_ = f32[1,128,384]{2,1,0:T(8,128)S(1)} collective-permute-done((f32[1,128,384]{2,1,0:T(8,128)S(1)}, f32[1,128,384]{2,1,0:T(8,128)S(1)}, u32[]{:S(2)}, u32[]{:S(2)}) %collective-permute-start.2) | collective-permute-done | bytes 196640 | tf_op jit(solution)/shard_map/ppermute | solution.py:558
  21.4 0.0 collective-permute-done.3.refs_3_
  21.4 0.5 %shard_map.59.refs_0_ = f32[1,128,384]{2,1,0:T(8,128)S(1)} custom-call(f32[1,128,384]{2,1,0:T(8,128)S(1)} %get-tuple-element.41.refs_0_, f32[1,128,384]{2,1,0:T(8,128)S(1)} %collective-permute-done.1.refs_1_, f32[1,128,384]{2,1,0:T(8,128)S(1)} %collective-permute-done.2.refs_2_, f32[1,128,384]{2,1,0:T(8,128)S(1)} %collective-permute-done.3.refs_3_), custom_call_target="tpu_custom_call" | custom-call | tf_op jit(solution)/shard_map/pallas_call | solution.py:65
  22.0 1.6 %collective-permute-start.5 = (f32[1,128,384]{2,1,0:T(8,128)S(1)}, f32[1,128,384]{2,1,0:T(8,128)S(1)}, u32[]{:S(2)}, u32[]{:S(2)}) collective-permute-start(f32[1,128,384]{2,1,0:T(8,128)S(1)} %shard_map.59.refs_0_), channel_id=1, source_target_pairs={{0,1},{1,0},{2,3},{3,2},{4,5},{5,4},{6,7},{7,6},{8,9},{9,8},{10,11... | collective-permute-start | bytes 589832 | tf_op jit(solution)/shard_map/ppermute | solution.py:585
  23.6 4.3 %collective-permute-done.5.refs_1_.refs_0_ = f32[1,128,384]{2,1,0:T(8,128)S(1)} collective-permute-done((f32[1,128,384]{2,1,0:T(8,128)S(1)}, f32[1,128,384]{2,1,0:T(8,128)S(1)}, u32[]{:S(2)}, u32[]{:S(2)}) %collective-permute-start.5) | collective-permute-done | bytes 196640 | tf_op jit(solution)/shard_map/ppermute | solution.py:585
  27.9 0.2 shard_map.60
  28.1 2.6 %collective-permute-start.6 = (f32[1,128,256]{2,1,0:T(8,128)S(1)}, f32[1,128,256]{2,1,0:T(8,128)S(1)}, u32[]{:S(2)}, u32[]{:S(2)}) collective-permute-start(f32[1,128,256]{2,1,0:T(8,128)S(1)} %shard_map.60), channel_id=1, source_target_pairs={{0,2},{1,3},{2,0},{3,1},{4,6},{5,7},{6,4},{7,5},{8,10},{9,11},{10,... | collective-permute-start | bytes 393224 | tf_op jit(solution)/shard_map/ppermute | solution.py:579
  30.8 0.5 shard_map.61.refs_1_
  31.2 0.1 shard_map.62.refs_1_
  31.3 4.2 %collective-permute-done.6.refs_0_ = f32[1,128,256]{2,1,0:T(8,128)S(1)} collective-permute-done((f32[1,128,256]{2,1,0:T(8,128)S(1)}, f32[1,128,256]{2,1,0:T(8,128)S(1)}, u32[]{:S(2)}, u32[]{:S(2)}) %collective-permute-start.6) | collective-permute-done | bytes 131104 | tf_op jit(solution)/shard_map/ppermute | solution.py:579
  35.4 0.3 shard_map.63
  35.7 1.7 %collective-permute-start.7 = (f32[1,128,256]{2,1,0:T(8,128)S(1)}, f32[1,128,256]{2,1,0:T(8,128)S(1)}, u32[]{:S(2)}, u32[]{:S(2)}) collective-permute-start(f32[1,128,256]{2,1,0:T(8,128)S(1)} %get-tuple-element.46), channel_id=1, source_target_pairs={{0,8},{4,12},{8,0},{12,4},{16,24},{20,28},{24,16},{28,20},{1,9},{5... | collective-permute-start | bytes 393224 | tf_op jit(solution)/shard_map/ppermute | solution.py:558
  37.5 0.3 collective-permute-start.10
  37.8 1.5 %collective-permute-start.11 = (f32[1,128,256]{2,1,0:T(8,128)S(1)}, f32[1,128,256]{2,1,0:T(8,128)S(1)}, u32[]{:S(2)}, u32[]{:S(2)}) collective-permute-start(f32[1,128,256]{2,1,0:T(8,128)S(1)} %get-tuple-element.48), channel_id=1, source_target_pairs={{0,24},{4,28},{8,16},{12,20},{16,8},{20,12},{24,0},{28,4},{1,25},{... | collective-permute-start | bytes 393224 | tf_op jit(solution)/shard_map/ppermute | solution.py:558
  39.3 0.0 collective-permute-start.8
  39.3 1.9 %collective-permute-done.7.refs_2_ = f32[1,128,256]{2,1,0:T(8,128)S(1)} collective-permute-done((f32[1,128,256]{2,1,0:T(8,128)S(1)}, f32[1,128,256]{2,1,0:T(8,128)S(1)}, u32[]{:S(2)}, u32[]{:S(2)}) %collective-permute-start.7) | collective-permute-done | bytes 131104 | tf_op jit(solution)/shard_map/ppermute | solution.py:558
  41.2 0.0 collective-permute-start.9
  41.2 2.6 %collective-permute-done.10.refs_2_ = f32[1,128,256]{2,1,0:T(8,128)S(1)} collective-permute-done((f32[1,128,256]{2,1,0:T(8,128)S(1)}, f32[1,128,256]{2,1,0:T(8,128)S(1)}, u32[]{:S(2)}, u32[]{:S(2)}) %collective-permute-start.10) | collective-permute-done | bytes 131104 | tf_op jit(solution)/shard_map/ppermute | solution.py:558
  43.8 0.0 collective-permute-start.12
  43.8 0.0 collective-permute-done.11.refs_3_
  43.8 0.5 %collective-permute-start.13 = (f32[1,128,256]{2,1,0:T(8,128)S(1)}, f32[1,128,256]{2,1,0:T(8,128)S(1)}, u32[]{:S(2)}, u32[]{:S(2)}) collective-permute-start(f32[1,128,256]{2,1,0:T(8,128)S(1)} %collective-permute-done.11.refs_3_), channel_id=1, source_target_pairs={{0,4},{4,0},{8,12},{12,8},{16,20},{20,16},{24,28},{28,24},{1,5},{5... | collective-permute-start | bytes 393224 | tf_op jit(solution)/shard_map/ppermute | solution.py:596
  44.4 0.0 collective-permute-done.8.refs_3_
  44.4 0.0 collective-permute-done.9.refs_4_
  44.4 0.3 shard_map.64.refs_1_
  44.7 0.5 %collective-permute-done.12.refs_4_ = f32[1,128,256]{2,1,0:T(8,128)S(1)} collective-permute-done((f32[1,128,256]{2,1,0:T(8,128)S(1)}, f32[1,128,256]{2,1,0:T(8,128)S(1)}, u32[]{:S(2)}, u32[]{:S(2)}) %collective-permute-start.12) | collective-permute-done | bytes 131104 | tf_op jit(solution)/shard_map/ppermute | solution.py:596
  45.2 0.2 collective-permute-done.13.refs_5_
  45.4 1.3 %shard_map.65 = bf16[128,8,256]{2,1,0:T(8,128)(2,1)} custom-call(f32[8,128,384]{2,1,0:T(8,128)S(1)} %shard_map.58.refs_0_, f32[2,2,1,128,256]{4,3,2,1,0:T(8,128)S(1)} %shard_map.64.refs_1_, f32[1,128,256]{2,1,0:T(8,128)S(1)} %collective-permute-done.10.refs_2_, f32[1,128,256]{2,1,0:T(8,128)S(1)} %collective-permute-done.11.refs_3_, ...), custom_call_target="tpu_custom_call" | custom-call | tf_op jit(solution)/shard_map/pallas_call | solution.py:65
Async XLA Ops:
  4.8 7.3 %copy-start = (bf16[128,8,128]{2,1,0:T(8,128)(2,1)S(1)}, bf16[128,8,128]{2,1,0:T(8,128)(2,1)}, u32[]{:S(2)}) copy-start(bf16[128,8,128]{2,1,0:T(8,128)(2,1)} %refs_0_.3) | copy-start | bytes 786436
  4.8 2.4 %collective-permute-start = (f32[4,128,384]{2,1,0:T(8,128)S(1)}, f32[4,128,384]{2,1,0:T(8,128)S(1)}, u32[]{:S(2)}, u32[]{:S(2)}) collective-permute-start(f32[4,128,384]{2,1,0:T(8,128)S(1)} %get-tuple-element.33), channel_id=1, source_target_pairs={{0,4},{4,0},{8,12},{12,8},{16,20},{20,16},{24,28},{28,24},{1,5},{5... | collective-permute-start | bytes 2359304 | tf_op jit(solution)/shard_map/ppermute | solution.py:540
  6.3 5.8 %collective-permute-start.4 = (f32[4,128,384]{2,1,0:T(8,128)S(1)}, f32[4,128,384]{2,1,0:T(8,128)S(1)}, u32[]{:S(2)}, u32[]{:S(2)}) collective-permute-start(f32[4,128,384]{2,1,0:T(8,128)S(1)} %get-tuple-element.32.refs_0_), channel_id=1, source_target_pairs={{0,4},{4,0},{8,12},{12,8},{16,20},{20,16},{24,28},{28,24},{1,5},{5... | collective-permute-start | bytes 2359304 | tf_op jit(solution)/shard_map/ppermute | solution.py:562
  7.6 8.6 %collective-permute-start.1 = (f32[1,128,384]{2,1,0:T(8,128)S(1)}, f32[1,128,384]{2,1,0:T(8,128)S(1)}, u32[]{:S(2)}, u32[]{:S(2)}) collective-permute-start(f32[1,128,384]{2,1,0:T(8,128)S(1)} %get-tuple-element.35), channel_id=1, source_target_pairs={{0,8},{4,12},{8,0},{12,4},{16,24},{20,28},{24,16},{28,20},{1,9},{5... | collective-permute-start | bytes 589832 | tf_op jit(solution)/shard_map/ppermute | solution.py:558
  10.6 10.9 %collective-permute-start.2 = (f32[1,128,384]{2,1,0:T(8,128)S(1)}, f32[1,128,384]{2,1,0:T(8,128)S(1)}, u32[]{:S(2)}, u32[]{:S(2)}) collective-permute-start(f32[1,128,384]{2,1,0:T(8,128)S(1)} %get-tuple-element.36), channel_id=1, source_target_pairs={{0,16},{4,20},{8,24},{12,28},{16,0},{20,4},{24,8},{28,12},{1,17},{... | collective-permute-start | bytes 589832 | tf_op jit(solution)/shard_map/ppermute | solution.py:558
  12.1 9.4 %collective-permute-start.3 = (f32[1,128,384]{2,1,0:T(8,128)S(1)}, f32[1,128,384]{2,1,0:T(8,128)S(1)}, u32[]{:S(2)}, u32[]{:S(2)}) collective-permute-start(f32[1,128,384]{2,1,0:T(8,128)S(1)} %get-tuple-element.37), channel_id=1, source_target_pairs={{0,24},{4,28},{8,16},{12,20},{16,8},{20,12},{24,0},{28,4},{1,25},{... | collective-permute-start | bytes 589832 | tf_op jit(solution)/shard_map/ppermute | solution.py:558
  22.0 6.0 %collective-permute-start.5 = (f32[1,128,384]{2,1,0:T(8,128)S(1)}, f32[1,128,384]{2,1,0:T(8,128)S(1)}, u32[]{:S(2)}, u32[]{:S(2)}) collective-permute-start(f32[1,128,384]{2,1,0:T(8,128)S(1)} %shard_map.59.refs_0_), channel_id=1, source_target_pairs={{0,1},{1,0},{2,3},{3,2},{4,5},{5,4},{6,7},{7,6},{8,9},{9,8},{10,11... | collective-permute-start | bytes 589832 | tf_op jit(solution)/shard_map/ppermute | solution.py:585
  28.1 7.3 %collective-permute-start.6 = (f32[1,128,256]{2,1,0:T(8,128)S(1)}, f32[1,128,256]{2,1,0:T(8,128)S(1)}, u32[]{:S(2)}, u32[]{:S(2)}) collective-permute-start(f32[1,128,256]{2,1,0:T(8,128)S(1)} %shard_map.60), channel_id=1, source_target_pairs={{0,2},{1,3},{2,0},{3,1},{4,6},{5,7},{6,4},{7,5},{8,10},{9,11},{10,... | collective-permute-start | bytes 393224 | tf_op jit(solution)/shard_map/ppermute | solution.py:579
  35.7 5.5 %collective-permute-start.7 = (f32[1,128,256]{2,1,0:T(8,128)S(1)}, f32[1,128,256]{2,1,0:T(8,128)S(1)}, u32[]{:S(2)}, u32[]{:S(2)}) collective-permute-start(f32[1,128,256]{2,1,0:T(8,128)S(1)} %get-tuple-element.46), channel_id=1, source_target_pairs={{0,8},{4,12},{8,0},{12,4},{16,24},{20,28},{24,16},{28,20},{1,9},{5... | collective-permute-start | bytes 393224 | tf_op jit(solution)/shard_map/ppermute | solution.py:558
  37.5 6.4 %collective-permute-start.10 = (f32[1,128,256]{2,1,0:T(8,128)S(1)}, f32[1,128,256]{2,1,0:T(8,128)S(1)}, u32[]{:S(2)}, u32[]{:S(2)}) collective-permute-start(f32[1,128,256]{2,1,0:T(8,128)S(1)} %get-tuple-element.47), channel_id=1, source_target_pairs={{0,16},{4,20},{8,24},{12,28},{16,0},{20,4},{24,8},{28,12},{1,17},{... | collective-permute-start | bytes 393224 | tf_op jit(solution)/shard_map/ppermute | solution.py:558
  37.8 6.0 %collective-permute-start.11 = (f32[1,128,256]{2,1,0:T(8,128)S(1)}, f32[1,128,256]{2,1,0:T(8,128)S(1)}, u32[]{:S(2)}, u32[]{:S(2)}) collective-permute-start(f32[1,128,256]{2,1,0:T(8,128)S(1)} %get-tuple-element.48), channel_id=1, source_target_pairs={{0,24},{4,28},{8,16},{12,20},{16,8},{20,12},{24,0},{28,4},{1,25},{... | collective-permute-start | bytes 393224 | tf_op jit(solution)/shard_map/ppermute | solution.py:558
  39.3 5.1 %collective-permute-start.8 = (f32[1,128,256]{2,1,0:T(8,128)S(1)}, f32[1,128,256]{2,1,0:T(8,128)S(1)}, u32[]{:S(2)}, u32[]{:S(2)}) collective-permute-start(f32[1,128,256]{2,1,0:T(8,128)S(1)} %get-tuple-element.45.refs_1_), channel_id=1, source_target_pairs={{0,4},{4,0},{8,12},{12,8},{16,20},{20,16},{24,28},{28,24},{1,5},{5... | collective-permute-start | bytes 393224 | tf_op jit(solution)/shard_map/ppermute | solution.py:596
  41.2 3.1 %collective-permute-start.9 = (f32[1,128,256]{2,1,0:T(8,128)S(1)}, f32[1,128,256]{2,1,0:T(8,128)S(1)}, u32[]{:S(2)}, u32[]{:S(2)}) collective-permute-start(f32[1,128,256]{2,1,0:T(8,128)S(1)} %collective-permute-done.7.refs_2_), channel_id=1, source_target_pairs={{0,4},{4,0},{8,12},{12,8},{16,20},{20,16},{24,28},{28,24},{1,5},{5... | collective-permute-start | bytes 393224 | tf_op jit(solution)/shard_map/ppermute | solution.py:596
  43.8 1.3 %collective-permute-start.12 = (f32[1,128,256]{2,1,0:T(8,128)S(1)}, f32[1,128,256]{2,1,0:T(8,128)S(1)}, u32[]{:S(2)}, u32[]{:S(2)}) collective-permute-start(f32[1,128,256]{2,1,0:T(8,128)S(1)} %collective-permute-done.10.refs_2_), channel_id=1, source_target_pairs={{0,4},{4,0},{8,12},{12,8},{16,20},{20,16},{24,28},{28,24},{1,5},{5... | collective-permute-start | bytes 393224 | tf_op jit(solution)/shard_map/ppermute | solution.py:596
  43.8 1.5 %collective-permute-start.13 = (f32[1,128,256]{2,1,0:T(8,128)S(1)}, f32[1,128,256]{2,1,0:T(8,128)S(1)}, u32[]{:S(2)}, u32[]{:S(2)}) collective-permute-start(f32[1,128,256]{2,1,0:T(8,128)S(1)} %collective-permute-done.11.refs_3_), channel_id=1, source_target_pairs={{0,4},{4,0},{8,12},{12,8},{16,20},{20,16},{24,28},{28,24},{1,5},{5... | collective-permute-start | bytes 393224 | tf_op jit(solution)/shard_map/ppermute | solution.py:596

commit v5 on v4

--- a/solution.py
+++ b/solution.py
@@ -46,6 +46,46 @@
     return jnp.concatenate(
         [moved[:, :key_dim], moved[:, key_dim:] + later[:, key_dim:]], axis=1
     )
+
+
+def turned(distance, chips):
+    bits = chips.bit_length() - 1
+    low = bits // 2
+    return (distance >> low) | ((distance & ((1 << low) - 1)) << (bits - low))
+
+
+def slot_list(chips):
+    plain = [chips - 1] + list(range(1, chips - 1)) + [0] if chips > 1 else [0]
+    return plain, plain
+
+
+def owner_of(slot, core, chip, chips):
+    plain, other = slot_list(chips)
+    if plain[slot] == other[slot]:
+        return jnp.bitwise_xor(chip, plain[slot])
+    return jnp.bitwise_xor(chip, jnp.where(core == 0, plain[slot], other[slot]))
+
+
+def by_distance(core, maps):
+    plain, other = slot_list(len(maps))
+    ordered = []
+    for d in range(len(maps)):
+        a, b = maps[plain.index(d)], maps[other.index(d)]
+        ordered.append(a if plain.index(d) == other.index(d) else jnp.where(core == 0, a, b))
+    return ordered
+
+
+def local_heads(core, chip, chips, half):
+    if half % chips:
+        return list(range(half))
+    per = half // chips
+    return [owner_of(n // per, core, chip, chips) * per + n % per for n in range(half)]
+
+
+def positions(heads, per):
+    half = heads // 2
+    first = [*range(per), *range(half, half + per)]
+    return first, [n for n in range(heads) if n not in first]
 
 
 def vmem(count):
@@ -93,11 +133,6 @@
 def stage_rows(ref, scratch):
     wide = ref[...].astype(F32)
     scratch[...] = wide.reshape(scratch.shape)
-
-
-def rolled(a, flip):
-    half = a.shape[0] // 2
-    return jnp.where(flip, jnp.concatenate([a[half:], a[:half]], axis=0), a)
 
 
 def mm3_packed(lhs, rhs):
@@ -192,13 +227,14 @@
 
 
 def basis_kernel(
-    place, k_hbm, v_hbm, g_hbm, b_hbm, m_ref, r_ref, kh_ref, trail_ref, rows_ref, inverse_ref, v_own_ref,
+    chips, per, place, k_hbm, v_hbm, g_hbm, b_hbm,
+    give_ref, own_ref, r_ref, kh_ref, trail_ref, rows_ref, inverse_ref, v_rest_ref,
     k_ref, v_ref, g_ref, b_ref, ks, vs0, vs1, sems,
 ):
     copies = [
         pltpu.make_async_copy(src, dst, sems.at[n])
         for n, (src, dst) in enumerate(
-            ((g_hbm, g_ref), (b_hbm, b_ref), (k_hbm, k_ref), (v_hbm, v_ref))
+            ((k_hbm, k_ref), (g_hbm, g_ref), (b_hbm, b_ref), (v_hbm, v_ref))
         )
     ]
     for copy in copies:
@@ -206,14 +242,17 @@
     tok, heads, key_dim = k_ref.shape
     value_dim = v_ref.shape[2]
     half = heads // 2
-    first_side = 1 - place[0]
-    flip = first_side == 1
-    order = [first_side * half + i for i in range(half)]
-    order += [(1 - first_side) * half + i for i in range(half)]
-    copies[0].wait()
+    core, chip = place[0], place[1]
+    order = [(1 - core) * half + h for h in local_heads(1 - core, chip, chips, half)]
+    order += [core * half + h for h in local_heads(core, chip, chips, half)]
     copies[1].wait()
-    cum_row = lane_cumsum(rolled(g_ref[...], flip))
-    beta_row = rolled(b_ref[...], flip)
+    copies[2].wait()
+
+    def picked(ref):
+        return jnp.concatenate([ref[pl.ds(h, 1), :] for h in order], axis=0)
+
+    cum_row = lane_cumsum(picked(g_ref))
+    beta_row = picked(b_ref)
     last_row = cum_row[:, tok - 1 :]
     decay_row = jnp.exp(cum_row)
     cum_col = cum_row.T
@@ -225,7 +264,7 @@
     eye = rows == cols
     eye_key = eye_mask(key_dim)
     every = range(heads)
-    copies[2].wait()
+    copies[0].wait()
     stage_rows(k_ref, ks)
     k_wide = [head_rows(ks, h, heads) for h in order]
     k_raw = [a.astype(BF16) for a in k_wide]
@@ -252,47 +291,59 @@
         ).astype(BF16)
         for h in order
     ]
-    for i in range(half):
-        v_own_ref[i] = v_raw[half + i]
+    first, rest = positions(heads, per)
+    for n, i in enumerate(rest):
+        v_rest_ref[n] = v_raw[i]
     inverse = block_inverse(strict)
     rows_ref[0] = jnp.concatenate(inv_row, axis=0)
     rows_ref[1] = cum_row
     rows_ref[2] = beta_row
     rows_ref[3] = -(decay_row * beta_row * jnp.concatenate(inv_row, axis=0))
-    for i in every:
+    for n, i in enumerate(first):
         trail = trail_col[:, i : i + 1] * inv_col[i]
-        if i < half:
-            beta_i = beta_row[i : i + 1, :]
-            key_scale = -(decay_row[i : i + 1, :] * beta_i * inv_row[i])
-            basis = updates_basis(inverse[i], k_raw[i], v_raw[i], beta_i, key_scale)
-            r_ref[i] = basis
-            m_ref[i] = trailing_map(
-                basis, trail, k_raw[i], jnp.exp(last_row[i : i + 1, :]), eye_key, key_dim
-            )
+        beta_i = beta_row[i : i + 1, :]
+        key_scale = -(decay_row[i : i + 1, :] * beta_i * inv_row[i])
+        basis = updates_basis(inverse[i], k_raw[i], v_raw[i], beta_i, key_scale)
+        r_ref[n] = basis
+        made = trailing_map(
+            basis, trail, k_raw[i], jnp.exp(last_row[i : i + 1, :]), eye_key, key_dim
+        )
+        if n < per:
+            give_ref[n] = made
         else:
-            trail_ref[i - half] = jnp.broadcast_to(trail, (tok, key_dim))
-            inverse_ref[i - half] = inverse[i]
-
-
-def own_map_kernel(place, inverse_ref, kh_ref, v_ref, trail_ref, rows_ref, m_ref, r_ref):
-    half, key_dim, wide = m_ref.shape
-    tok = r_ref.shape[1]
+            own_ref[n - per] = made
+    for n, i in enumerate(rest):
+        trail_ref[n] = jnp.broadcast_to(trail_col[:, i : i + 1] * inv_col[i], (tok, key_dim))
+        inverse_ref[n] = inverse[i]
+
+
+def rest_kernel(place, inverse_ref, kh_ref, v_ref, trail_ref, rows_ref, give_ref, own_ref, r_ref):
+    rest, tok, wide = r_ref.shape
+    key_dim = wide - v_ref.shape[2]
+    heads = kh_ref.shape[0]
     eye_key = eye_mask(key_dim)
-    for i in range(half):
-        at = slice(half + i, half + i + 1)
-        k_raw = kh_ref[half + i]
+    for n, i in enumerate(positions(heads, (heads - rest) // 2)[1]):
+        at = slice(i, i + 1)
+        k_raw = kh_ref[i]
         basis = updates_basis(
-            inverse_ref[i], k_raw, v_ref[i], rows_ref[2, at, :], rows_ref[3, at, :]
+            inverse_ref[n], k_raw, v_ref[n], rows_ref[2, at, :], rows_ref[3, at, :]
         )
-        r_ref[i] = basis
+        r_ref[n] = basis
         last = jnp.exp(rows_ref[1, at, tok - 1 :])
-        m_ref[i] = trailing_map(basis, trail_ref[i][:, :1], k_raw, last, eye_key, key_dim)
-
-
-def query_kernel(place, q_ref, kh_ref, rows_ref, r_give, r_own, got_ref, got_own_ref, f_ref, qs):
+        made = trailing_map(basis, trail_ref[n][:, :1], k_raw, last, eye_key, key_dim)
+        if n < rest // 2:
+            give_ref[n] = made
+        else:
+            own_ref[n - rest // 2] = made
+
+
+def query_rows(chips, place, q_ref, kh_ref, rows_ref, r_first, r_rest, f_ref, qs):
     heads, tok, key_dim = kh_ref.shape
     half = heads // 2
-    core = place[0]
+    first, rest = positions(heads, r_first.shape[0] // 2)
+    core, chip = place[0], place[1]
+    order = [(1 - core) * half + h for h in local_heads(1 - core, chip, chips, half)]
+    order += [core * half + h for h in local_heads(core, chip, chips, half)]
     stage_rows(q_ref, qs)
     cum_row = rows_ref[1]
     cum_col = cum_row.T
@@ -300,36 +351,87 @@
     cols = lax.broadcasted_iota(jnp.int32, (tok, tok), 1)
     lower = rows >= cols
     for i in range(heads):
-        head = ((1 - core) * half + i) if i < half else (core * half + i - half)
-        q_wide = head_rows(qs, head, heads)
+        q_wide = head_rows(qs, order[i], heads)
         q_inv = lax.rsqrt(jnp.sum(q_wide * q_wide, axis=1, keepdims=True) + 1e-6)
         dots = mm_nt(q_wide.astype(BF16), kh_ref[i])
         gap = cum_col[:, i : i + 1] - cum_row[i : i + 1, :]
         decay = jnp.exp(jnp.where(lower, gap, 0.0))
         scores = jnp.where(lower, dots * decay * q_inv * rows_ref[0, i : i + 1, :], 0.0)
-        folded = mm3(scores, r_give[i] if i < half else r_own[i - half])
+        folded = mm3(scores, r_first[first.index(i)] if i in first else r_rest[rest.index(i)])
         gated = q_wide * (q_inv * jnp.exp(cum_col[:, i : i + 1]))
         f_ref[i] = jnp.concatenate(
             [folded[:, :key_dim] + gated, folded[:, key_dim:]], axis=1
         )
 
-    @pl.when(core == 1)
+
+def query_kernel(chips, place, *refs):
+    @pl.when(place[0] == 0)
     def _():
-        for i in range(heads):
-            earlier = got_own_ref[i] if i < half else got_ref[i - half]
-            f_ref[i] = compose(f_ref[i], earlier, key_dim)
-
-
-def chip_kernel(key_dim, outs_per, place, own_ref, got_ref, *out_refs):
+        query_rows(chips, place, *refs)
+
+
+def query_late_kernel(chips, place, done_ref, *refs):
+    f_ref = refs[-2]
+
+    @pl.when(place[0] == 0)
+    def _():
+        f_ref[...] = done_ref[...]
+
+    @pl.when(place[0] != 0)
+    def _():
+        query_rows(chips, place, *refs)
+
+
+def read_out(folded, state):
+    key_dim = state.shape[0]
+    return mm3(folded[:, :key_dim], state) + folded[:, key_dim:]
+
+
+def pair_kernel(chips, slot, place, *refs):
+    map_refs, (state_ref, keep_ref, give_ref) = refs[:-3], refs[-3:]
     core, chip = place[0], place[1]
-    half = own_ref.shape[0]
-    owners = half // outs_per
-    for r, out in enumerate(out_refs):
-        owner = jnp.bitwise_xor(chip, r)
-        owner = jnp.where(owner < owners, owner, 0)
-        for j in range(outs_per):
-            head = owner * outs_per + j
-            own, got = own_ref[head], got_ref[head]
+    per = state_ref.shape[0]
+    for j in range(per):
+        own, got = picked_maps(map_refs, slot, j, per, chips, core, chip)
+        state = state_ref[j]
+        second = read_out(jnp.where(core == 0, own, got), state)
+        keep_ref[j] = jnp.where(core == 0, state, second)
+        give_ref[j] = jnp.where(core == 0, second, state)
+
+
+def picked_maps(refs, slot, j, per, chips, core, chip):
+    own_first, own_rest, got_first, got_rest = refs
+    half = per + own_rest.shape[0]
+    if half % chips:
+        at = owner_of(slot, core, chip, chips) * per + j
+        at_tail = jnp.clip(at - per, 0, half - per - 1)
+        return tuple(
+            jnp.where(at < per, first[0], rest[at_tail])
+            for first, rest in ((own_first, own_rest), (got_first, got_rest))
+        )
+    at = slot * per + j
+    if at < per:
+        return own_first[at], got_first[at]
+    return own_rest[at - per], got_rest[at - per]
+
+
+def chip_kernel(key_dim, chips, slots, place, *refs):
+    in_refs, out_refs = refs[: -len(slots)], refs[-len(slots) :]
+    core, chip = place[0], place[1]
+    per = out_refs[0].shape[0]
+    for slot, out in zip(slots, out_refs):
+        for j in range(per):
+            if len(in_refs) == 4:
+                at = owner_of(slot, core, chip, chips) * per + j
+                tail = in_refs[1].shape[0]
+                at_tail = jnp.clip(at - per, 0, tail - 1)
+                own, got = (
+                    jnp.where(at < per, head[0], rest[at_tail])
+                    for head, rest in (in_refs[:2], in_refs[2:])
+                )
+            else:
+                at = (slot - slots[0]) * per + j
+                own, got = in_refs[0][at], in_refs[1][at]
             earlier = jnp.where(core == 0, own, got)
             later = jnp.where(core == 0, got, own)
             out[j] = compose(later, earlier, key_dim)
@@ -349,7 +451,7 @@
     maps, total = refs[:-1], refs[-1]
     chip = place[1]
     for j in range(total.shape[0]):
-        level = [ref[j] for ref in maps]
+        level = by_distance(place[0], [ref[j] for ref in maps])
         bit = 1
         while len(level) > 1:
             swapped = jnp.bitwise_and(chip, bit) != 0
@@ -366,7 +468,7 @@
 def prefix_kernel(key_dim, place, *refs):
     maps, prefix = refs[:-1], refs[-1]
     for j in range(prefix.shape[1]):
-        ordered = in_order(place[1], [ref[j] for ref in maps])
+        ordered = in_order(place[1], by_distance(place[0], [ref[j] for ref in maps]))
         running = ordered[0]
         prefix[0, j] = running
         for index in range(1, len(ordered) - 1):
@@ -423,74 +525,65 @@
 
 
 def enter_kernel(key_dim, level, place, got_ref, prefix_ref, *out_refs):
-    chip = place[1]
+    core, chip, chips = place[0], place[1], len(out_refs)
     upper = is_upper(place, level)
     for j in range(got_ref.shape[0]):
         eh, el = split2(jnp.where(upper, got_ref[j], 0.0))
         twice = jnp.concatenate([eh, eh], axis=0)
-        for r, out in enumerate(out_refs):
-            one = prefix_ref[jnp.bitwise_xor(chip, r), j]
+        for slot, out in enumerate(out_refs):
+            one = prefix_ref[owner_of(slot, core, chip, chips), j]
             th, tl = split2(one[:, :key_dim])
             moved = mm(jnp.concatenate([th, tl], axis=1), twice) + mm(th, el)
             out[j] = moved + one[:, key_dim:]
 
 
-def read_out(folded, state):
-    key_dim = state.shape[0]
-    return mm3(folded[:, :key_dim], state) + folded[:, key_dim:]
-
-
-def early_kernel(per, owners, first, chips, place, f_ref, *refs):
+def each_slot(place, slots, chips, half, per, use):
+    core, chip = place[0], place[1]
+    for n, slot in enumerate(slots):
+        for own in (True, False):
+            side = core if own else 1 - core
+            owner = owner_of(slot, side, chip, chips)
+
+            def run(n=n, slot=slot, own=own, side=side, owner=owner):
+                for j in range(per):
+                    local = owner * per + j
+                    position = local if half % chips else slot * per + j
+                    use(n, j, own, position + (half if own else 0), side * half + local)
+
+            if half % chips:
+                pl.when(owner < half // per)(run)
+            else:
+                run()
+
+
+def early_kernel(per, slots, chips, place, f_ref, *refs):
     parts, out_ref = refs[:-1], refs[-1]
-    half = f_ref.shape[0] // 2
-    chip = place[1]
-    count = len(parts) // 2
-    for n in range(count):
-        owner = jnp.bitwise_xor(chip, first + n)
-
-        def both(owner=owner, n=n):
-            for j in range(per):
-                head = owner * per + j
-                out_ref[n, 0, j] = read_out(f_ref[half + head], parts[n][j])
-                out_ref[n, 1, j] = read_out(f_ref[head], parts[count + n][j])
-
-        if owners < chips:
-            pl.when(owner < owners)(both)
-        else:
-            both()
-
-
-def output_kernel(per, owners, first, chips, place, f_ref, early_ref, *refs):
+
+    def use(n, j, own, position, head):
+        part = parts[n if own else len(slots) + n]
+        out_ref[n, 0 if own else 1, j] = read_out(f_ref[position], part[j])
+
+    each_slot(place, slots, chips, f_ref.shape[0] // 2, per, use)
+
+
+def output_kernel(per, early, late, chips, place, f_ref, early_ref, *refs):
     o_ref, os0, os1 = refs[-3:]
     parts = refs[:-3]
-    count = len(parts) // 2
     heads, tok, wide = f_ref.shape
-    half = heads // 2
-    core, chip = place[0], place[1]
     mid = o_ref.shape[2] // 2
 
     def put(head, out):
         os0[pl.ds(head, tok, stride=heads), :] = out[:, :mid]
         os1[pl.ds(head, tok, stride=heads), :] = out[:, mid:]
 
-    for r in range(chips):
-        owner = jnp.bitwise_xor(chip, r)
-
-        def both(owner=owner, r=r):
-            for j in range(per):
-                head = owner * per + j
-                if r < first:
-                    own, other = early_ref[r, 0, j], early_ref[r, 1, j]
-                else:
-                    own = read_out(f_ref[half + head], parts[r - first][j])
-                    other = read_out(f_ref[head], parts[count + r - first][j])
-                put(core * half + head, own)
-                put((1 - core) * half + head, other)
-
-        if owners < chips:
-            pl.when(owner < owners)(both)
-        else:
-            both()
+    def use_early(n, j, own, position, head):
+        put(head, early_ref[n, 0 if own else 1, j])
+
+    def use_late(n, j, own, position, head):
+        put(head, read_out(f_ref[position], parts[n if own else len(late) + n][j]))
+
+    each_slot(place, early, chips, heads // 2, per, use_early)
+    each_slot(place, late, chips, heads // 2, per, use_late)
     o_ref[:, :, :mid] = os0[...].reshape(tok, heads, mid).astype(BF16)
     o_ref[:, :, mid:] = os1[...].reshape(tok, heads, mid).astype(BF16)
 
@@ -509,19 +602,20 @@
     unit = 2 * tok * key_dim * key_dim
     sibling = [(i, i ^ 1) for i in range(seq)]
 
-    give_map, give_basis, k_heads, trail, rows, inverse, v_own = pl.pallas_call(
-        placed(basis_kernel),
+    give_first, own_first, first_basis, k_heads, trail, rows, inverse, v_rest = pl.pallas_call(
+        placed(functools.partial(basis_kernel, chips, per)),
         out_shape=(
-            f32(half, key_dim, wide),
-            f32(half, tok, wide),
+            f32(per, key_dim, wide),
+            f32(per, key_dim, wide),
+            f32(2 * per, tok, wide),
             jax.ShapeDtypeStruct((heads, tok, key_dim), BF16),
-            f32(half, tok, key_dim),
+            f32(heads - 2 * per, tok, key_dim),
             f32(4, heads, tok),
-            f32(half, tok, tok),
-            jax.ShapeDtypeStruct((half, tok, value_dim), BF16),
+            f32(heads - 2 * per, tok, tok),
+            jax.ShapeDtypeStruct((heads - 2 * per, tok, value_dim), BF16),
         ),
         in_specs=[pl.BlockSpec(memory_space=pltpu.HBM)] * 4,
-        out_specs=tuple(vmem(7)),
+        out_specs=tuple(vmem(8)),
         scratch_shapes=[
             pltpu.VMEM((tok, heads, key_dim), BF16),
             pltpu.VMEM((tok, heads, value_dim), BF16),
@@ -536,37 +630,67 @@
         cost_estimate=pl.CostEstimate(
             flops=50 * heads * unit, bytes_accessed=0, transcendentals=0
         ),
-    )(*(pltpu.with_memory_space_constraint(a, pltpu.HBM) for a in (key_rows, value_rows, log_gate, beta_rate)))
-    got_map = lax.ppermute(give_map, "seq", sibling)
-    own_map, own_basis = call(
-        own_map_kernel,
-        (f32(half, key_dim, wide), f32(half, tok, wide)),
-        flops=12 * half * unit,
-    )(inverse, k_heads, v_own, trail, rows)
-    chip_maps = call(
-        functools.partial(chip_kernel, key_dim, per), [f32(per, key_dim, wide)] * chips
-    )(own_map, got_map)
+    )(
+        *(
+            pltpu.with_memory_space_constraint(a, pltpu.HBM)
+            for a in (key_rows, value_rows, log_gate, beta_rate)
+        )
+    )
+    got_first = lax.ppermute(give_first, "seq", sibling)
+    give_rest, own_rest, rest_basis = call(
+        rest_kernel,
+        (
+            f32(half - per, key_dim, wide),
+            f32(half - per, key_dim, wide),
+            f32(heads - 2 * per, tok, wide),
+        ),
+        flops=200 * heads * unit,
+    )(inverse, k_heads, v_rest, trail, rows)
+    give_rest, got_first = lax.optimization_barrier((give_rest, got_first))
+    got_rest = lax.ppermute(give_rest, "seq", sibling)
+
+    def chip_maps(slots, *maps):
+        return call(
+            functools.partial(chip_kernel, key_dim, chips, slots),
+            [f32(per, key_dim, wide)] * len(slots),
+        )(*maps)
+
+    slots = list(range(chips))
+    if half % chips:
+        made = chip_maps(slots, own_first, own_rest, got_first, got_rest)
+    else:
+        made = chip_maps(slots[:1], own_first, got_first)
+        if chips > 1:
+            made = made + chip_maps(slots[1:], own_rest, got_rest)
+    distances = slot_list(chips)
 
     def across(parts, to_owner):
-        moved = [parts[0]]
-        for r in range(1, chips):
-            pairs = [
-                (i, i ^ (2 * r))
-                for i in range(seq)
-                if ((i ^ (2 * r)) // 2 if to_owner else i // 2) < owners
-            ]
-            moved.append(lax.ppermute(parts[r], "seq", pairs))
-        return moved
-
-    owned = across(chip_maps, True)
-    got_own = lax.ppermute(own_map, "seq", sibling)
-    folded = call(
-        query_kernel, f32(heads, tok, wide), [tall(key_dim)], flops=20 * heads * unit
-    )(queries, k_heads, rows, give_basis, own_basis, got_map, got_own)
+        moved = []
+        for slot in slots[:-1]:
+            swap = [(i, i ^ (2 * distances[i % 2][slot])) for i in range(seq)]
+            pairs = [(a, b) for a, b in swap if (b if to_owner else a) // 2 < owners]
+            moved.append(lax.ppermute(parts[slot], "seq", pairs))
+        return moved + [parts[-1]]
+
+    def folded_by(kernel, *arrays):
+        return call(
+            functools.partial(kernel, chips),
+            f32(heads, tok, wide),
+            [tall(key_dim)],
+            flops=20 * heads * unit,
+        )(*arrays, queries, k_heads, rows, first_basis, rest_basis)
+
+    made = list(made)
+    folded = folded_by(query_kernel)
+    made[0], folded = lax.optimization_barrier((made[0], folded))
+    owned = across(made, True)
+    owned[0], folded = lax.optimization_barrier((owned[0], folded))
+    folded = folded_by(query_late_kernel, folded)
     owned, folded = lax.optimization_barrier((owned, folded))
     total = call(functools.partial(total_kernel, key_dim), f32(per, key_dim, wide))(
         *owned
     )
+    total, *owned = lax.optimization_barrier((total, *owned))
     prefix = call(
         functools.partial(prefix_kernel, key_dim), f32(chips - 1, per, key_dim, wide)
     )(*owned)
@@ -593,18 +717,26 @@
             )(got, prefix)
         level += 1
     arrived = across(states, False)
-    others = [lax.ppermute(part, "seq", sibling) for part in arrived]
-    first = max(chips // 2, 1)
-    early = call(
-        functools.partial(early_kernel, per, owners, 0, chips),
-        f32(first, 2, per, tok, value_dim),
-        flops=6 * first * per * unit,
-    )(folded, *arrived[:first], *others[:first])
+    kept, others = [], []
+    for slot, part in enumerate(arrived):
+        keep, give = call(
+            functools.partial(pair_kernel, chips, slot),
+            [f32(per, key_dim, value_dim)] * 2,
+        )(own_first, own_rest, got_first, got_rest, part)
+        kept.append(keep)
+        others.append(lax.ppermute(give, "seq", sibling))
+    early = (slots[-1:] + slots[:-1])[: max(chips // 2, 1)]
+    late = [slot for slot in slots if slot not in early]
+    early_outs = call(
+        functools.partial(early_kernel, per, early, chips),
+        f32(len(early), 2, per, tok, value_dim),
+        flops=6 * len(early) * per * unit,
+    )(folded, *(kept[n] for n in early), *(others[n] for n in early))
     return call(
-        functools.partial(output_kernel, per, owners, first, chips),
+        functools.partial(output_kernel, per, early, late, chips),
         jax.ShapeDtypeStruct((tok, heads, value_dim), BF16),
         [tall(value_dim // 2), tall(value_dim // 2)],
-    )(folded, early, *arrived[first:], *others[first:])
+    )(folded, early_outs, *(kept[n] for n in late), *(others[n] for n in late))
 
 
 def solution(mesh):

time: 46.9 us -> 45.4 us (0.968)
  waiting for transfers between devices: 22 us -> 19.1 us
  Pallas kernels: 11.1 us -> 12.2 us
    ppermute x12, waiting for transfers between devices: 13.5 us -> 11 us  [the longest x6 10.3 us: across(): moved.append(lax.ppermute(parts[slot], 'seq', pairs))]
    pallas_call x10 -> x16, Pallas kernels: 6.37 us -> 7.78 us  [run(): pl.pallas_call(placed(kernel), out_shape=out_shape, in_specs=vmem(len(arr...]
  transfers between devices with their start and end apart: 14 -> 14, of which waited for: 9 -> 10; matrix products, arithmetic and copies ran while one was open for 0% -> 0% of each run, Pallas kernels for 9% -> 12%
where the time goes in v5:
time: 45.4 us; the launch traced here: 45.3 us
  waiting for transfers between devices  19.1 us (42%)
  starting transfers between devices  13.8 us (30%)
  Pallas kernels  12.2 us (27%)
    ppermute x6, waiting for transfers between devices, across(): moved.append(lax.ppermute(parts[slot], 'seq', pairs))  10.3 us
    ppermute x6, starting transfers between devices, across(): moved.append(lax.ppermute(parts[slot], 'seq', pairs))  8.17 us
    pallas_call x16, Pallas kernels, run(): pl.pallas_call(placed(kernel), out_shape=out_shape, in_specs=vmem(len(arr...  7.78 us
    pallas_call x1, Pallas kernels, body(): pl.pallas_call(placed(functools.partial(basis_kernel, chips, per)), out_s...  4.4 us
    ppermute x1, waiting for transfers between devices, body(): got_state = lax.ppermute(total, 'grp', swap)  4.08 us
    ppermute x1, waiting for transfers between devices, body(): got = lax.ppermute(total, 'grp', swap)  4.03 us
    ppermute x1, starting transfers between devices, body(): got_state = lax.ppermute(total, 'grp', swap)  2.71 us
    ppermute x1, starting transfers between devices, body(): got = lax.ppermute(total, 'grp', swap)  1.7 us
  transfers between devices with their start and end apart: 14, of which 10 were waited for; matrix products, arithmetic and copies ran while one was open for 0% of the time, Pallas kernels for 12%

profile of v5, /device:TPU:0, one launch (start us, length us, event | category | flops | bytes accessed | tf_op | source)
XLA Modules:
  0.0 45.3 jit_solution(6350109228545765933)
XLA Ops:
  0.0 4.4 %shard_map.55 = (f32[1,128,384]{2,1,0:T(8,128)S(1)}, f32[1,128,384]{2,1,0:T(8,128)S(1)}, f32[2,128,384]{2,1,0:T(8,128)S(1)}, bf16[8,128,128]{2,1,0:T(8,128)(2,1)...) custom-call(bf16[128,8,128]{2,1,0:T(8,128)(2,1)} %refs_0_.2, ...), custom_call_target="tpu_custom_call" | custom-call | flops 1677721600 | tf_op jit(solution)/shard_map/pallas_call | solution.py:605
  4.4 0.5 %collective-permute-start = (f32[1,128,384]{2,1,0:T(8,128)S(1)}, f32[1,128,384]{2,1,0:T(8,128)S(1)}, u32[]{:S(2)}, u32[]{:S(2)}) collective-permute-start(f32[1,128,384]{2,1,0:T(8,128)S(1)} %get-tuple-element.54), channel_id=1, source_target_pairs={{0,4},{4,0},{8,12},{12,8},{16,20},{20,16},{24,28},{28,24},{1,5},{5... | collective-permute-start | bytes 589832 | tf_op jit(solution)/shard_map/ppermute | solution.py:639
  4.9 0.0 copy-start
  4.9 1.4 %shard_map.56 = (f32[3,128,384]{2,1,0:T(8,128)S(1)}, f32[3,128,384]{2,1,0:T(8,128)S(1)}, f32[6,128,384]{2,1,0:T(8,128)S(1)}) custom-call(f32[6,128,128]{2,1,0:T(8,128)S(1)} %get-tuple-element.48.refs_0_, bf16[8,128,128]{2,1,0:T(8,128)(2,1)S(1)} %get-tuple-element.49.refs_1_.refs_2_, bf16[6,128,256]{2,1,0:T(8,128)(2,1)S(1)} %get-tuple-element.50.refs_2_, ...), custom_call_target="tpu_custom_call" | custom-call | flops 6710886400 | tf_op jit(solution)/shard_map/pallas_call | solution.py:105
  6.3 0.0 collective-permute-done.refs_1_.refs_2_
  6.4 0.1 collective-permute-start.2
  6.5 0.0 copy-done
  6.5 1.8 %shard_map.58.refs_0_ = f32[8,128,384]{2,1,0:T(8,128)S(1)} custom-call(bf16[128,8,128]{2,1,0:T(8,128)(2,1)S(1)} %copy-done, bf16[8,128,128]{2,1,0:T(8,128)(2,1)S(1)} %get-tuple-element.49.refs_1_.refs_2_, f32[4,8,128]{2,1,0:T(8,128)S(1)} %get-tuple-element.52.refs_4_.refs_2_.refs_3_, f32[2,128,384]{2,1,0:T(8,128)S(1)} %get-tuple-element.56.refs_3_.refs_4_, ...), custom_call_target="tpu_custom_call" | custom-call | flops 671088640 | tf_op jit(solution)/shard_map/pallas_call | solution.py:105
  8.3 0.2 shard_map.57
  8.5 4.0 %collective-permute-start.1 = (f32[1,128,384]{2,1,0:T(8,128)S(1)}, f32[1,128,384]{2,1,0:T(8,128)S(1)}, u32[]{:S(2)}, u32[]{:S(2)}) collective-permute-start(f32[1,128,384]{2,1,0:T(8,128)S(1)} %shard_map.57), channel_id=1, source_target_pairs={{0,24},{4,28},{8,16},{12,20},{16,8},{20,12},{24,0},{28,4},{1,25},{... | collective-permute-start | bytes 589832 | tf_op jit(solution)/shard_map/ppermute | solution.py:672
  12.5 0.0 collective-permute-done.2.refs_1_.refs_3_
  12.5 0.4 shard_map.59
  12.9 0.6 %collective-permute-start.3 = (f32[1,128,384]{2,1,0:T(8,128)S(1)}, f32[1,128,384]{2,1,0:T(8,128)S(1)}, u32[]{:S(2)}, u32[]{:S(2)}) collective-permute-start(f32[1,128,384]{2,1,0:T(8,128)S(1)} %get-tuple-element.63), channel_id=1, source_target_pairs={{0,8},{4,12},{8,0},{12,4},{16,24},{20,28},{24,16},{28,20},{1,9},{5... | collective-permute-start | bytes 589832 | tf_op jit(solution)/shard_map/ppermute | solution.py:672
  13.5 0.1 collective-permute-start.4
  13.5 4.7 %collective-permute-done.1.refs_0_ = f32[1,128,384]{2,1,0:T(8,128)S(1)} collective-permute-done((f32[1,128,384]{2,1,0:T(8,128)S(1)}, f32[1,128,384]{2,1,0:T(8,128)S(1)}, u32[]{:S(2)}, u32[]{:S(2)}) %collective-permute-start.1) | collective-permute-done | bytes 196640 | tf_op jit(solution)/shard_map/ppermute | solution.py:672
  18.2 0.1 shard_map.60.refs_0_
  18.3 1.9 %collective-permute-done.3.refs_1_ = f32[1,128,384]{2,1,0:T(8,128)S(1)} collective-permute-done((f32[1,128,384]{2,1,0:T(8,128)S(1)}, f32[1,128,384]{2,1,0:T(8,128)S(1)}, u32[]{:S(2)}, u32[]{:S(2)}) %collective-permute-start.3) | collective-permute-done | bytes 196640 | tf_op jit(solution)/shard_map/ppermute | solution.py:672
  20.3 0.2 collective-permute-done.4.refs_2_
  20.4 0.5 %shard_map.61.refs_0_ = f32[1,128,384]{2,1,0:T(8,128)S(1)} custom-call(f32[1,128,384]{2,1,0:T(8,128)S(1)} %collective-permute-done.1.refs_0_, f32[1,128,384]{2,1,0:T(8,128)S(1)} %collective-permute-done.3.refs_1_, f32[1,128,384]{2,1,0:T(8,128)S(1)} %collective-permute-done.4.refs_2_, f32[1,128,384]{2,1,0:T(8,128)S(1)} %get-tuple-element.76.refs_3_), custom_call_target="tpu_custom_call" | custom-call | tf_op jit(solution)/shard_map/pallas_call | solution.py:105
  20.9 1.7 %collective-permute-start.5 = (f32[1,128,384]{2,1,0:T(8,128)S(1)}, f32[1,128,384]{2,1,0:T(8,128)S(1)}, u32[]{:S(2)}, u32[]{:S(2)}) collective-permute-start(f32[1,128,384]{2,1,0:T(8,128)S(1)} %shard_map.61.refs_0_), channel_id=1, source_target_pairs={{0,1},{1,0},{2,3},{3,2},{4,5},{5,4},{6,7},{7,6},{8,9},{9,8},{10,11... | collective-permute-start | bytes 589832 | tf_op jit(solution)/shard_map/ppermute | solution.py:709
  22.6 4.0 %collective-permute-done.5.refs_1_.refs_0_ = f32[1,128,384]{2,1,0:T(8,128)S(1)} collective-permute-done((f32[1,128,384]{2,1,0:T(8,128)S(1)}, f32[1,128,384]{2,1,0:T(8,128)S(1)}, u32[]{:S(2)}, u32[]{:S(2)}) %collective-permute-start.5) | collective-permute-done | bytes 196640 | tf_op jit(solution)/shard_map/ppermute | solution.py:709
  26.7 0.2 shard_map.62
  26.9 2.7 %collective-permute-start.6 = (f32[1,128,256]{2,1,0:T(8,128)S(1)}, f32[1,128,256]{2,1,0:T(8,128)S(1)}, u32[]{:S(2)}, u32[]{:S(2)}) collective-permute-start(f32[1,128,256]{2,1,0:T(8,128)S(1)} %shard_map.62), channel_id=1, source_target_pairs={{0,2},{1,3},{2,0},{3,1},{4,6},{5,7},{6,4},{7,5},{8,10},{9,11},{10,... | collective-permute-start | bytes 393224 | tf_op jit(solution)/shard_map/ppermute | solution.py:703
  29.6 0.5 %shard_map.63.refs_1_ = f32[3,1,128,384]{3,2,1,0:T(8,128)S(1)} custom-call(f32[1,128,384]{2,1,0:T(8,128)S(1)} %collective-permute-done.1.refs_0_, f32[1,128,384]{2,1,0:T(8,128)S(1)} %collective-permute-done.3.refs_1_, f32[1,128,384]{2,1,0:T(8,128)S(1)} %collective-permute-done.4.refs_2_, f32[1,128,384]{2,1,0:T(8,128)S(1)} %get-tuple-element.76.refs_3_), custom_call_target="tpu_custom_call" | custom-call | tf_op jit(solution)/shard_map/pallas_call | solution.py:105
  30.1 0.1 shard_map.64.refs_1_
  30.1 4.1 %collective-permute-done.6.refs_0_ = f32[1,128,256]{2,1,0:T(8,128)S(1)} collective-permute-done((f32[1,128,256]{2,1,0:T(8,128)S(1)}, f32[1,128,256]{2,1,0:T(8,128)S(1)}, u32[]{:S(2)}, u32[]{:S(2)}) %collective-permute-start.6) | collective-permute-done | bytes 131104 | tf_op jit(solution)/shard_map/ppermute | solution.py:703
  34.2 0.3 shard_map.65
  34.5 2.3 %collective-permute-start.7 = (f32[1,128,256]{2,1,0:T(8,128)S(1)}, f32[1,128,256]{2,1,0:T(8,128)S(1)}, u32[]{:S(2)}, u32[]{:S(2)}) collective-permute-start(f32[1,128,256]{2,1,0:T(8,128)S(1)} %get-tuple-element.79), channel_id=1, source_target_pairs={{0,24},{4,28},{8,16},{12,20},{16,8},{20,12},{24,0},{28,4},{1,25},{... | collective-permute-start | bytes 393224 | tf_op jit(solution)/shard_map/ppermute | solution.py:672
  36.8 0.6 %collective-permute-start.11 = (f32[1,128,256]{2,1,0:T(8,128)S(1)}, f32[1,128,256]{2,1,0:T(8,128)S(1)}, u32[]{:S(2)}, u32[]{:S(2)}) collective-permute-start(f32[1,128,256]{2,1,0:T(8,128)S(1)} %get-tuple-element.85), channel_id=1, source_target_pairs={{0,16},{4,20},{8,24},{12,28},{16,0},{20,4},{24,8},{28,12},{1,17},{... | collective-permute-start | bytes 393224 | tf_op jit(solution)/shard_map/ppermute | solution.py:672
  37.4 0.7 %collective-permute-start.10 = (f32[1,128,256]{2,1,0:T(8,128)S(1)}, f32[1,128,256]{2,1,0:T(8,128)S(1)}, u32[]{:S(2)}, u32[]{:S(2)}) collective-permute-start(f32[1,128,256]{2,1,0:T(8,128)S(1)} %get-tuple-element.83), channel_id=1, source_target_pairs={{0,8},{4,12},{8,0},{12,4},{16,24},{20,28},{24,16},{28,20},{1,9},{5... | collective-permute-start | bytes 393224 | tf_op jit(solution)/shard_map/ppermute | solution.py:672
  38.1 0.2 shard_map.66
  38.3 0.1 collective-permute-start.8
  38.3 2.1 %collective-permute-done.7.refs_4_ = f32[1,128,256]{2,1,0:T(8,128)S(1)} collective-permute-done((f32[1,128,256]{2,1,0:T(8,128)S(1)}, f32[1,128,256]{2,1,0:T(8,128)S(1)}, u32[]{:S(2)}, u32[]{:S(2)}) %collective-permute-start.7) | collective-permute-done | bytes 131104 | tf_op jit(solution)/shard_map/ppermute | solution.py:672
  40.4 0.2 shard_map.67
  40.6 0.1 collective-permute-start.9
  40.7 1.1 %collective-permute-done.11.refs_4_ = f32[1,128,256]{2,1,0:T(8,128)S(1)} collective-permute-done((f32[1,128,256]{2,1,0:T(8,128)S(1)}, f32[1,128,256]{2,1,0:T(8,128)S(1)}, u32[]{:S(2)}, u32[]{:S(2)}) %collective-permute-start.11) | collective-permute-done | bytes 131104 | tf_op jit(solution)/shard_map/ppermute | solution.py:672
  41.8 0.2 shard_map.70
  42.0 0.1 collective-permute-start.13
  42.1 0.2 collective-permute-done.10.refs_4_
  42.3 0.2 shard_map.69
  42.5 0.3 collective-permute-start.12
  42.9 0.0 collective-permute-done.8.refs_3_
  42.9 0.0 collective-permute-done.9.refs_4_
  42.9 0.3 shard_map.68.refs_1_
  43.2 0.3 collective-permute-done.13.refs_5_
  43.4 0.5 %collective-permute-done.12.refs_4_ = f32[1,128,256]{2,1,0:T(8,128)S(1)} collective-permute-done((f32[1,128,256]{2,1,0:T(8,128)S(1)}, f32[1,128,256]{2,1,0:T(8,128)S(1)}, u32[]{:S(2)}, u32[]{:S(2)}) %collective-permute-start.12) | collective-permute-done | bytes 131104 | tf_op jit(solution)/shard_map/ppermute | solution.py:727
  43.9 1.3 %shard_map.71 = bf16[128,8,256]{2,1,0:T(8,128)(2,1)} custom-call(f32[8,128,384]{2,1,0:T(8,128)S(1)} %shard_map.60.refs_0_, f32[2,2,1,128,256]{4,3,2,1,0:T(8,128)S(1)} %shard_map.68.refs_1_, f32[1,128,256]{2,1,0:T(8,128)S(1)} %get-tuple-element.84.refs_2_, f32[1,128,256]{2,1,0:T(8,128)S(1)} %get-tuple-element.86.refs_3_, ...), custom_call_target="tpu_custom_call" | custom-call | tf_op jit(solution)/shard_map/pallas_call | solution.py:105
Async XLA Ops:
  4.4 1.9 %collective-permute-start = (f32[1,128,384]{2,1,0:T(8,128)S(1)}, f32[1,128,384]{2,1,0:T(8,128)S(1)}, u32[]{:S(2)}, u32[]{:S(2)}) collective-permute-start(f32[1,128,384]{2,1,0:T(8,128)S(1)} %get-tuple-element.54), channel_id=1, source_target_pairs={{0,4},{4,0},{8,12},{12,8},{16,20},{20,16},{24,28},{28,24},{1,5},{5... | collective-permute-start | bytes 589832 | tf_op jit(solution)/shard_map/ppermute | solution.py:639
  4.9 1.5 %copy-start = (bf16[128,8,128]{2,1,0:T(8,128)(2,1)S(1)}, bf16[128,8,128]{2,1,0:T(8,128)(2,1)}, u32[]{:S(2)}) copy-start(bf16[128,8,128]{2,1,0:T(8,128)(2,1)} %refs_1_.3) | copy-start | bytes 786436
  6.4 6.2 %collective-permute-start.2 = (f32[3,128,384]{2,1,0:T(8,128)S(1)}, f32[3,128,384]{2,1,0:T(8,128)S(1)}, u32[]{:S(2)}, u32[]{:S(2)}) collective-permute-start(f32[3,128,384]{2,1,0:T(8,128)S(1)} %get-tuple-element.62), channel_id=1, source_target_pairs={{0,4},{4,0},{8,12},{12,8},{16,20},{20,16},{24,28},{28,24},{1,5},{5... | collective-permute-start | bytes 1769480 | tf_op jit(solution)/shard_map/ppermute | solution.py:650
  8.5 9.7 %collective-permute-start.1 = (f32[1,128,384]{2,1,0:T(8,128)S(1)}, f32[1,128,384]{2,1,0:T(8,128)S(1)}, u32[]{:S(2)}, u32[]{:S(2)}) collective-permute-start(f32[1,128,384]{2,1,0:T(8,128)S(1)} %shard_map.57), channel_id=1, source_target_pairs={{0,24},{4,28},{8,16},{12,20},{16,8},{20,12},{24,0},{28,4},{1,25},{... | collective-permute-start | bytes 589832 | tf_op jit(solution)/shard_map/ppermute | solution.py:672
  12.9 7.4 %collective-permute-start.3 = (f32[1,128,384]{2,1,0:T(8,128)S(1)}, f32[1,128,384]{2,1,0:T(8,128)S(1)}, u32[]{:S(2)}, u32[]{:S(2)}) collective-permute-start(f32[1,128,384]{2,1,0:T(8,128)S(1)} %get-tuple-element.63), channel_id=1, source_target_pairs={{0,8},{4,12},{8,0},{12,4},{16,24},{20,28},{24,16},{28,20},{1,9},{5... | collective-permute-start | bytes 589832 | tf_op jit(solution)/shard_map/ppermute | solution.py:672
  13.5 7.0 %collective-permute-start.4 = (f32[1,128,384]{2,1,0:T(8,128)S(1)}, f32[1,128,384]{2,1,0:T(8,128)S(1)}, u32[]{:S(2)}, u32[]{:S(2)}) collective-permute-start(f32[1,128,384]{2,1,0:T(8,128)S(1)} %get-tuple-element.64), channel_id=1, source_target_pairs={{0,16},{4,20},{8,24},{12,28},{16,0},{20,4},{24,8},{28,12},{1,17},{... | collective-permute-start | bytes 589832 | tf_op jit(solution)/shard_map/ppermute | solution.py:672
  20.9 5.7 %collective-permute-start.5 = (f32[1,128,384]{2,1,0:T(8,128)S(1)}, f32[1,128,384]{2,1,0:T(8,128)S(1)}, u32[]{:S(2)}, u32[]{:S(2)}) collective-permute-start(f32[1,128,384]{2,1,0:T(8,128)S(1)} %shard_map.61.refs_0_), channel_id=1, source_target_pairs={{0,1},{1,0},{2,3},{3,2},{4,5},{5,4},{6,7},{7,6},{8,9},{9,8},{10,11... | collective-permute-start | bytes 589832 | tf_op jit(solution)/shard_map/ppermute | solution.py:709
  26.9 7.3 %collective-permute-start.6 = (f32[1,128,256]{2,1,0:T(8,128)S(1)}, f32[1,128,256]{2,1,0:T(8,128)S(1)}, u32[]{:S(2)}, u32[]{:S(2)}) collective-permute-start(f32[1,128,256]{2,1,0:T(8,128)S(1)} %shard_map.62), channel_id=1, source_target_pairs={{0,2},{1,3},{2,0},{3,1},{4,6},{5,7},{6,4},{7,5},{8,10},{9,11},{10,... | collective-permute-start | bytes 393224 | tf_op jit(solution)/shard_map/ppermute | solution.py:703
  34.5 5.9 %collective-permute-start.7 = (f32[1,128,256]{2,1,0:T(8,128)S(1)}, f32[1,128,256]{2,1,0:T(8,128)S(1)}, u32[]{:S(2)}, u32[]{:S(2)}) collective-permute-start(f32[1,128,256]{2,1,0:T(8,128)S(1)} %get-tuple-element.79), channel_id=1, source_target_pairs={{0,24},{4,28},{8,16},{12,20},{16,8},{20,12},{24,0},{28,4},{1,25},{... | collective-permute-start | bytes 393224 | tf_op jit(solution)/shard_map/ppermute | solution.py:672
  36.8 5.0 %collective-permute-start.11 = (f32[1,128,256]{2,1,0:T(8,128)S(1)}, f32[1,128,256]{2,1,0:T(8,128)S(1)}, u32[]{:S(2)}, u32[]{:S(2)}) collective-permute-start(f32[1,128,256]{2,1,0:T(8,128)S(1)} %get-tuple-element.85), channel_id=1, source_target_pairs={{0,16},{4,20},{8,24},{12,28},{16,0},{20,4},{24,8},{28,12},{1,17},{... | collective-permute-start | bytes 393224 | tf_op jit(solution)/shard_map/ppermute | solution.py:672
  37.4 5.0 %collective-permute-start.10 = (f32[1,128,256]{2,1,0:T(8,128)S(1)}, f32[1,128,256]{2,1,0:T(8,128)S(1)}, u32[]{:S(2)}, u32[]{:S(2)}) collective-permute-start(f32[1,128,256]{2,1,0:T(8,128)S(1)} %get-tuple-element.83), channel_id=1, source_target_pairs={{0,8},{4,12},{8,0},{12,4},{16,24},{20,28},{24,16},{28,20},{1,9},{5... | collective-permute-start | bytes 393224 | tf_op jit(solution)/shard_map/ppermute | solution.py:672
  38.3 4.6 %collective-permute-start.8 = (f32[1,128,256]{2,1,0:T(8,128)S(1)}, f32[1,128,256]{2,1,0:T(8,128)S(1)}, u32[]{:S(2)}, u32[]{:S(2)}) collective-permute-start(f32[1,128,256]{2,1,0:T(8,128)S(1)} %get-tuple-element.81), channel_id=1, source_target_pairs={{0,4},{4,0},{8,12},{12,8},{16,20},{20,16},{24,28},{28,24},{1,5},{5... | collective-permute-start | bytes 393224 | tf_op jit(solution)/shard_map/ppermute | solution.py:727
  40.6 2.2 %collective-permute-start.9 = (f32[1,128,256]{2,1,0:T(8,128)S(1)}, f32[1,128,256]{2,1,0:T(8,128)S(1)}, u32[]{:S(2)}, u32[]{:S(2)}) collective-permute-start(f32[1,128,256]{2,1,0:T(8,128)S(1)} %get-tuple-element.82), channel_id=1, source_target_pairs={{0,4},{4,0},{8,12},{12,8},{16,20},{20,16},{24,28},{28,24},{1,5},{5... | collective-permute-start | bytes 393224 | tf_op jit(solution)/shard_map/ppermute | solution.py:727
  42.0 1.4 %collective-permute-start.13 = (f32[1,128,256]{2,1,0:T(8,128)S(1)}, f32[1,128,256]{2,1,0:T(8,128)S(1)}, u32[]{:S(2)}, u32[]{:S(2)}) collective-permute-start(f32[1,128,256]{2,1,0:T(8,128)S(1)} %get-tuple-element.88), channel_id=1, source_target_pairs={{0,4},{4,0},{8,12},{12,8},{16,20},{20,16},{24,28},{28,24},{1,5},{5... | collective-permute-start | bytes 393224 | tf_op jit(solution)/shard_map/ppermute | solution.py:727
  42.5 1.4 %collective-permute-start.12 = (f32[1,128,256]{2,1,0:T(8,128)S(1)}, f32[1,128,256]{2,1,0:T(8,128)S(1)}, u32[]{:S(2)}, u32[]{:S(2)}) collective-permute-start(f32[1,128,256]{2,1,0:T(8,128)S(1)} %get-tuple-element.87), channel_id=1, source_target_pairs={{0,4},{4,0},{8,12},{12,8},{16,20},{20,16},{24,28},{28,24},{1,5},{5... | collective-permute-start | bytes 393224 | tf_op jit(solution)/shard_map/ppermute | solution.py:727

commit v6 on v5

--- a/solution.py
+++ b/solution.py
@@ -322,19 +322,26 @@
     key_dim = wide - v_ref.shape[2]
     heads = kh_ref.shape[0]
     eye_key = eye_mask(key_dim)
-    for n, i in enumerate(positions(heads, (heads - rest) // 2)[1]):
-        at = slice(i, i + 1)
-        k_raw = kh_ref[i]
-        basis = updates_basis(
-            inverse_ref[n], k_raw, v_ref[n], rows_ref[2, at, :], rows_ref[3, at, :]
+    where = positions(heads, (heads - rest) // 2)[1]
+    k_raw = [kh_ref[i] for i in where]
+    trail = [trail_ref[n][:, :1] for n in range(rest)]
+    last = [jnp.exp(rows_ref[1, i : i + 1, tok - 1 :]) for i in where]
+    bases = [
+        updates_basis(
+            inverse_ref[n], k_raw[n], v_ref[n], rows_ref[2, i : i + 1, :], rows_ref[3, i : i + 1, :]
         )
-        r_ref[n] = basis
-        last = jnp.exp(rows_ref[1, at, tok - 1 :])
-        made = trailing_map(basis, trail_ref[n][:, :1], k_raw, last, eye_key, key_dim)
+        for n, i in enumerate(where)
+    ]
+    made = [
+        trailing_map(b, t, k, e, eye_key, key_dim)
+        for b, t, k, e in zip(bases, trail, k_raw, last)
+    ]
+    for n in range(rest):
+        r_ref[n] = bases[n]
         if n < rest // 2:
-            give_ref[n] = made
+            give_ref[n] = made[n]
         else:
-            own_ref[n - rest // 2] = made
+            own_ref[n - rest // 2] = made[n]
 
 
 def query_rows(chips, place, q_ref, kh_ref, rows_ref, r_first, r_rest, f_ref, qs):
@@ -717,6 +724,7 @@
             )(got, prefix)
         level += 1
     arrived = across(states, False)
+    arrived[0], arrived[-1] = lax.optimization_barrier((arrived[0], arrived[-1]))
     kept, others = [], []
     for slot, part in enumerate(arrived):
         keep, give = call(

time: 45.4 us -> 45.3 us (level)
  Pallas kernels: 12.2 us -> 11.4 us
    pallas_call x16, Pallas kernels: 7.78 us -> 6.99 us  [run(): pl.pallas_call(placed(kernel), out_shape=out_shape, in_specs=vmem(len(arr...]
    ppermute x4, starting transfers between devices: 0.55 us -> 1.05 us  [body(): others.append(lax.ppermute(give, 'seq', sibling))]
  transfers between devices with their start and end apart: 14 -> 14, of which waited for: 10 -> 10; matrix products, arithmetic and copies ran while one was open for 0% -> 0% of each run, Pallas kernels for 12% -> 10%
where the time goes in v6:
time: 45.3 us; the launch traced here: 45.2 us
  waiting for transfers between devices  19.5 us (43%)
  starting transfers between devices  14.1 us (31%)
  Pallas kernels  11.4 us (25%)
    ppermute x6, waiting for transfers between devices, across(): moved.append(lax.ppermute(parts[slot], 'seq', pairs))  10.1 us
    ppermute x6, starting transfers between devices, across(): moved.append(lax.ppermute(parts[slot], 'seq', pairs))  7.86 us
    pallas_call x16, Pallas kernels, run(): pl.pallas_call(placed(kernel), out_shape=out_shape, in_specs=vmem(len(arr...  6.99 us
    pallas_call x1, Pallas kernels, body(): pl.pallas_call(placed(functools.partial(basis_kernel, chips, per)), out_s...  4.4 us
    ppermute x1, waiting for transfers between devices, body(): got_state = lax.ppermute(total, 'grp', swap)  4.15 us
    ppermute x1, waiting for transfers between devices, body(): got = lax.ppermute(total, 'grp', swap)  4.09 us
    ppermute x1, starting transfers between devices, body(): got_state = lax.ppermute(total, 'grp', swap)  2.65 us
    ppermute x1, starting transfers between devices, body(): got = lax.ppermute(total, 'grp', swap)  1.64 us
  transfers between devices with their start and end apart: 14, of which 10 were waited for; matrix products, arithmetic and copies ran while one was open for 0% of the time, Pallas kernels for 10%

profile of v6, /device:TPU:0, one launch (start us, length us, event | category | flops | bytes accessed | tf_op | source)
XLA Modules:
  0.0 45.2 jit_solution(16216603787554510183)
XLA Ops:
  0.0 4.4 %shard_map.55 = (f32[1,128,384]{2,1,0:T(8,128)S(1)}, f32[1,128,384]{2,1,0:T(8,128)S(1)}, f32[2,128,384]{2,1,0:T(8,128)S(1)}, bf16[8,128,128]{2,1,0:T(8,128)(2,1)...) custom-call(bf16[128,8,128]{2,1,0:T(8,128)(2,1)} %refs_0_.2, ...), custom_call_target="tpu_custom_call" | custom-call | flops 1677721600 | tf_op jit(solution)/shard_map/pallas_call | solution.py:612
  4.4 0.5 %collective-permute-start = (f32[1,128,384]{2,1,0:T(8,128)S(1)}, f32[1,128,384]{2,1,0:T(8,128)S(1)}, u32[]{:S(2)}, u32[]{:S(2)}) collective-permute-start(f32[1,128,384]{2,1,0:T(8,128)S(1)} %get-tuple-element.56), channel_id=1, source_target_pairs={{0,4},{4,0},{8,12},{12,8},{16,20},{20,16},{24,28},{28,24},{1,5},{5... | collective-permute-start | bytes 589832 | tf_op jit(solution)/shard_map/ppermute | solution.py:646
  4.9 0.0 copy-start
  4.9 0.6 %shard_map.56 = (f32[3,128,384]{2,1,0:T(8,128)S(1)}, f32[3,128,384]{2,1,0:T(8,128)S(1)}, f32[6,128,384]{2,1,0:T(8,128)S(1)}) custom-call(f32[6,128,128]{2,1,0:T(8,128)S(1)} %get-tuple-element.50.refs_0_, bf16[8,128,128]{2,1,0:T(8,128)(2,1)S(1)} %get-tuple-element.51.refs_1_.refs_2_, bf16[6,128,256]{2,1,0:T(8,128)(2,1)S(1)} %get-tuple-element.52.refs_2_, ...), custom_call_target="tpu_custom_call" | custom-call | flops 6710886400 | tf_op jit(solution)/shard_map/pallas_call | solution.py:105
  5.6 0.4 collective-permute-done.refs_1_.refs_2_
  6.0 0.4 collective-permute-start.2
  6.4 0.0 copy-done
  6.4 1.8 %shard_map.58.refs_0_ = f32[8,128,384]{2,1,0:T(8,128)S(1)} custom-call(bf16[128,8,128]{2,1,0:T(8,128)(2,1)S(1)} %copy-done, bf16[8,128,128]{2,1,0:T(8,128)(2,1)S(1)} %get-tuple-element.51.refs_1_.refs_2_, f32[4,8,128]{2,1,0:T(8,128)S(1)} %get-tuple-element.54.refs_4_.refs_2_.refs_3_, f32[2,128,384]{2,1,0:T(8,128)S(1)} %get-tuple-element.58.refs_3_.refs_4_, ...), custom_call_target="tpu_custom_call" | custom-call | flops 671088640 | tf_op jit(solution)/shard_map/pallas_call | solution.py:105
  8.2 0.2 shard_map.57
  8.4 3.6 %collective-permute-start.1 = (f32[1,128,384]{2,1,0:T(8,128)S(1)}, f32[1,128,384]{2,1,0:T(8,128)S(1)}, u32[]{:S(2)}, u32[]{:S(2)}) collective-permute-start(f32[1,128,384]{2,1,0:T(8,128)S(1)} %shard_map.57), channel_id=1, source_target_pairs={{0,24},{4,28},{8,16},{12,20},{16,8},{20,12},{24,0},{28,4},{1,25},{... | collective-permute-start | bytes 589832 | tf_op jit(solution)/shard_map/ppermute | solution.py:679
  12.1 0.0 collective-permute-done.2.refs_1_.refs_3_
  12.1 0.4 shard_map.59
  12.5 0.6 %collective-permute-start.3 = (f32[1,128,384]{2,1,0:T(8,128)S(1)}, f32[1,128,384]{2,1,0:T(8,128)S(1)}, u32[]{:S(2)}, u32[]{:S(2)}) collective-permute-start(f32[1,128,384]{2,1,0:T(8,128)S(1)} %get-tuple-element.65), channel_id=1, source_target_pairs={{0,8},{4,12},{8,0},{12,4},{16,24},{20,28},{24,16},{28,20},{1,9},{5... | collective-permute-start | bytes 589832 | tf_op jit(solution)/shard_map/ppermute | solution.py:679
  13.1 0.1 collective-permute-start.4
  13.1 4.8 %collective-permute-done.1.refs_0_ = f32[1,128,384]{2,1,0:T(8,128)S(1)} collective-permute-done((f32[1,128,384]{2,1,0:T(8,128)S(1)}, f32[1,128,384]{2,1,0:T(8,128)S(1)}, u32[]{:S(2)}, u32[]{:S(2)}) %collective-permute-start.1) | collective-permute-done | bytes 196640 | tf_op jit(solution)/shard_map/ppermute | solution.py:679
  17.9 0.1 shard_map.60.refs_0_
  18.0 2.1 %collective-permute-done.3.refs_1_ = f32[1,128,384]{2,1,0:T(8,128)S(1)} collective-permute-done((f32[1,128,384]{2,1,0:T(8,128)S(1)}, f32[1,128,384]{2,1,0:T(8,128)S(1)}, u32[]{:S(2)}, u32[]{:S(2)}) %collective-permute-start.3) | collective-permute-done | bytes 196640 | tf_op jit(solution)/shard_map/ppermute | solution.py:679
  20.2 0.0 collective-permute-done.4.refs_2_
  20.2 0.5 %shard_map.61.refs_0_ = f32[1,128,384]{2,1,0:T(8,128)S(1)} custom-call(f32[1,128,384]{2,1,0:T(8,128)S(1)} %collective-permute-done.1.refs_0_, f32[1,128,384]{2,1,0:T(8,128)S(1)} %collective-permute-done.3.refs_1_, f32[1,128,384]{2,1,0:T(8,128)S(1)} %collective-permute-done.4.refs_2_, f32[1,128,384]{2,1,0:T(8,128)S(1)} %get-tuple-element.78.refs_3_), custom_call_target="tpu_custom_call" | custom-call | tf_op jit(solution)/shard_map/pallas_call | solution.py:105
  20.7 1.6 %collective-permute-start.5 = (f32[1,128,384]{2,1,0:T(8,128)S(1)}, f32[1,128,384]{2,1,0:T(8,128)S(1)}, u32[]{:S(2)}, u32[]{:S(2)}) collective-permute-start(f32[1,128,384]{2,1,0:T(8,128)S(1)} %shard_map.61.refs_0_), channel_id=1, source_target_pairs={{0,1},{1,0},{2,3},{3,2},{4,5},{5,4},{6,7},{7,6},{8,9},{9,8},{10,11... | collective-permute-start | bytes 589832 | tf_op jit(solution)/shard_map/ppermute | solution.py:716
  22.3 4.1 %collective-permute-done.5.refs_1_.refs_0_ = f32[1,128,384]{2,1,0:T(8,128)S(1)} collective-permute-done((f32[1,128,384]{2,1,0:T(8,128)S(1)}, f32[1,128,384]{2,1,0:T(8,128)S(1)}, u32[]{:S(2)}, u32[]{:S(2)}) %collective-permute-start.5) | collective-permute-done | bytes 196640 | tf_op jit(solution)/shard_map/ppermute | solution.py:716
  26.4 0.2 shard_map.62
  26.6 2.6 %collective-permute-start.6 = (f32[1,128,256]{2,1,0:T(8,128)S(1)}, f32[1,128,256]{2,1,0:T(8,128)S(1)}, u32[]{:S(2)}, u32[]{:S(2)}) collective-permute-start(f32[1,128,256]{2,1,0:T(8,128)S(1)} %shard_map.62), channel_id=1, source_target_pairs={{0,2},{1,3},{2,0},{3,1},{4,6},{5,7},{6,4},{7,5},{8,10},{9,11},{10,... | collective-permute-start | bytes 393224 | tf_op jit(solution)/shard_map/ppermute | solution.py:710
  29.3 0.5 %shard_map.63.refs_1_ = f32[3,1,128,384]{3,2,1,0:T(8,128)S(1)} custom-call(f32[1,128,384]{2,1,0:T(8,128)S(1)} %collective-permute-done.1.refs_0_, f32[1,128,384]{2,1,0:T(8,128)S(1)} %collective-permute-done.3.refs_1_, f32[1,128,384]{2,1,0:T(8,128)S(1)} %collective-permute-done.4.refs_2_, f32[1,128,384]{2,1,0:T(8,128)S(1)} %get-tuple-element.78.refs_3_), custom_call_target="tpu_custom_call" | custom-call | tf_op jit(solution)/shard_map/pallas_call | solution.py:105
  29.7 0.1 shard_map.64.refs_1_
  29.8 4.2 %collective-permute-done.6.refs_0_ = f32[1,128,256]{2,1,0:T(8,128)S(1)} collective-permute-done((f32[1,128,256]{2,1,0:T(8,128)S(1)}, f32[1,128,256]{2,1,0:T(8,128)S(1)}, u32[]{:S(2)}, u32[]{:S(2)}) %collective-permute-start.6) | collective-permute-done | bytes 131104 | tf_op jit(solution)/shard_map/ppermute | solution.py:710
  34.0 0.3 shard_map.65
  34.2 2.5 %collective-permute-start.7 = (f32[1,128,256]{2,1,0:T(8,128)S(1)}, f32[1,128,256]{2,1,0:T(8,128)S(1)}, u32[]{:S(2)}, u32[]{:S(2)}) collective-permute-start(f32[1,128,256]{2,1,0:T(8,128)S(1)} %get-tuple-element.79), channel_id=1, source_target_pairs={{0,24},{4,28},{8,16},{12,20},{16,8},{20,12},{24,0},{28,4},{1,25},{... | collective-permute-start | bytes 393224 | tf_op jit(solution)/shard_map/ppermute | solution.py:679
  36.8 0.5 %collective-permute-start.11 = (f32[1,128,256]{2,1,0:T(8,128)S(1)}, f32[1,128,256]{2,1,0:T(8,128)S(1)}, u32[]{:S(2)}, u32[]{:S(2)}) collective-permute-start(f32[1,128,256]{2,1,0:T(8,128)S(1)} %get-tuple-element.89), channel_id=1, source_target_pairs={{0,16},{4,20},{8,24},{12,28},{16,0},{20,4},{24,8},{28,12},{1,17},{... | collective-permute-start | bytes 393224 | tf_op jit(solution)/shard_map/ppermute | solution.py:679
  37.3 0.5 %collective-permute-start.10 = (f32[1,128,256]{2,1,0:T(8,128)S(1)}, f32[1,128,256]{2,1,0:T(8,128)S(1)}, u32[]{:S(2)}, u32[]{:S(2)}) collective-permute-start(f32[1,128,256]{2,1,0:T(8,128)S(1)} %get-tuple-element.87), channel_id=1, source_target_pairs={{0,8},{4,12},{8,0},{12,4},{16,24},{20,28},{24,16},{28,20},{1,9},{5... | collective-permute-start | bytes 393224 | tf_op jit(solution)/shard_map/ppermute | solution.py:679
  37.8 2.4 %collective-permute-done.7.refs_4_ = f32[1,128,256]{2,1,0:T(8,128)S(1)} collective-permute-done((f32[1,128,256]{2,1,0:T(8,128)S(1)}, f32[1,128,256]{2,1,0:T(8,128)S(1)}, u32[]{:S(2)}, u32[]{:S(2)}) %collective-permute-start.7) | collective-permute-done | bytes 131104 | tf_op jit(solution)/shard_map/ppermute | solution.py:679
  40.2 0.2 shard_map.67
  40.4 0.1 collective-permute-start.9
  40.4 0.2 shard_map.66
  40.6 0.6 %collective-permute-start.8 = (f32[1,128,256]{2,1,0:T(8,128)S(1)}, f32[1,128,256]{2,1,0:T(8,128)S(1)}, u32[]{:S(2)}, u32[]{:S(2)}) collective-permute-start(f32[1,128,256]{2,1,0:T(8,128)S(1)} %get-tuple-element.85), channel_id=1, source_target_pairs={{0,4},{4,0},{8,12},{12,8},{16,20},{20,16},{24,28},{28,24},{1,5},{5... | collective-permute-start | bytes 393224 | tf_op jit(solution)/shard_map/ppermute | solution.py:735
  41.2 0.6 %collective-permute-done.11.refs_4_ = f32[1,128,256]{2,1,0:T(8,128)S(1)} collective-permute-done((f32[1,128,256]{2,1,0:T(8,128)S(1)}, f32[1,128,256]{2,1,0:T(8,128)S(1)}, u32[]{:S(2)}, u32[]{:S(2)}) %collective-permute-start.11) | collective-permute-done | bytes 131104 | tf_op jit(solution)/shard_map/ppermute | solution.py:679
  41.8 0.2 shard_map.70
  41.9 0.1 collective-permute-start.13
  42.0 0.2 collective-permute-done.10.refs_4_
  42.2 0.2 shard_map.69
  42.4 0.4 collective-permute-start.12
  42.8 0.0 collective-permute-done.9.refs_4_
  42.8 0.0 collective-permute-done.8.refs_3_
  42.8 0.3 shard_map.68.refs_1_
  43.1 0.3 collective-permute-done.13.refs_5_
  43.4 0.5 %collective-permute-done.12.refs_4_ = f32[1,128,256]{2,1,0:T(8,128)S(1)} collective-permute-done((f32[1,128,256]{2,1,0:T(8,128)S(1)}, f32[1,128,256]{2,1,0:T(8,128)S(1)}, u32[]{:S(2)}, u32[]{:S(2)}) %collective-permute-start.12) | collective-permute-done | bytes 131104 | tf_op jit(solution)/shard_map/ppermute | solution.py:735
  43.8 1.3 %shard_map.71 = bf16[128,8,256]{2,1,0:T(8,128)(2,1)} custom-call(f32[8,128,384]{2,1,0:T(8,128)S(1)} %shard_map.60.refs_0_, f32[2,2,1,128,256]{4,3,2,1,0:T(8,128)S(1)} %shard_map.68.refs_1_, f32[1,128,256]{2,1,0:T(8,128)S(1)} %get-tuple-element.88.refs_2_, f32[1,128,256]{2,1,0:T(8,128)S(1)} %get-tuple-element.90.refs_3_, ...), custom_call_target="tpu_custom_call" | custom-call | tf_op jit(solution)/shard_map/pallas_call | solution.py:105
Async XLA Ops:
  4.4 1.6 %collective-permute-start = (f32[1,128,384]{2,1,0:T(8,128)S(1)}, f32[1,128,384]{2,1,0:T(8,128)S(1)}, u32[]{:S(2)}, u32[]{:S(2)}) collective-permute-start(f32[1,128,384]{2,1,0:T(8,128)S(1)} %get-tuple-element.56), channel_id=1, source_target_pairs={{0,4},{4,0},{8,12},{12,8},{16,20},{20,16},{24,28},{28,24},{1,5},{5... | collective-permute-start | bytes 589832 | tf_op jit(solution)/shard_map/ppermute | solution.py:646
  4.9 1.4 %copy-start = (bf16[128,8,128]{2,1,0:T(8,128)(2,1)S(1)}, bf16[128,8,128]{2,1,0:T(8,128)(2,1)}, u32[]{:S(2)}) copy-start(bf16[128,8,128]{2,1,0:T(8,128)(2,1)} %refs_1_.3) | copy-start | bytes 786436
  6.0 6.1 %collective-permute-start.2 = (f32[3,128,384]{2,1,0:T(8,128)S(1)}, f32[3,128,384]{2,1,0:T(8,128)S(1)}, u32[]{:S(2)}, u32[]{:S(2)}) collective-permute-start(f32[3,128,384]{2,1,0:T(8,128)S(1)} %get-tuple-element.64), channel_id=1, source_target_pairs={{0,4},{4,0},{8,12},{12,8},{16,20},{20,16},{24,28},{28,24},{1,5},{5... | collective-permute-start | bytes 1769480 | tf_op jit(solution)/shard_map/ppermute | solution.py:657
  8.4 9.5 %collective-permute-start.1 = (f32[1,128,384]{2,1,0:T(8,128)S(1)}, f32[1,128,384]{2,1,0:T(8,128)S(1)}, u32[]{:S(2)}, u32[]{:S(2)}) collective-permute-start(f32[1,128,384]{2,1,0:T(8,128)S(1)} %shard_map.57), channel_id=1, source_target_pairs={{0,24},{4,28},{8,16},{12,20},{16,8},{20,12},{24,0},{28,4},{1,25},{... | collective-permute-start | bytes 589832 | tf_op jit(solution)/shard_map/ppermute | solution.py:679
  12.5 7.7 %collective-permute-start.3 = (f32[1,128,384]{2,1,0:T(8,128)S(1)}, f32[1,128,384]{2,1,0:T(8,128)S(1)}, u32[]{:S(2)}, u32[]{:S(2)}) collective-permute-start(f32[1,128,384]{2,1,0:T(8,128)S(1)} %get-tuple-element.65), channel_id=1, source_target_pairs={{0,8},{4,12},{8,0},{12,4},{16,24},{20,28},{24,16},{28,20},{1,9},{5... | collective-permute-start | bytes 589832 | tf_op jit(solution)/shard_map/ppermute | solution.py:679
  13.1 7.1 %collective-permute-start.4 = (f32[1,128,384]{2,1,0:T(8,128)S(1)}, f32[1,128,384]{2,1,0:T(8,128)S(1)}, u32[]{:S(2)}, u32[]{:S(2)}) collective-permute-start(f32[1,128,384]{2,1,0:T(8,128)S(1)} %get-tuple-element.66), channel_id=1, source_target_pairs={{0,16},{4,20},{8,24},{12,28},{16,0},{20,4},{24,8},{28,12},{1,17},{... | collective-permute-start | bytes 589832 | tf_op jit(solution)/shard_map/ppermute | solution.py:679
  20.7 5.7 %collective-permute-start.5 = (f32[1,128,384]{2,1,0:T(8,128)S(1)}, f32[1,128,384]{2,1,0:T(8,128)S(1)}, u32[]{:S(2)}, u32[]{:S(2)}) collective-permute-start(f32[1,128,384]{2,1,0:T(8,128)S(1)} %shard_map.61.refs_0_), channel_id=1, source_target_pairs={{0,1},{1,0},{2,3},{3,2},{4,5},{5,4},{6,7},{7,6},{8,9},{9,8},{10,11... | collective-permute-start | bytes 589832 | tf_op jit(solution)/shard_map/ppermute | solution.py:716
  26.6 7.3 %collective-permute-start.6 = (f32[1,128,256]{2,1,0:T(8,128)S(1)}, f32[1,128,256]{2,1,0:T(8,128)S(1)}, u32[]{:S(2)}, u32[]{:S(2)}) collective-permute-start(f32[1,128,256]{2,1,0:T(8,128)S(1)} %shard_map.62), channel_id=1, source_target_pairs={{0,2},{1,3},{2,0},{3,1},{4,6},{5,7},{6,4},{7,5},{8,10},{9,11},{10,... | collective-permute-start | bytes 393224 | tf_op jit(solution)/shard_map/ppermute | solution.py:710
  34.2 5.9 %collective-permute-start.7 = (f32[1,128,256]{2,1,0:T(8,128)S(1)}, f32[1,128,256]{2,1,0:T(8,128)S(1)}, u32[]{:S(2)}, u32[]{:S(2)}) collective-permute-start(f32[1,128,256]{2,1,0:T(8,128)S(1)} %get-tuple-element.79), channel_id=1, source_target_pairs={{0,24},{4,28},{8,16},{12,20},{16,8},{20,12},{24,0},{28,4},{1,25},{... | collective-permute-start | bytes 393224 | tf_op jit(solution)/shard_map/ppermute | solution.py:679
  36.8 5.0 %collective-permute-start.11 = (f32[1,128,256]{2,1,0:T(8,128)S(1)}, f32[1,128,256]{2,1,0:T(8,128)S(1)}, u32[]{:S(2)}, u32[]{:S(2)}) collective-permute-start(f32[1,128,256]{2,1,0:T(8,128)S(1)} %get-tuple-element.89), channel_id=1, source_target_pairs={{0,16},{4,20},{8,24},{12,28},{16,0},{20,4},{24,8},{28,12},{1,17},{... | collective-permute-start | bytes 393224 | tf_op jit(solution)/shard_map/ppermute | solution.py:679
  37.3 5.0 %collective-permute-start.10 = (f32[1,128,256]{2,1,0:T(8,128)S(1)}, f32[1,128,256]{2,1,0:T(8,128)S(1)}, u32[]{:S(2)}, u32[]{:S(2)}) collective-permute-start(f32[1,128,256]{2,1,0:T(8,128)S(1)} %get-tuple-element.87), channel_id=1, source_target_pairs={{0,8},{4,12},{8,0},{12,4},{16,24},{20,28},{24,16},{28,20},{1,9},{5... | collective-permute-start | bytes 393224 | tf_op jit(solution)/shard_map/ppermute | solution.py:679
  40.4 2.4 %collective-permute-start.9 = (f32[1,128,256]{2,1,0:T(8,128)S(1)}, f32[1,128,256]{2,1,0:T(8,128)S(1)}, u32[]{:S(2)}, u32[]{:S(2)}) collective-permute-start(f32[1,128,256]{2,1,0:T(8,128)S(1)} %get-tuple-element.86), channel_id=1, source_target_pairs={{0,4},{4,0},{8,12},{12,8},{16,20},{20,16},{24,28},{28,24},{1,5},{5... | collective-permute-start | bytes 393224 | tf_op jit(solution)/shard_map/ppermute | solution.py:735
  40.6 2.1 %collective-permute-start.8 = (f32[1,128,256]{2,1,0:T(8,128)S(1)}, f32[1,128,256]{2,1,0:T(8,128)S(1)}, u32[]{:S(2)}, u32[]{:S(2)}) collective-permute-start(f32[1,128,256]{2,1,0:T(8,128)S(1)} %get-tuple-element.85), channel_id=1, source_target_pairs={{0,4},{4,0},{8,12},{12,8},{16,20},{20,16},{24,28},{28,24},{1,5},{5... | collective-permute-start | bytes 393224 | tf_op jit(solution)/shard_map/ppermute | solution.py:735
  41.9 1.4 %collective-permute-start.13 = (f32[1,128,256]{2,1,0:T(8,128)S(1)}, f32[1,128,256]{2,1,0:T(8,128)S(1)}, u32[]{:S(2)}, u32[]{:S(2)}) collective-permute-start(f32[1,128,256]{2,1,0:T(8,128)S(1)} %get-tuple-element.92), channel_id=1, source_target_pairs={{0,4},{4,0},{8,12},{12,8},{16,20},{20,16},{24,28},{28,24},{1,5},{5... | collective-permute-start | bytes 393224 | tf_op jit(solution)/shard_map/ppermute | solution.py:735
  42.4 1.4 %collective-permute-start.12 = (f32[1,128,256]{2,1,0:T(8,128)S(1)}, f32[1,128,256]{2,1,0:T(8,128)S(1)}, u32[]{:S(2)}, u32[]{:S(2)}) collective-permute-start(f32[1,128,256]{2,1,0:T(8,128)S(1)} %get-tuple-element.91), channel_id=1, source_target_pairs={{0,4},{4,0},{8,12},{12,8},{16,20},{20,16},{24,28},{28,24},{1,5},{5... | collective-permute-start | bytes 393224 | tf_op jit(solution)/shard_map/ppermute | solution.py:735

commit v7 on v6

--- a/solution.py
+++ b/solution.py
@@ -574,8 +574,8 @@
 
 
 def output_kernel(per, early, late, chips, place, f_ref, early_ref, *refs):
-    o_ref, os0, os1 = refs[-3:]
-    parts = refs[:-3]
+    o_ref, ob, os0, os1, sems = refs[-5:]
+    parts = refs[:-5]
     heads, tok, wide = f_ref.shape
     mid = o_ref.shape[2] // 2
 
@@ -591,8 +591,19 @@
 
     each_slot(place, early, chips, heads // 2, per, use_early)
     each_slot(place, late, chips, heads // 2, per, use_late)
-    o_ref[:, :, :mid] = os0[...].reshape(tok, heads, mid).astype(BF16)
-    o_ref[:, :, mid:] = os1[...].reshape(tok, heads, mid).astype(BF16)
+    pieces = sems.shape[0]
+    rows = tok // pieces
+    copies = []
+    for n in range(pieces):
+        some = pl.ds(n * rows, rows)
+        flat = pl.ds(n * rows * heads, rows * heads)
+        ob[some, :, :mid] = os0[flat, :].reshape(rows, heads, mid).astype(BF16)
+        ob[some, :, mid:] = os1[flat, :].reshape(rows, heads, mid).astype(BF16)
+        copy = pltpu.make_async_copy(ob.at[some], o_ref.at[some], sems.at[n])
+        copy.start()
+        copies.append(copy)
+    for copy in copies:
+        copy.wait()
 
 
 def body(queries, key_rows, value_rows, log_gate, beta_rate):
@@ -740,11 +751,25 @@
         f32(len(early), 2, per, tok, value_dim),
         flops=6 * len(early) * per * unit,
     )(folded, *(kept[n] for n in early), *(others[n] for n in early))
-    return call(
-        functools.partial(output_kernel, per, early, late, chips),
-        jax.ShapeDtypeStruct((tok, heads, value_dim), BF16),
-        [tall(value_dim // 2), tall(value_dim // 2)],
-    )(folded, early_outs, *(kept[n] for n in late), *(others[n] for n in late))
+    inputs = (
+        folded,
+        early_outs,
+        *(kept[n] for n in late),
+        *(others[n] for n in late),
+    )
+    return pl.pallas_call(
+        placed(functools.partial(output_kernel, per, early, late, chips)),
+        out_shape=jax.ShapeDtypeStruct((tok, heads, value_dim), BF16),
+        in_specs=vmem(len(inputs)),
+        out_specs=pl.BlockSpec(memory_space=pltpu.HBM),
+        scratch_shapes=[
+            pltpu.VMEM((tok, heads, value_dim), BF16),
+            tall(value_dim // 2),
+            tall(value_dim // 2),
+            pltpu.SemaphoreType.DMA((2 if tok % 32 == 0 else 1,)),
+        ],
+        compiler_params=pltpu.CompilerParams(vmem_limit_bytes=VMEM_LIMIT),
+    )(*inputs)
 
 
 def solution(mesh):

time: 45.3 us -> 45.3 us (level)
    pallas_call x16 -> x15, Pallas kernels: 6.99 us -> 5.67 us  [run(): pl.pallas_call(placed(kernel), out_shape=out_shape, in_specs=vmem(len(arr...]
    pallas_call x0 -> x1, Pallas kernels: none -> 1.27 us  [body(): pl.pallas_call(placed(functools.partial(output_kernel, per, early, late,...]
where the time goes in v7:
time: 45.3 us; the launch traced here: 45.1 us
  waiting for transfers between devices  19.5 us (43%)
  starting transfers between devices  14.1 us (31%)
  Pallas kernels  11.3 us (25%)
    ppermute x6, waiting for transfers between devices, across(): moved.append(lax.ppermute(parts[slot], 'seq', pairs))  10.1 us
    ppermute x6, starting transfers between devices, across(): moved.append(lax.ppermute(parts[slot], 'seq', pairs))  7.86 us
    pallas_call x15, Pallas kernels, run(): pl.pallas_call(placed(kernel), out_shape=out_shape, in_specs=vmem(len(arr...  5.67 us
    pallas_call x1, Pallas kernels, body(): pl.pallas_call(placed(functools.partial(basis_kernel, chips, per)), out_s...  4.4 us
    ppermute x1, waiting for transfers between devices, body(): got_state = lax.ppermute(total, 'grp', swap)  4.15 us
    ppermute x1, waiting for transfers between devices, body(): got = lax.ppermute(total, 'grp', swap)  4.09 us
    ppermute x1, starting transfers between devices, body(): got_state = lax.ppermute(total, 'grp', swap)  2.65 us
    ppermute x1, starting transfers between devices, body(): got = lax.ppermute(total, 'grp', swap)  1.64 us
  transfers between devices with their start and end apart: 14, of which 10 were waited for; matrix products, arithmetic and copies ran while one was open for 0% of the time, Pallas kernels for 10%

profile of v7, /device:TPU:0, one launch (start us, length us, event | category | flops | bytes accessed | tf_op | source)
XLA Modules:
  0.0 45.1 jit_solution(8486946227334191613)
XLA Ops:
  0.0 4.4 %shard_map.55 = (f32[1,128,384]{2,1,0:T(8,128)S(1)}, f32[1,128,384]{2,1,0:T(8,128)S(1)}, f32[2,128,384]{2,1,0:T(8,128)S(1)}, bf16[8,128,128]{2,1,0:T(8,128)(2,1)...) custom-call(bf16[128,8,128]{2,1,0:T(8,128)(2,1)} %refs_0_.2, ...), custom_call_target="tpu_custom_call" | custom-call | flops 1677721600 | tf_op jit(solution)/shard_map/pallas_call | solution.py:623
  4.4 0.5 %collective-permute-start = (f32[1,128,384]{2,1,0:T(8,128)S(1)}, f32[1,128,384]{2,1,0:T(8,128)S(1)}, u32[]{:S(2)}, u32[]{:S(2)}) collective-permute-start(f32[1,128,384]{2,1,0:T(8,128)S(1)} %get-tuple-element.56), channel_id=1, source_target_pairs={{0,4},{4,0},{8,12},{12,8},{16,20},{20,16},{24,28},{28,24},{1,5},{5... | collective-permute-start | bytes 589832 | tf_op jit(solution)/shard_map/ppermute | solution.py:657
  4.9 0.0 copy-start
  4.9 0.6 %shard_map.56 = (f32[3,128,384]{2,1,0:T(8,128)S(1)}, f32[3,128,384]{2,1,0:T(8,128)S(1)}, f32[6,128,384]{2,1,0:T(8,128)S(1)}) custom-call(f32[6,128,128]{2,1,0:T(8,128)S(1)} %get-tuple-element.50.refs_0_, bf16[8,128,128]{2,1,0:T(8,128)(2,1)S(1)} %get-tuple-element.51.refs_1_.refs_2_, bf16[6,128,256]{2,1,0:T(8,128)(2,1)S(1)} %get-tuple-element.52.refs_2_, ...), custom_call_target="tpu_custom_call" | custom-call | flops 6710886400 | tf_op jit(solution)/shard_map/pallas_call | solution.py:105
  5.6 0.4 collective-permute-done.refs_1_.refs_2_
  6.0 0.4 collective-permute-start.2
  6.4 0.0 copy-done
  6.4 1.8 %shard_map.58.refs_0_ = f32[8,128,384]{2,1,0:T(8,128)S(1)} custom-call(bf16[128,8,128]{2,1,0:T(8,128)(2,1)S(1)} %copy-done, bf16[8,128,128]{2,1,0:T(8,128)(2,1)S(1)} %get-tuple-element.51.refs_1_.refs_2_, f32[4,8,128]{2,1,0:T(8,128)S(1)} %get-tuple-element.54.refs_4_.refs_2_.refs_3_, f32[2,128,384]{2,1,0:T(8,128)S(1)} %get-tuple-element.58.refs_3_.refs_4_, ...), custom_call_target="tpu_custom_call" | custom-call | flops 671088640 | tf_op jit(solution)/shard_map/pallas_call | solution.py:105
  8.2 0.2 shard_map.57
  8.4 3.6 %collective-permute-start.1 = (f32[1,128,384]{2,1,0:T(8,128)S(1)}, f32[1,128,384]{2,1,0:T(8,128)S(1)}, u32[]{:S(2)}, u32[]{:S(2)}) collective-permute-start(f32[1,128,384]{2,1,0:T(8,128)S(1)} %shard_map.57), channel_id=1, source_target_pairs={{0,24},{4,28},{8,16},{12,20},{16,8},{20,12},{24,0},{28,4},{1,25},{... | collective-permute-start | bytes 589832 | tf_op jit(solution)/shard_map/ppermute | solution.py:690
  12.1 0.0 collective-permute-done.2.refs_1_.refs_3_
  12.1 0.4 shard_map.59
  12.5 0.6 %collective-permute-start.3 = (f32[1,128,384]{2,1,0:T(8,128)S(1)}, f32[1,128,384]{2,1,0:T(8,128)S(1)}, u32[]{:S(2)}, u32[]{:S(2)}) collective-permute-start(f32[1,128,384]{2,1,0:T(8,128)S(1)} %get-tuple-element.65), channel_id=1, source_target_pairs={{0,8},{4,12},{8,0},{12,4},{16,24},{20,28},{24,16},{28,20},{1,9},{5... | collective-permute-start | bytes 589832 | tf_op jit(solution)/shard_map/ppermute | solution.py:690
  13.1 0.1 collective-permute-start.4
  13.1 4.8 %collective-permute-done.1.refs_0_ = f32[1,128,384]{2,1,0:T(8,128)S(1)} collective-permute-done((f32[1,128,384]{2,1,0:T(8,128)S(1)}, f32[1,128,384]{2,1,0:T(8,128)S(1)}, u32[]{:S(2)}, u32[]{:S(2)}) %collective-permute-start.1) | collective-permute-done | bytes 196640 | tf_op jit(solution)/shard_map/ppermute | solution.py:690
  17.9 0.1 shard_map.60.refs_0_
  18.0 2.1 %collective-permute-done.3.refs_1_ = f32[1,128,384]{2,1,0:T(8,128)S(1)} collective-permute-done((f32[1,128,384]{2,1,0:T(8,128)S(1)}, f32[1,128,384]{2,1,0:T(8,128)S(1)}, u32[]{:S(2)}, u32[]{:S(2)}) %collective-permute-start.3) | collective-permute-done | bytes 196640 | tf_op jit(solution)/shard_map/ppermute | solution.py:690
  20.2 0.0 collective-permute-done.4.refs_2_
  20.2 0.5 %shard_map.61.refs_0_ = f32[1,128,384]{2,1,0:T(8,128)S(1)} custom-call(f32[1,128,384]{2,1,0:T(8,128)S(1)} %collective-permute-done.1.refs_0_, f32[1,128,384]{2,1,0:T(8,128)S(1)} %collective-permute-done.3.refs_1_, f32[1,128,384]{2,1,0:T(8,128)S(1)} %collective-permute-done.4.refs_2_, f32[1,128,384]{2,1,0:T(8,128)S(1)} %get-tuple-element.78.refs_3_), custom_call_target="tpu_custom_call" | custom-call | tf_op jit(solution)/shard_map/pallas_call | solution.py:105
  20.7 1.6 %collective-permute-start.5 = (f32[1,128,384]{2,1,0:T(8,128)S(1)}, f32[1,128,384]{2,1,0:T(8,128)S(1)}, u32[]{:S(2)}, u32[]{:S(2)}) collective-permute-start(f32[1,128,384]{2,1,0:T(8,128)S(1)} %shard_map.61.refs_0_), channel_id=1, source_target_pairs={{0,1},{1,0},{2,3},{3,2},{4,5},{5,4},{6,7},{7,6},{8,9},{9,8},{10,11... | collective-permute-start | bytes 589832 | tf_op jit(solution)/shard_map/ppermute | solution.py:727
  22.3 4.1 %collective-permute-done.5.refs_1_.refs_0_ = f32[1,128,384]{2,1,0:T(8,128)S(1)} collective-permute-done((f32[1,128,384]{2,1,0:T(8,128)S(1)}, f32[1,128,384]{2,1,0:T(8,128)S(1)}, u32[]{:S(2)}, u32[]{:S(2)}) %collective-permute-start.5) | collective-permute-done | bytes 196640 | tf_op jit(solution)/shard_map/ppermute | solution.py:727
  26.4 0.2 shard_map.62
  26.6 2.6 %collective-permute-start.6 = (f32[1,128,256]{2,1,0:T(8,128)S(1)}, f32[1,128,256]{2,1,0:T(8,128)S(1)}, u32[]{:S(2)}, u32[]{:S(2)}) collective-permute-start(f32[1,128,256]{2,1,0:T(8,128)S(1)} %shard_map.62), channel_id=1, source_target_pairs={{0,2},{1,3},{2,0},{3,1},{4,6},{5,7},{6,4},{7,5},{8,10},{9,11},{10,... | collective-permute-start | bytes 393224 | tf_op jit(solution)/shard_map/ppermute | solution.py:721
  29.3 0.5 %shard_map.63.refs_1_ = f32[3,1,128,384]{3,2,1,0:T(8,128)S(1)} custom-call(f32[1,128,384]{2,1,0:T(8,128)S(1)} %collective-permute-done.1.refs_0_, f32[1,128,384]{2,1,0:T(8,128)S(1)} %collective-permute-done.3.refs_1_, f32[1,128,384]{2,1,0:T(8,128)S(1)} %collective-permute-done.4.refs_2_, f32[1,128,384]{2,1,0:T(8,128)S(1)} %get-tuple-element.78.refs_3_), custom_call_target="tpu_custom_call" | custom-call | tf_op jit(solution)/shard_map/pallas_call | solution.py:105
  29.7 0.1 shard_map.64.refs_1_
  29.8 4.2 %collective-permute-done.6.refs_0_ = f32[1,128,256]{2,1,0:T(8,128)S(1)} collective-permute-done((f32[1,128,256]{2,1,0:T(8,128)S(1)}, f32[1,128,256]{2,1,0:T(8,128)S(1)}, u32[]{:S(2)}, u32[]{:S(2)}) %collective-permute-start.6) | collective-permute-done | bytes 131104 | tf_op jit(solution)/shard_map/ppermute | solution.py:721
  34.0 0.3 shard_map.65
  34.2 2.5 %collective-permute-start.7 = (f32[1,128,256]{2,1,0:T(8,128)S(1)}, f32[1,128,256]{2,1,0:T(8,128)S(1)}, u32[]{:S(2)}, u32[]{:S(2)}) collective-permute-start(f32[1,128,256]{2,1,0:T(8,128)S(1)} %get-tuple-element.79), channel_id=1, source_target_pairs={{0,24},{4,28},{8,16},{12,20},{16,8},{20,12},{24,0},{28,4},{1,25},{... | collective-permute-start | bytes 393224 | tf_op jit(solution)/shard_map/ppermute | solution.py:690
  36.8 0.5 %collective-permute-start.11 = (f32[1,128,256]{2,1,0:T(8,128)S(1)}, f32[1,128,256]{2,1,0:T(8,128)S(1)}, u32[]{:S(2)}, u32[]{:S(2)}) collective-permute-start(f32[1,128,256]{2,1,0:T(8,128)S(1)} %get-tuple-element.89), channel_id=1, source_target_pairs={{0,16},{4,20},{8,24},{12,28},{16,0},{20,4},{24,8},{28,12},{1,17},{... | collective-permute-start | bytes 393224 | tf_op jit(solution)/shard_map/ppermute | solution.py:690
  37.3 0.5 %collective-permute-start.10 = (f32[1,128,256]{2,1,0:T(8,128)S(1)}, f32[1,128,256]{2,1,0:T(8,128)S(1)}, u32[]{:S(2)}, u32[]{:S(2)}) collective-permute-start(f32[1,128,256]{2,1,0:T(8,128)S(1)} %get-tuple-element.87), channel_id=1, source_target_pairs={{0,8},{4,12},{8,0},{12,4},{16,24},{20,28},{24,16},{28,20},{1,9},{5... | collective-permute-start | bytes 393224 | tf_op jit(solution)/shard_map/ppermute | solution.py:690
  37.8 2.4 %collective-permute-done.7.refs_4_ = f32[1,128,256]{2,1,0:T(8,128)S(1)} collective-permute-done((f32[1,128,256]{2,1,0:T(8,128)S(1)}, f32[1,128,256]{2,1,0:T(8,128)S(1)}, u32[]{:S(2)}, u32[]{:S(2)}) %collective-permute-start.7) | collective-permute-done | bytes 131104 | tf_op jit(solution)/shard_map/ppermute | solution.py:690
  40.2 0.2 shard_map.67
  40.4 0.1 collective-permute-start.9
  40.4 0.2 shard_map.66
  40.6 0.6 %collective-permute-start.8 = (f32[1,128,256]{2,1,0:T(8,128)S(1)}, f32[1,128,256]{2,1,0:T(8,128)S(1)}, u32[]{:S(2)}, u32[]{:S(2)}) collective-permute-start(f32[1,128,256]{2,1,0:T(8,128)S(1)} %get-tuple-element.85), channel_id=1, source_target_pairs={{0,4},{4,0},{8,12},{12,8},{16,20},{20,16},{24,28},{28,24},{1,5},{5... | collective-permute-start | bytes 393224 | tf_op jit(solution)/shard_map/ppermute | solution.py:746
  41.2 0.6 %collective-permute-done.11.refs_4_ = f32[1,128,256]{2,1,0:T(8,128)S(1)} collective-permute-done((f32[1,128,256]{2,1,0:T(8,128)S(1)}, f32[1,128,256]{2,1,0:T(8,128)S(1)}, u32[]{:S(2)}, u32[]{:S(2)}) %collective-permute-start.11) | collective-permute-done | bytes 131104 | tf_op jit(solution)/shard_map/ppermute | solution.py:690
  41.8 0.2 shard_map.70
  41.9 0.1 collective-permute-start.13
  42.0 0.2 collective-permute-done.10.refs_4_
  42.2 0.2 shard_map.69
  42.4 0.4 collective-permute-start.12
  42.8 0.0 collective-permute-done.9.refs_4_
  42.8 0.0 collective-permute-done.8.refs_3_
  42.8 0.3 shard_map.68.refs_1_
  43.1 0.3 collective-permute-done.13.refs_5_
  43.4 0.5 %collective-permute-done.12.refs_4_ = f32[1,128,256]{2,1,0:T(8,128)S(1)} collective-permute-done((f32[1,128,256]{2,1,0:T(8,128)S(1)}, f32[1,128,256]{2,1,0:T(8,128)S(1)}, u32[]{:S(2)}, u32[]{:S(2)}) %collective-permute-start.12) | collective-permute-done | bytes 131104 | tf_op jit(solution)/shard_map/ppermute | solution.py:746
  43.8 1.3 %shard_map.71 = bf16[128,8,256]{2,1,0:T(8,128)(2,1)} custom-call(f32[8,128,384]{2,1,0:T(8,128)S(1)} %shard_map.60.refs_0_, f32[2,2,1,128,256]{4,3,2,1,0:T(8,128)S(1)} %shard_map.68.refs_1_, f32[1,128,256]{2,1,0:T(8,128)S(1)} %get-tuple-element.88.refs_2_, f32[1,128,256]{2,1,0:T(8,128)S(1)} %get-tuple-element.90.refs_3_, ...), custom_call_target="tpu_custom_call" | custom-call | tf_op jit(solution)/shard_map/pallas_call | solution.py:760
Async XLA Ops:
  4.4 1.6 %collective-permute-start = (f32[1,128,384]{2,1,0:T(8,128)S(1)}, f32[1,128,384]{2,1,0:T(8,128)S(1)}, u32[]{:S(2)}, u32[]{:S(2)}) collective-permute-start(f32[1,128,384]{2,1,0:T(8,128)S(1)} %get-tuple-element.56), channel_id=1, source_target_pairs={{0,4},{4,0},{8,12},{12,8},{16,20},{20,16},{24,28},{28,24},{1,5},{5... | collective-permute-start | bytes 589832 | tf_op jit(solution)/shard_map/ppermute | solution.py:657
  4.9 1.4 %copy-start = (bf16[128,8,128]{2,1,0:T(8,128)(2,1)S(1)}, bf16[128,8,128]{2,1,0:T(8,128)(2,1)}, u32[]{:S(2)}) copy-start(bf16[128,8,128]{2,1,0:T(8,128)(2,1)} %refs_1_.3) | copy-start | bytes 786436
  6.0 6.1 %collective-permute-start.2 = (f32[3,128,384]{2,1,0:T(8,128)S(1)}, f32[3,128,384]{2,1,0:T(8,128)S(1)}, u32[]{:S(2)}, u32[]{:S(2)}) collective-permute-start(f32[3,128,384]{2,1,0:T(8,128)S(1)} %get-tuple-element.64), channel_id=1, source_target_pairs={{0,4},{4,0},{8,12},{12,8},{16,20},{20,16},{24,28},{28,24},{1,5},{5... | collective-permute-start | bytes 1769480 | tf_op jit(solution)/shard_map/ppermute | solution.py:668
  8.4 9.5 %collective-permute-start.1 = (f32[1,128,384]{2,1,0:T(8,128)S(1)}, f32[1,128,384]{2,1,0:T(8,128)S(1)}, u32[]{:S(2)}, u32[]{:S(2)}) collective-permute-start(f32[1,128,384]{2,1,0:T(8,128)S(1)} %shard_map.57), channel_id=1, source_target_pairs={{0,24},{4,28},{8,16},{12,20},{16,8},{20,12},{24,0},{28,4},{1,25},{... | collective-permute-start | bytes 589832 | tf_op jit(solution)/shard_map/ppermute | solution.py:690
  12.5 7.7 %collective-permute-start.3 = (f32[1,128,384]{2,1,0:T(8,128)S(1)}, f32[1,128,384]{2,1,0:T(8,128)S(1)}, u32[]{:S(2)}, u32[]{:S(2)}) collective-permute-start(f32[1,128,384]{2,1,0:T(8,128)S(1)} %get-tuple-element.65), channel_id=1, source_target_pairs={{0,8},{4,12},{8,0},{12,4},{16,24},{20,28},{24,16},{28,20},{1,9},{5... | collective-permute-start | bytes 589832 | tf_op jit(solution)/shard_map/ppermute | solution.py:690
  13.1 7.1 %collective-permute-start.4 = (f32[1,128,384]{2,1,0:T(8,128)S(1)}, f32[1,128,384]{2,1,0:T(8,128)S(1)}, u32[]{:S(2)}, u32[]{:S(2)}) collective-permute-start(f32[1,128,384]{2,1,0:T(8,128)S(1)} %get-tuple-element.66), channel_id=1, source_target_pairs={{0,16},{4,20},{8,24},{12,28},{16,0},{20,4},{24,8},{28,12},{1,17},{... | collective-permute-start | bytes 589832 | tf_op jit(solution)/shard_map/ppermute | solution.py:690
  20.7 5.7 %collective-permute-start.5 = (f32[1,128,384]{2,1,0:T(8,128)S(1)}, f32[1,128,384]{2,1,0:T(8,128)S(1)}, u32[]{:S(2)}, u32[]{:S(2)}) collective-permute-start(f32[1,128,384]{2,1,0:T(8,128)S(1)} %shard_map.61.refs_0_), channel_id=1, source_target_pairs={{0,1},{1,0},{2,3},{3,2},{4,5},{5,4},{6,7},{7,6},{8,9},{9,8},{10,11... | collective-permute-start | bytes 589832 | tf_op jit(solution)/shard_map/ppermute | solution.py:727
  26.6 7.3 %collective-permute-start.6 = (f32[1,128,256]{2,1,0:T(8,128)S(1)}, f32[1,128,256]{2,1,0:T(8,128)S(1)}, u32[]{:S(2)}, u32[]{:S(2)}) collective-permute-start(f32[1,128,256]{2,1,0:T(8,128)S(1)} %shard_map.62), channel_id=1, source_target_pairs={{0,2},{1,3},{2,0},{3,1},{4,6},{5,7},{6,4},{7,5},{8,10},{9,11},{10,... | collective-permute-start | bytes 393224 | tf_op jit(solution)/shard_map/ppermute | solution.py:721
  34.2 5.9 %collective-permute-start.7 = (f32[1,128,256]{2,1,0:T(8,128)S(1)}, f32[1,128,256]{2,1,0:T(8,128)S(1)}, u32[]{:S(2)}, u32[]{:S(2)}) collective-permute-start(f32[1,128,256]{2,1,0:T(8,128)S(1)} %get-tuple-element.79), channel_id=1, source_target_pairs={{0,24},{4,28},{8,16},{12,20},{16,8},{20,12},{24,0},{28,4},{1,25},{... | collective-permute-start | bytes 393224 | tf_op jit(solution)/shard_map/ppermute | solution.py:690
  36.8 5.0 %collective-permute-start.11 = (f32[1,128,256]{2,1,0:T(8,128)S(1)}, f32[1,128,256]{2,1,0:T(8,128)S(1)}, u32[]{:S(2)}, u32[]{:S(2)}) collective-permute-start(f32[1,128,256]{2,1,0:T(8,128)S(1)} %get-tuple-element.89), channel_id=1, source_target_pairs={{0,16},{4,20},{8,24},{12,28},{16,0},{20,4},{24,8},{28,12},{1,17},{... | collective-permute-start | bytes 393224 | tf_op jit(solution)/shard_map/ppermute | solution.py:690
  37.3 5.0 %collective-permute-start.10 = (f32[1,128,256]{2,1,0:T(8,128)S(1)}, f32[1,128,256]{2,1,0:T(8,128)S(1)}, u32[]{:S(2)}, u32[]{:S(2)}) collective-permute-start(f32[1,128,256]{2,1,0:T(8,128)S(1)} %get-tuple-element.87), channel_id=1, source_target_pairs={{0,8},{4,12},{8,0},{12,4},{16,24},{20,28},{24,16},{28,20},{1,9},{5... | collective-permute-start | bytes 393224 | tf_op jit(solution)/shard_map/ppermute | solution.py:690
  40.4 2.4 %collective-permute-start.9 = (f32[1,128,256]{2,1,0:T(8,128)S(1)}, f32[1,128,256]{2,1,0:T(8,128)S(1)}, u32[]{:S(2)}, u32[]{:S(2)}) collective-permute-start(f32[1,128,256]{2,1,0:T(8,128)S(1)} %get-tuple-element.86), channel_id=1, source_target_pairs={{0,4},{4,0},{8,12},{12,8},{16,20},{20,16},{24,28},{28,24},{1,5},{5... | collective-permute-start | bytes 393224 | tf_op jit(solution)/shard_map/ppermute | solution.py:746
  40.6 2.1 %collective-permute-start.8 = (f32[1,128,256]{2,1,0:T(8,128)S(1)}, f32[1,128,256]{2,1,0:T(8,128)S(1)}, u32[]{:S(2)}, u32[]{:S(2)}) collective-permute-start(f32[1,128,256]{2,1,0:T(8,128)S(1)} %get-tuple-element.85), channel_id=1, source_target_pairs={{0,4},{4,0},{8,12},{12,8},{16,20},{20,16},{24,28},{28,24},{1,5},{5... | collective-permute-start | bytes 393224 | tf_op jit(solution)/shard_map/ppermute | solution.py:746
  41.9 1.4 %collective-permute-start.13 = (f32[1,128,256]{2,1,0:T(8,128)S(1)}, f32[1,128,256]{2,1,0:T(8,128)S(1)}, u32[]{:S(2)}, u32[]{:S(2)}) collective-permute-start(f32[1,128,256]{2,1,0:T(8,128)S(1)} %get-tuple-element.92), channel_id=1, source_target_pairs={{0,4},{4,0},{8,12},{12,8},{16,20},{20,16},{24,28},{28,24},{1,5},{5... | collective-permute-start | bytes 393224 | tf_op jit(solution)/shard_map/ppermute | solution.py:746
  42.4 1.4 %collective-permute-start.12 = (f32[1,128,256]{2,1,0:T(8,128)S(1)}, f32[1,128,256]{2,1,0:T(8,128)S(1)}, u32[]{:S(2)}, u32[]{:S(2)}) collective-permute-start(f32[1,128,256]{2,1,0:T(8,128)S(1)} %get-tuple-element.91), channel_id=1, source_target_pairs={{0,4},{4,0},{8,12},{12,8},{16,20},{20,16},{24,28},{28,24},{1,5},{5... | collective-permute-start | bytes 393224 | tf_op jit(solution)/shard_map/ppermute | solution.py:746

commit v8 on v7

--- a/solution.py
+++ b/solution.py
@@ -234,7 +234,7 @@
     copies = [
         pltpu.make_async_copy(src, dst, sems.at[n])
         for n, (src, dst) in enumerate(
-            ((k_hbm, k_ref), (g_hbm, g_ref), (b_hbm, b_ref), (v_hbm, v_ref))
+            ((g_hbm, g_ref), (k_hbm, k_ref), (b_hbm, b_ref), (v_hbm, v_ref))
         )
     ]
     for copy in copies:
@@ -245,7 +245,7 @@
     core, chip = place[0], place[1]
     order = [(1 - core) * half + h for h in local_heads(1 - core, chip, chips, half)]
     order += [core * half + h for h in local_heads(core, chip, chips, half)]
-    copies[1].wait()
+    copies[0].wait()
     copies[2].wait()
 
     def picked(ref):
@@ -264,7 +264,7 @@
     eye = rows == cols
     eye_key = eye_mask(key_dim)
     every = range(heads)
-    copies[0].wait()
+    copies[1].wait()
     stage_rows(k_ref, ks)
     k_wide = [head_rows(ks, h, heads) for h in order]
     k_raw = [a.astype(BF16) for a in k_wide]
@@ -766,7 +766,7 @@
             pltpu.VMEM((tok, heads, value_dim), BF16),
             tall(value_dim // 2),
             tall(value_dim // 2),
-            pltpu.SemaphoreType.DMA((2 if tok % 32 == 0 else 1,)),
+            pltpu.SemaphoreType.DMA((4 if tok % 64 == 0 else 1,)),
         ],
         compiler_params=pltpu.CompilerParams(vmem_limit_bytes=VMEM_LIMIT),
     )(*inputs)

time: 45.3 us -> 45.3 us (level)
  no operation moved by 1% of the time
where the time goes in v8:
time: 45.3 us; the launch traced here: 45.1 us
  waiting for transfers between devices  19.5 us (43%)
  starting transfers between devices  14.1 us (31%)
  Pallas kernels  11.3 us (25%)
    ppermute x6, waiting for transfers between devices, across(): moved.append(lax.ppermute(parts[slot], 'seq', pairs))  10.1 us
    ppermute x6, starting transfers between devices, across(): moved.append(lax.ppermute(parts[slot], 'seq', pairs))  7.88 us
    pallas_call x15, Pallas kernels, run(): pl.pallas_call(placed(kernel), out_shape=out_shape, in_specs=vmem(len(arr...  5.67 us
    pallas_call x1, Pallas kernels, body(): pl.pallas_call(placed(functools.partial(basis_kernel, chips, per)), out_s...  4.4 us
    ppermute x1, waiting for transfers between devices, body(): got_state = lax.ppermute(total, 'grp', swap)  4.15 us
    ppermute x1, waiting for transfers between devices, body(): got = lax.ppermute(total, 'grp', swap)  4.09 us
    ppermute x1, starting transfers between devices, body(): got_state = lax.ppermute(total, 'grp', swap)  2.65 us
    ppermute x1, starting transfers between devices, body(): got = lax.ppermute(total, 'grp', swap)  1.65 us
  transfers between devices with their start and end apart: 14, of which 10 were waited for; matrix products, arithmetic and copies ran while one was open for 0% of the time, Pallas kernels for 10%

profile of v8, /device:TPU:0, one launch (start us, length us, event | category | flops | bytes accessed | tf_op | source)
XLA Modules:
  0.0 45.1 jit_solution(9289071414137391893)
XLA Ops:
  0.0 4.4 %shard_map.55 = (f32[1,128,384]{2,1,0:T(8,128)S(1)}, f32[1,128,384]{2,1,0:T(8,128)S(1)}, f32[2,128,384]{2,1,0:T(8,128)S(1)}, bf16[8,128,128]{2,1,0:T(8,128)(2,1)...) custom-call(bf16[128,8,128]{2,1,0:T(8,128)(2,1)} %refs_0_.2, ...), custom_call_target="tpu_custom_call" | custom-call | flops 1677721600 | tf_op jit(solution)/shard_map/pallas_call | solution.py:623
  4.4 0.5 %collective-permute-start = (f32[1,128,384]{2,1,0:T(8,128)S(1)}, f32[1,128,384]{2,1,0:T(8,128)S(1)}, u32[]{:S(2)}, u32[]{:S(2)}) collective-permute-start(f32[1,128,384]{2,1,0:T(8,128)S(1)} %get-tuple-element.56), channel_id=1, source_target_pairs={{0,4},{4,0},{8,12},{12,8},{16,20},{20,16},{24,28},{28,24},{1,5},{5... | collective-permute-start | bytes 589832 | tf_op jit(solution)/shard_map/ppermute | solution.py:657
  4.9 0.0 copy-start
  4.9 0.6 %shard_map.56 = (f32[3,128,384]{2,1,0:T(8,128)S(1)}, f32[3,128,384]{2,1,0:T(8,128)S(1)}, f32[6,128,384]{2,1,0:T(8,128)S(1)}) custom-call(f32[6,128,128]{2,1,0:T(8,128)S(1)} %get-tuple-element.50.refs_0_, bf16[8,128,128]{2,1,0:T(8,128)(2,1)S(1)} %get-tuple-element.51.refs_1_.refs_2_, bf16[6,128,256]{2,1,0:T(8,128)(2,1)S(1)} %get-tuple-element.52.refs_2_, ...), custom_call_target="tpu_custom_call" | custom-call | flops 6710886400 | tf_op jit(solution)/shard_map/pallas_call | solution.py:105
  5.5 0.4 collective-permute-done.refs_1_.refs_2_
  6.0 0.4 collective-permute-start.2
  6.4 0.0 copy-done
  6.4 1.8 %shard_map.58.refs_0_ = f32[8,128,384]{2,1,0:T(8,128)S(1)} custom-call(bf16[128,8,128]{2,1,0:T(8,128)(2,1)S(1)} %copy-done, bf16[8,128,128]{2,1,0:T(8,128)(2,1)S(1)} %get-tuple-element.51.refs_1_.refs_2_, f32[4,8,128]{2,1,0:T(8,128)S(1)} %get-tuple-element.54.refs_4_.refs_2_.refs_3_, f32[2,128,384]{2,1,0:T(8,128)S(1)} %get-tuple-element.58.refs_3_.refs_4_, ...), custom_call_target="tpu_custom_call" | custom-call | flops 671088640 | tf_op jit(solution)/shard_map/pallas_call | solution.py:105
  8.2 0.2 shard_map.57
  8.4 3.7 %collective-permute-start.1 = (f32[1,128,384]{2,1,0:T(8,128)S(1)}, f32[1,128,384]{2,1,0:T(8,128)S(1)}, u32[]{:S(2)}, u32[]{:S(2)}) collective-permute-start(f32[1,128,384]{2,1,0:T(8,128)S(1)} %shard_map.57), channel_id=1, source_target_pairs={{0,24},{4,28},{8,16},{12,20},{16,8},{20,12},{24,0},{28,4},{1,25},{... | collective-permute-start | bytes 589832 | tf_op jit(solution)/shard_map/ppermute | solution.py:690
  12.1 0.0 collective-permute-done.2.refs_1_.refs_3_
  12.1 0.4 shard_map.59
  12.5 0.6 %collective-permute-start.3 = (f32[1,128,384]{2,1,0:T(8,128)S(1)}, f32[1,128,384]{2,1,0:T(8,128)S(1)}, u32[]{:S(2)}, u32[]{:S(2)}) collective-permute-start(f32[1,128,384]{2,1,0:T(8,128)S(1)} %get-tuple-element.65), channel_id=1, source_target_pairs={{0,8},{4,12},{8,0},{12,4},{16,24},{20,28},{24,16},{28,20},{1,9},{5... | collective-permute-start | bytes 589832 | tf_op jit(solution)/shard_map/ppermute | solution.py:690
  13.1 0.1 collective-permute-start.4
  13.1 4.8 %collective-permute-done.1.refs_0_ = f32[1,128,384]{2,1,0:T(8,128)S(1)} collective-permute-done((f32[1,128,384]{2,1,0:T(8,128)S(1)}, f32[1,128,384]{2,1,0:T(8,128)S(1)}, u32[]{:S(2)}, u32[]{:S(2)}) %collective-permute-start.1) | collective-permute-done | bytes 196640 | tf_op jit(solution)/shard_map/ppermute | solution.py:690
  17.9 0.1 shard_map.60.refs_0_
  18.0 2.1 %collective-permute-done.3.refs_1_ = f32[1,128,384]{2,1,0:T(8,128)S(1)} collective-permute-done((f32[1,128,384]{2,1,0:T(8,128)S(1)}, f32[1,128,384]{2,1,0:T(8,128)S(1)}, u32[]{:S(2)}, u32[]{:S(2)}) %collective-permute-start.3) | collective-permute-done | bytes 196640 | tf_op jit(solution)/shard_map/ppermute | solution.py:690
  20.2 0.0 collective-permute-done.4.refs_2_
  20.2 0.5 %shard_map.61.refs_0_ = f32[1,128,384]{2,1,0:T(8,128)S(1)} custom-call(f32[1,128,384]{2,1,0:T(8,128)S(1)} %collective-permute-done.1.refs_0_, f32[1,128,384]{2,1,0:T(8,128)S(1)} %collective-permute-done.3.refs_1_, f32[1,128,384]{2,1,0:T(8,128)S(1)} %collective-permute-done.4.refs_2_, f32[1,128,384]{2,1,0:T(8,128)S(1)} %get-tuple-element.78.refs_3_), custom_call_target="tpu_custom_call" | custom-call | tf_op jit(solution)/shard_map/pallas_call | solution.py:105
  20.7 1.6 %collective-permute-start.5 = (f32[1,128,384]{2,1,0:T(8,128)S(1)}, f32[1,128,384]{2,1,0:T(8,128)S(1)}, u32[]{:S(2)}, u32[]{:S(2)}) collective-permute-start(f32[1,128,384]{2,1,0:T(8,128)S(1)} %shard_map.61.refs_0_), channel_id=1, source_target_pairs={{0,1},{1,0},{2,3},{3,2},{4,5},{5,4},{6,7},{7,6},{8,9},{9,8},{10,11... | collective-permute-start | bytes 589832 | tf_op jit(solution)/shard_map/ppermute | solution.py:727
  22.3 4.1 %collective-permute-done.5.refs_1_.refs_0_ = f32[1,128,384]{2,1,0:T(8,128)S(1)} collective-permute-done((f32[1,128,384]{2,1,0:T(8,128)S(1)}, f32[1,128,384]{2,1,0:T(8,128)S(1)}, u32[]{:S(2)}, u32[]{:S(2)}) %collective-permute-start.5) | collective-permute-done | bytes 196640 | tf_op jit(solution)/shard_map/ppermute | solution.py:727
  26.4 0.2 shard_map.62
  26.6 2.6 %collective-permute-start.6 = (f32[1,128,256]{2,1,0:T(8,128)S(1)}, f32[1,128,256]{2,1,0:T(8,128)S(1)}, u32[]{:S(2)}, u32[]{:S(2)}) collective-permute-start(f32[1,128,256]{2,1,0:T(8,128)S(1)} %shard_map.62), channel_id=1, source_target_pairs={{0,2},{1,3},{2,0},{3,1},{4,6},{5,7},{6,4},{7,5},{8,10},{9,11},{10,... | collective-permute-start | bytes 393224 | tf_op jit(solution)/shard_map/ppermute | solution.py:721
  29.3 0.5 %shard_map.63.refs_1_ = f32[3,1,128,384]{3,2,1,0:T(8,128)S(1)} custom-call(f32[1,128,384]{2,1,0:T(8,128)S(1)} %collective-permute-done.1.refs_0_, f32[1,128,384]{2,1,0:T(8,128)S(1)} %collective-permute-done.3.refs_1_, f32[1,128,384]{2,1,0:T(8,128)S(1)} %collective-permute-done.4.refs_2_, f32[1,128,384]{2,1,0:T(8,128)S(1)} %get-tuple-element.78.refs_3_), custom_call_target="tpu_custom_call" | custom-call | tf_op jit(solution)/shard_map/pallas_call | solution.py:105
  29.7 0.1 shard_map.64.refs_1_
  29.8 4.2 %collective-permute-done.6.refs_0_ = f32[1,128,256]{2,1,0:T(8,128)S(1)} collective-permute-done((f32[1,128,256]{2,1,0:T(8,128)S(1)}, f32[1,128,256]{2,1,0:T(8,128)S(1)}, u32[]{:S(2)}, u32[]{:S(2)}) %collective-permute-start.6) | collective-permute-done | bytes 131104 | tf_op jit(solution)/shard_map/ppermute | solution.py:721
  34.0 0.3 shard_map.65
  34.2 2.6 %collective-permute-start.7 = (f32[1,128,256]{2,1,0:T(8,128)S(1)}, f32[1,128,256]{2,1,0:T(8,128)S(1)}, u32[]{:S(2)}, u32[]{:S(2)}) collective-permute-start(f32[1,128,256]{2,1,0:T(8,128)S(1)} %get-tuple-element.79), channel_id=1, source_target_pairs={{0,24},{4,28},{8,16},{12,20},{16,8},{20,12},{24,0},{28,4},{1,25},{... | collective-permute-start | bytes 393224 | tf_op jit(solution)/shard_map/ppermute | solution.py:690
  36.8 0.5 %collective-permute-start.11 = (f32[1,128,256]{2,1,0:T(8,128)S(1)}, f32[1,128,256]{2,1,0:T(8,128)S(1)}, u32[]{:S(2)}, u32[]{:S(2)}) collective-permute-start(f32[1,128,256]{2,1,0:T(8,128)S(1)} %get-tuple-element.89), channel_id=1, source_target_pairs={{0,16},{4,20},{8,24},{12,28},{16,0},{20,4},{24,8},{28,12},{1,17},{... | collective-permute-start | bytes 393224 | tf_op jit(solution)/shard_map/ppermute | solution.py:690
  37.3 0.5 %collective-permute-start.10 = (f32[1,128,256]{2,1,0:T(8,128)S(1)}, f32[1,128,256]{2,1,0:T(8,128)S(1)}, u32[]{:S(2)}, u32[]{:S(2)}) collective-permute-start(f32[1,128,256]{2,1,0:T(8,128)S(1)} %get-tuple-element.87), channel_id=1, source_target_pairs={{0,8},{4,12},{8,0},{12,4},{16,24},{20,28},{24,16},{28,20},{1,9},{5... | collective-permute-start | bytes 393224 | tf_op jit(solution)/shard_map/ppermute | solution.py:690
  37.8 2.4 %collective-permute-done.7.refs_4_ = f32[1,128,256]{2,1,0:T(8,128)S(1)} collective-permute-done((f32[1,128,256]{2,1,0:T(8,128)S(1)}, f32[1,128,256]{2,1,0:T(8,128)S(1)}, u32[]{:S(2)}, u32[]{:S(2)}) %collective-permute-start.7) | collective-permute-done | bytes 131104 | tf_op jit(solution)/shard_map/ppermute | solution.py:690
  40.2 0.2 shard_map.67
  40.4 0.1 collective-permute-start.9
  40.4 0.2 shard_map.66
  40.6 0.6 %collective-permute-start.8 = (f32[1,128,256]{2,1,0:T(8,128)S(1)}, f32[1,128,256]{2,1,0:T(8,128)S(1)}, u32[]{:S(2)}, u32[]{:S(2)}) collective-permute-start(f32[1,128,256]{2,1,0:T(8,128)S(1)} %get-tuple-element.85), channel_id=1, source_target_pairs={{0,4},{4,0},{8,12},{12,8},{16,20},{20,16},{24,28},{28,24},{1,5},{5... | collective-permute-start | bytes 393224 | tf_op jit(solution)/shard_map/ppermute | solution.py:746
  41.2 0.6 %collective-permute-done.11.refs_4_ = f32[1,128,256]{2,1,0:T(8,128)S(1)} collective-permute-done((f32[1,128,256]{2,1,0:T(8,128)S(1)}, f32[1,128,256]{2,1,0:T(8,128)S(1)}, u32[]{:S(2)}, u32[]{:S(2)}) %collective-permute-start.11) | collective-permute-done | bytes 131104 | tf_op jit(solution)/shard_map/ppermute | solution.py:690
  41.8 0.2 shard_map.70
  42.0 0.1 collective-permute-start.13
  42.0 0.2 collective-permute-done.10.refs_4_
  42.2 0.2 shard_map.69
  42.4 0.4 collective-permute-start.12
  42.8 0.0 collective-permute-done.9.refs_4_
  42.8 0.0 collective-permute-done.8.refs_3_
  42.8 0.3 shard_map.68.refs_1_
  43.1 0.3 collective-permute-done.13.refs_5_
  43.4 0.5 %collective-permute-done.12.refs_4_ = f32[1,128,256]{2,1,0:T(8,128)S(1)} collective-permute-done((f32[1,128,256]{2,1,0:T(8,128)S(1)}, f32[1,128,256]{2,1,0:T(8,128)S(1)}, u32[]{:S(2)}, u32[]{:S(2)}) %collective-permute-start.12) | collective-permute-done | bytes 131104 | tf_op jit(solution)/shard_map/ppermute | solution.py:746
  43.8 1.3 %shard_map.71 = bf16[128,8,256]{2,1,0:T(8,128)(2,1)} custom-call(f32[8,128,384]{2,1,0:T(8,128)S(1)} %shard_map.60.refs_0_, f32[2,2,1,128,256]{4,3,2,1,0:T(8,128)S(1)} %shard_map.68.refs_1_, f32[1,128,256]{2,1,0:T(8,128)S(1)} %get-tuple-element.88.refs_2_, f32[1,128,256]{2,1,0:T(8,128)S(1)} %get-tuple-element.90.refs_3_, ...), custom_call_target="tpu_custom_call" | custom-call | tf_op jit(solution)/shard_map/pallas_call | solution.py:760
Async XLA Ops:
  4.4 1.6 %collective-permute-start = (f32[1,128,384]{2,1,0:T(8,128)S(1)}, f32[1,128,384]{2,1,0:T(8,128)S(1)}, u32[]{:S(2)}, u32[]{:S(2)}) collective-permute-start(f32[1,128,384]{2,1,0:T(8,128)S(1)} %get-tuple-element.56), channel_id=1, source_target_pairs={{0,4},{4,0},{8,12},{12,8},{16,20},{20,16},{24,28},{28,24},{1,5},{5... | collective-permute-start | bytes 589832 | tf_op jit(solution)/shard_map/ppermute | solution.py:657
  4.9 1.4 %copy-start = (bf16[128,8,128]{2,1,0:T(8,128)(2,1)S(1)}, bf16[128,8,128]{2,1,0:T(8,128)(2,1)}, u32[]{:S(2)}) copy-start(bf16[128,8,128]{2,1,0:T(8,128)(2,1)} %refs_1_.3) | copy-start | bytes 786436
  6.0 6.1 %collective-permute-start.2 = (f32[3,128,384]{2,1,0:T(8,128)S(1)}, f32[3,128,384]{2,1,0:T(8,128)S(1)}, u32[]{:S(2)}, u32[]{:S(2)}) collective-permute-start(f32[3,128,384]{2,1,0:T(8,128)S(1)} %get-tuple-element.64), channel_id=1, source_target_pairs={{0,4},{4,0},{8,12},{12,8},{16,20},{20,16},{24,28},{28,24},{1,5},{5... | collective-permute-start | bytes 1769480 | tf_op jit(solution)/shard_map/ppermute | solution.py:668
  8.4 9.5 %collective-permute-start.1 = (f32[1,128,384]{2,1,0:T(8,128)S(1)}, f32[1,128,384]{2,1,0:T(8,128)S(1)}, u32[]{:S(2)}, u32[]{:S(2)}) collective-permute-start(f32[1,128,384]{2,1,0:T(8,128)S(1)} %shard_map.57), channel_id=1, source_target_pairs={{0,24},{4,28},{8,16},{12,20},{16,8},{20,12},{24,0},{28,4},{1,25},{... | collective-permute-start | bytes 589832 | tf_op jit(solution)/shard_map/ppermute | solution.py:690
  12.5 7.7 %collective-permute-start.3 = (f32[1,128,384]{2,1,0:T(8,128)S(1)}, f32[1,128,384]{2,1,0:T(8,128)S(1)}, u32[]{:S(2)}, u32[]{:S(2)}) collective-permute-start(f32[1,128,384]{2,1,0:T(8,128)S(1)} %get-tuple-element.65), channel_id=1, source_target_pairs={{0,8},{4,12},{8,0},{12,4},{16,24},{20,28},{24,16},{28,20},{1,9},{5... | collective-permute-start | bytes 589832 | tf_op jit(solution)/shard_map/ppermute | solution.py:690
  13.1 7.1 %collective-permute-start.4 = (f32[1,128,384]{2,1,0:T(8,128)S(1)}, f32[1,128,384]{2,1,0:T(8,128)S(1)}, u32[]{:S(2)}, u32[]{:S(2)}) collective-permute-start(f32[1,128,384]{2,1,0:T(8,128)S(1)} %get-tuple-element.66), channel_id=1, source_target_pairs={{0,16},{4,20},{8,24},{12,28},{16,0},{20,4},{24,8},{28,12},{1,17},{... | collective-permute-start | bytes 589832 | tf_op jit(solution)/shard_map/ppermute | solution.py:690
  20.7 5.7 %collective-permute-start.5 = (f32[1,128,384]{2,1,0:T(8,128)S(1)}, f32[1,128,384]{2,1,0:T(8,128)S(1)}, u32[]{:S(2)}, u32[]{:S(2)}) collective-permute-start(f32[1,128,384]{2,1,0:T(8,128)S(1)} %shard_map.61.refs_0_), channel_id=1, source_target_pairs={{0,1},{1,0},{2,3},{3,2},{4,5},{5,4},{6,7},{7,6},{8,9},{9,8},{10,11... | collective-permute-start | bytes 589832 | tf_op jit(solution)/shard_map/ppermute | solution.py:727
  26.6 7.3 %collective-permute-start.6 = (f32[1,128,256]{2,1,0:T(8,128)S(1)}, f32[1,128,256]{2,1,0:T(8,128)S(1)}, u32[]{:S(2)}, u32[]{:S(2)}) collective-permute-start(f32[1,128,256]{2,1,0:T(8,128)S(1)} %shard_map.62), channel_id=1, source_target_pairs={{0,2},{1,3},{2,0},{3,1},{4,6},{5,7},{6,4},{7,5},{8,10},{9,11},{10,... | collective-permute-start | bytes 393224 | tf_op jit(solution)/shard_map/ppermute | solution.py:721
  34.2 5.9 %collective-permute-start.7 = (f32[1,128,256]{2,1,0:T(8,128)S(1)}, f32[1,128,256]{2,1,0:T(8,128)S(1)}, u32[]{:S(2)}, u32[]{:S(2)}) collective-permute-start(f32[1,128,256]{2,1,0:T(8,128)S(1)} %get-tuple-element.79), channel_id=1, source_target_pairs={{0,24},{4,28},{8,16},{12,20},{16,8},{20,12},{24,0},{28,4},{1,25},{... | collective-permute-start | bytes 393224 | tf_op jit(solution)/shard_map/ppermute | solution.py:690
  36.8 5.0 %collective-permute-start.11 = (f32[1,128,256]{2,1,0:T(8,128)S(1)}, f32[1,128,256]{2,1,0:T(8,128)S(1)}, u32[]{:S(2)}, u32[]{:S(2)}) collective-permute-start(f32[1,128,256]{2,1,0:T(8,128)S(1)} %get-tuple-element.89), channel_id=1, source_target_pairs={{0,16},{4,20},{8,24},{12,28},{16,0},{20,4},{24,8},{28,12},{1,17},{... | collective-permute-start | bytes 393224 | tf_op jit(solution)/shard_map/ppermute | solution.py:690
  37.3 5.0 %collective-permute-start.10 = (f32[1,128,256]{2,1,0:T(8,128)S(1)}, f32[1,128,256]{2,1,0:T(8,128)S(1)}, u32[]{:S(2)}, u32[]{:S(2)}) collective-permute-start(f32[1,128,256]{2,1,0:T(8,128)S(1)} %get-tuple-element.87), channel_id=1, source_target_pairs={{0,8},{4,12},{8,0},{12,4},{16,24},{20,28},{24,16},{28,20},{1,9},{5... | collective-permute-start | bytes 393224 | tf_op jit(solution)/shard_map/ppermute | solution.py:690
  40.4 2.4 %collective-permute-start.9 = (f32[1,128,256]{2,1,0:T(8,128)S(1)}, f32[1,128,256]{2,1,0:T(8,128)S(1)}, u32[]{:S(2)}, u32[]{:S(2)}) collective-permute-start(f32[1,128,256]{2,1,0:T(8,128)S(1)} %get-tuple-element.86), channel_id=1, source_target_pairs={{0,4},{4,0},{8,12},{12,8},{16,20},{20,16},{24,28},{28,24},{1,5},{5... | collective-permute-start | bytes 393224 | tf_op jit(solution)/shard_map/ppermute | solution.py:746
  40.6 2.2 %collective-permute-start.8 = (f32[1,128,256]{2,1,0:T(8,128)S(1)}, f32[1,128,256]{2,1,0:T(8,128)S(1)}, u32[]{:S(2)}, u32[]{:S(2)}) collective-permute-start(f32[1,128,256]{2,1,0:T(8,128)S(1)} %get-tuple-element.85), channel_id=1, source_target_pairs={{0,4},{4,0},{8,12},{12,8},{16,20},{20,16},{24,28},{28,24},{1,5},{5... | collective-permute-start | bytes 393224 | tf_op jit(solution)/shard_map/ppermute | solution.py:746
  42.0 1.4 %collective-permute-start.13 = (f32[1,128,256]{2,1,0:T(8,128)S(1)}, f32[1,128,256]{2,1,0:T(8,128)S(1)}, u32[]{:S(2)}, u32[]{:S(2)}) collective-permute-start(f32[1,128,256]{2,1,0:T(8,128)S(1)} %get-tuple-element.92), channel_id=1, source_target_pairs={{0,4},{4,0},{8,12},{12,8},{16,20},{20,16},{24,28},{28,24},{1,5},{5... | collective-permute-start | bytes 393224 | tf_op jit(solution)/shard_map/ppermute | solution.py:746
  42.4 1.4 %collective-permute-start.12 = (f32[1,128,256]{2,1,0:T(8,128)S(1)}, f32[1,128,256]{2,1,0:T(8,128)S(1)}, u32[]{:S(2)}, u32[]{:S(2)}) collective-permute-start(f32[1,128,256]{2,1,0:T(8,128)S(1)} %get-tuple-element.91), channel_id=1, source_target_pairs={{0,4},{4,0},{8,12},{12,8},{16,20},{20,16},{24,28},{28,24},{1,5},{5... | collective-permute-start | bytes 393224 | tf_op jit(solution)/shard_map/ppermute | solution.py:746
